TPU v7x, 32 devices: a whole 2x2x4 slice. The times are simulated.
32 devices in a mesh: seq: 8 (over y, x, core), shard: 4 (over z).
Axes of the slice: x: 2, y: 2, z: 4, core: 2. Of those that a mesh axis runs over, the one named last changes fastest.
Arguments:
- hidden_in: bfloat16 [8192, 2048], P('seq'), may hold values from -6 to 6
- out_grad: bfloat16 [8192, 2048], P('seq'), may hold values from -6 to 6
- deal: int32 [8192], P('seq'), may hold values from 0 to 8191, as said below
- lengths: int32 [4], replicated, may hold values from 1024 to 4096, as said below
- qkv_weight: float32 [2048, 3, 2048], P('seq', None, 'shard'), may hold values from -0.125 to 0.125
- qkv_first: float32 [2048, 3, 2048], P('seq', None, 'shard'), may hold values from -32 to 32
- qkv_second: float32 [2048, 3, 2048], P('seq', None, 'shard'), may hold values from 54.0672 to 860.16
- beta_weight: float32 [2048, 16], P('seq', 'shard'), may hold values from -0.125 to 0.125
- beta_first: float32 [2048, 16], P('seq', 'shard'), may hold values from -16 to 16
- beta_second: float32 [2048, 16], P('seq', 'shard'), may hold values from 19.6608 to 311.296
- out_weight: float32 [2048, 2048], P('shard', 'seq'), may hold values from -0.125 to 0.125
- out_first: float32 [2048, 2048], P('shard', 'seq'), may hold values from -64 to 64
- out_second: float32 [2048, 2048], P('shard', 'seq'), may hold values from 212.992 to 3440.64
- gate_up_weight: float32 [2048, 2, 5632], P('seq', None, 'shard'), may hold values from -0.125 to 0.125
- gate_up_first: float32 [2048, 2, 5632], P('seq', None, 'shard'), may hold values from -32 to 32
- gate_up_second: float32 [2048, 2, 5632], P('seq', None, 'shard'), may hold values from 54.0672 to 860.16
- down_weight: float32 [5632, 2048], P('shard', 'seq'), may hold values from -0.078125 to 0.078125
- down_first: float32 [5632, 2048], P('shard', 'seq'), may hold values from -24 to 24
- down_second: float32 [5632, 2048], P('shard', 'seq'), may hold values from 34.4064 to 548.864
- conv_weight: float32 [4, 3, 2048], P(None, None, 'shard'), may hold values from -2 to 2
- conv_first: float32 [4, 3, 2048], P(None, None, 'shard'), may hold values from -32 to 32
- conv_second: float32 [4, 3, 2048], P(None, None, 'shard'), may hold values from 54.0672 to 860.16
- gains: float32 [4224], replicated, may hold values from 0.5 to 1.5
- gains_first: float32 [4224], replicated, may hold values from -64 to 64
- gains_second: float32 [4224], replicated, may hold values from 212.992 to 3440.64
Outputs:
- hidden_out: bfloat16 [8192, 2048], P('seq')
- input_grad: bfloat16 [8192, 2048], P('seq')
- new_qkv_weight: float32 [2048, 3, 2048], P('seq', None, 'shard')
- new_qkv_first: float32 [2048, 3, 2048], P('seq', None, 'shard')
- new_qkv_second: float32 [2048, 3, 2048], P('seq', None, 'shard')
- new_beta_weight: float32 [2048, 16], P('seq', 'shard')
- new_beta_first: float32 [2048, 16], P('seq', 'shard')
- new_beta_second: float32 [2048, 16], P('seq', 'shard')
- new_out_weight: float32 [2048, 2048], P('shard', 'seq')
- new_out_first: float32 [2048, 2048], P('shard', 'seq')
- new_out_second: float32 [2048, 2048], P('shard', 'seq')
- new_gate_up_weight: float32 [2048, 2, 5632], P('seq', None, 'shard')
- new_gate_up_first: float32 [2048, 2, 5632], P('seq', None, 'shard')
- new_gate_up_second: float32 [2048, 2, 5632], P('seq', None, 'shard')
- new_down_weight: float32 [5632, 2048], P('shard', 'seq')
- new_down_first: float32 [5632, 2048], P('shard', 'seq')
- new_down_second: float32 [5632, 2048], P('shard', 'seq')
- new_conv_weight: float32 [4, 3, 2048], P(None, None, 'shard')
- new_conv_first: float32 [4, 3, 2048], P(None, None, 'shard')
- new_conv_second: float32 [4, 3, 2048], P(None, None, 'shard')
- new_gains: float32 [4224], replicated
- new_gains_first: float32 [4224], replicated
- new_gains_second: float32 [4224], replicated
Inputs may be any that keep to these rules, and one draw needn't show every extreme that they name: Row r of the input stands at place deal[r] of the concatenated sequences; every place is named once, and of the rows that one device holds, the same number land in every device's block of 1024 places. `lengths`: each length is a multiple of 64; they sum to 8192; the largest is exactly 4096.
All inputs are finite; a program needn't handle non-finite values.
Results may differ from a plain program's by a relative error of at most 0.019.
The roundings to bfloat16 on the way count: a program that leaves them out, or rounds other values in their place, can miss the bound.
Values may be sent and summed in bfloat16 or wider, within the bound.
A program may use at most 320 MiB of HBM per device.

v0:
```python
import jax
import jax.numpy as jnp
from jax import lax
from jax.sharding import PartitionSpec as P

HEAD = 128
TAPS = 4
GROUP = 64
STEP = 10


EPSILON = 1e-06
PRECISE = lax.Precision.HIGHEST
FIRST_DECAY = 0.9
SECOND_DECAY = 0.95
ADAM_EPSILON = 1e-08
RATE_WIDE = 0.044
RATE_DOWN = 0.027
RATE_CONV = 0.8
RATE_GAIN = 0.3
SHRINK = 0.1


def passed_along(value, axis, by):
    count = lax.axis_size(axis)
    pairs = [(i, i + by) for i in range(count) if 0 <= i + by < count]
    return lax.ppermute(value, axis, pairs)


def rms_scale(values, gain_vec):
    return (
        values * lax.rsqrt(jnp.mean(values * values, axis=-1, keepdims=True) + EPSILON) * gain_vec
    )


def unit_rows(values):
    return values * lax.rsqrt(jnp.sum(values * values, axis=-1, keepdims=True) + EPSILON)


def conv_taps(extended, weights, offset):
    row_count = offset.shape[0]
    tap_count = weights.shape[0]
    running = jnp.zeros((row_count, weights.shape[1]), jnp.float32)
    for tap_index in range(tap_count):
        valid_rows = (offset >= tap_count - 1 - tap_index).astype(jnp.float32)[:, None]
        running = (
            running + weights[tap_index] * extended[tap_index : tap_index + row_count] * valid_rows
        )
    return running


def mixer_inputs(extended, logits, weights, offset, head_count):
    activated = jax.nn.silu(conv_taps(extended, weights, offset))
    row_count = activated.shape[0]
    inner_width = activated.shape[1] // 3
    queries = unit_rows(activated[:, :inner_width].reshape(row_count, head_count, -1))
    key_rows = unit_rows(
        activated[:, inner_width : 2 * inner_width].reshape(row_count, head_count, -1)
    )
    values = activated[:, 2 * inner_width :].reshape(row_count, head_count, -1)
    return (queries, key_rows, values, jax.nn.sigmoid(logits))


def group_step(carry_in, inputs):
    state_now, product = carry_in
    queries, key_rows, values, strength, keep_flag = inputs
    block_len = key_rows.shape[0]
    key_width = key_rows.shape[-1]
    state_start = state_now * keep_flag
    start_map = product * keep_flag
    queries = jnp.swapaxes(queries, 0, 1)
    key_rows = jnp.swapaxes(key_rows, 0, 1)
    values = jnp.swapaxes(values, 0, 1)
    strength = jnp.swapaxes(strength, 0, 1)[:, :, None]
    positions = jnp.arange(block_len)
    strict = (positions[:, None] > positions[None, :]).astype(jnp.float32)
    inclusive = (positions[:, None] >= positions[None, :]).astype(jnp.float32)
    intersection = jnp.einsum("hcd,hed->hce", key_rows, key_rows, precision=PRECISE)
    system = jnp.eye(block_len, dtype=jnp.float32) + strict * strength * intersection
    right_side = jnp.concatenate([strength * key_rows, strength * values], axis=-1)
    solved = jax.scipy.linalg.solve_triangular(system, right_side, lower=True, unit_diagonal=True)
    write_rows = solved[..., :key_width]
    fresh_values = solved[..., key_width:] - jnp.einsum(
        "hcd,hde->hce", write_rows, state_start, precision=PRECISE
    )
    scores = inclusive * jnp.einsum("hcd,hed->hce", queries, key_rows, precision=PRECISE)
    outputs = jnp.einsum("hcd,hde->hce", queries, state_start, precision=PRECISE) + jnp.einsum(
        "hce,hef->hcf", scores, fresh_values, precision=PRECISE
    )
    outputs = outputs * key_width ** (-0.5)
    reach = (
        queries - jnp.einsum("hce,hed->hcd", scores, write_rows, precision=PRECISE)
    ) * key_width ** (-0.5)
    state_end = state_start + jnp.einsum("hcd,hce->hde", key_rows, fresh_values, precision=PRECISE)
    factor = jnp.eye(key_width, dtype=jnp.float32) - jnp.einsum(
        "hcd,hce->hde", key_rows, write_rows, precision=PRECISE
    )
    product = jnp.einsum("hde,hef->hdf", factor, start_map, precision=PRECISE)
    return (
        (state_end, product),
        (jnp.swapaxes(outputs, 0, 1), jnp.swapaxes(reach, 0, 1), start_map),
    )


def local_rule(queries, key_rows, values, strength, keep, head_count, key_width):
    group_count = queries.shape[0] // GROUP

    def to_groups(array):
        return array.reshape((group_count, GROUP) + array.shape[1:])

    zero_state = jnp.zeros((head_count, key_width, key_width), jnp.float32)
    identity = jnp.broadcast_to(
        jnp.eye(key_width, dtype=jnp.float32), (head_count, key_width, key_width)
    )
    (state_end, product), (outputs, reach, maps) = lax.scan(
        group_step,
        (zero_state, identity),
        (to_groups(queries), to_groups(key_rows), to_groups(values), to_groups(strength), keep),
    )
    return (outputs, reach, maps, state_end, product)


def shard_total(values):
    return lax.psum(values, "shard")


def adamw(weight, first, second, grad, rate, decay):
    first = FIRST_DECAY * first + (1.0 - FIRST_DECAY) * grad
    second = SECOND_DECAY * second + (1.0 - SECOND_DECAY) * grad * grad
    stepped = (
        first
        / (1.0 - FIRST_DECAY**STEP)
        / (jnp.sqrt(second / (1.0 - SECOND_DECAY**STEP)) + ADAM_EPSILON)
    )
    return (weight - rate * (stepped + decay * weight), first, second)


def per_device(
    hidden_in,
    out_grad,
    deal,
    lengths,
    qkv_weight,
    qkv_first,
    qkv_second,
    beta_weight,
    beta_first,
    beta_second,
    out_weight,
    out_first,
    out_second,
    gate_up_weight,
    gate_up_first,
    gate_up_second,
    down_weight,
    down_first,
    down_second,
    conv_weight,
    conv_first,
    conv_second,
    gains,
    gains_first,
    gains_second,
):
    row_count = hidden_in.shape[0]
    local_heads = beta_weight.shape[1]
    inner_width = qkv_weight.shape[2]
    unit_count = down_weight.shape[0]
    edge_count = TAPS - 1
    target = deal // row_count
    order = jnp.argsort(target, stable=True)
    got_x, got_dy, got_place = (
        lax.all_to_all(hidden_in[order], "seq", split_axis=0, concat_axis=0, tiled=True),
        lax.all_to_all(out_grad[order], "seq", split_axis=0, concat_axis=0, tiled=True),
        lax.all_to_all(deal[order] % row_count, "seq", split_axis=0, concat_axis=0, tiled=True),
    )
    arranged = jnp.argsort(got_place)
    chain_x = got_x[arranged].astype(jnp.float32)
    chain_dy = got_dy[arranged]
    first_place = lax.axis_index("seq") * row_count
    places = first_place + jnp.arange(row_count, dtype=jnp.int32)
    starts = jnp.cumsum(lengths) - lengths
    latest = jnp.max(jnp.where(starts[None, :] <= places[:, None], starts[None, :], 0), axis=1)
    offset = places - latest
    keep = (offset[::GROUP] > 0).astype(jnp.float32)
    qkv_full, beta_full, gate_up_full, out_full, down_full = (
        lax.all_gather(qkv_weight.astype(jnp.bfloat16), "seq", axis=0, tiled=True),
        lax.all_gather(beta_weight.astype(jnp.bfloat16), "seq", axis=0, tiled=True),
        lax.all_gather(gate_up_weight.astype(jnp.bfloat16), "seq", axis=0, tiled=True),
        lax.all_gather(out_weight.astype(jnp.bfloat16), "seq", axis=1, tiled=True),
        lax.all_gather(down_weight.astype(jnp.bfloat16), "seq", axis=1, tiled=True),
    )
    model_width = qkv_full.shape[0]
    qkv_mat = qkv_full.reshape(model_width, 3 * inner_width)
    gate_up_mat = gate_up_full.reshape(model_width, 2 * unit_count)
    gain_in = gains[:model_width]
    gain_ff = gains[model_width : 2 * model_width]
    gain_out = gains[2 * model_width :]
    normed_in_float, norm_in_back = jax.vjp(rms_scale, chain_x, gain_in)
    normed_in = normed_in_float.astype(jnp.bfloat16)
    projected = jnp.dot(normed_in, qkv_mat, preferred_element_type=jnp.float32).astype(jnp.bfloat16)
    logits = jnp.dot(normed_in, beta_full, preferred_element_type=jnp.float32)
    edge_rows = passed_along(projected[row_count - edge_count :], "seq", 1)
    extended = jnp.concatenate([edge_rows, projected], axis=0).astype(jnp.float32)
    conv_mat = conv_weight.reshape(TAPS, 3 * inner_width)

    def inputs_of(extended_rows, logit_rows, tap_rows):
        return mixer_inputs(extended_rows, logit_rows, tap_rows, offset, local_heads)

    (queries, key_rows, values, strength), inputs_back = jax.vjp(
        inputs_of, extended, logits, conv_mat
    )

    def maps_of(query_rows, key_part, value_part, strength_part):
        return local_rule(query_rows, key_part, value_part, strength_part, keep, local_heads, HEAD)

    (zero_out, reach, maps, carried, product), rule_back = jax.vjp(
        maps_of, queries, key_rows, values, strength
    )
    zero_state = jnp.zeros((local_heads, HEAD, HEAD), jnp.float32)

    def relay_turn(turn, state_now):
        advanced = jnp.einsum("hde,hef->hdf", product, state_now, precision=PRECISE) + carried
        return passed_along(advanced, "seq", 1)

    incoming = lax.fori_loop(0, lax.axis_size("seq") - 1, relay_turn, zero_state)
    block_states = jnp.einsum("nhde,hef->nhdf", maps, incoming, precision=PRECISE)
    mixer_blocks = zero_out + jnp.einsum("nchd,nhdf->nchf", reach, block_states, precision=PRECISE)
    mixer_out = mixer_blocks.reshape(row_count, local_heads, HEAD)

    def head_norm(mixed_rows, gain_vec):
        return rms_scale(mixed_rows, gain_vec).reshape(row_count, inner_width)

    normed_float, head_norm_back = jax.vjp(head_norm, mixer_out, gain_out)
    normed = normed_float.astype(jnp.bfloat16)
    residual = chain_x + shard_total(jnp.dot(normed, out_full, preferred_element_type=jnp.float32))
    normed_ff_float, norm_ff_back = jax.vjp(rms_scale, residual, gain_ff)
    normed_ff = normed_ff_float.astype(jnp.bfloat16)
    gate_up_out = jnp.dot(normed_ff, gate_up_mat, preferred_element_type=jnp.float32)

    def swiglu(both_rows):
        return jax.nn.silu(both_rows[:, :unit_count]) * both_rows[:, unit_count:]

    hidden_float, swiglu_back = jax.vjp(swiglu, gate_up_out)
    hidden_units = hidden_float.astype(jnp.bfloat16)
    result = residual + shard_total(
        jnp.dot(hidden_units, down_full, preferred_element_type=jnp.float32)
    )
    qkv_full, beta_full, gate_up_full, out_full, down_full = (
        lax.all_gather(qkv_weight.astype(jnp.bfloat16), "seq", axis=0, tiled=True),
        lax.all_gather(beta_weight.astype(jnp.bfloat16), "seq", axis=0, tiled=True),
        lax.all_gather(gate_up_weight.astype(jnp.bfloat16), "seq", axis=0, tiled=True),
        lax.all_gather(out_weight.astype(jnp.bfloat16), "seq", axis=1, tiled=True),
        lax.all_gather(down_weight.astype(jnp.bfloat16), "seq", axis=1, tiled=True),
    )
    qkv_mat = qkv_full.reshape(model_width, 3 * inner_width)
    gate_up_mat = gate_up_full.reshape(model_width, 2 * unit_count)
    grad_down = jnp.einsum("tf,td->fd", hidden_units, chain_dy, preferred_element_type=jnp.float32)
    d_hidden = jnp.einsum("td,fd->tf", chain_dy, down_full, preferred_element_type=jnp.float32)
    (d_gate_up,) = swiglu_back(d_hidden)
    d_gate_up_low = d_gate_up.astype(jnp.bfloat16)
    grad_gate_up = jnp.einsum(
        "td,tf->df", normed_ff, d_gate_up_low, preferred_element_type=jnp.float32
    )
    d_normed_ff = shard_total(
        jnp.einsum("tf,df->td", d_gate_up_low, gate_up_mat, preferred_element_type=jnp.float32)
    )
    d_residual_norm, grad_gain_ff = norm_ff_back(d_normed_ff)
    d_residual = chain_dy.astype(jnp.float32) + d_residual_norm
    d_mix = d_residual.astype(jnp.bfloat16)
    grad_out = jnp.einsum("te,td->ed", normed, d_mix, preferred_element_type=jnp.float32)
    d_normed = jnp.einsum("td,ed->te", d_mix, out_full, preferred_element_type=jnp.float32)
    d_mixer_out, grad_gain_out = head_norm_back(d_normed)
    d_blocks = d_mixer_out.reshape(mixer_blocks.shape)
    d_reach = jnp.einsum("nchf,nhdf->nchd", d_blocks, block_states, precision=PRECISE)
    d_block_states = jnp.einsum("nchd,nchf->nhdf", reach, d_blocks, precision=PRECISE)
    local_term = jnp.einsum("nhde,nhdf->hef", maps, d_block_states, precision=PRECISE)
    flipped = jnp.swapaxes(product, 1, 2)

    def back_turn(turn, grad_now):
        advanced = jnp.einsum("hde,hef->hdf", flipped, grad_now, precision=PRECISE) + local_term
        return passed_along(advanced, "seq", -1)

    outgoing = lax.fori_loop(0, lax.axis_size("seq") - 1, back_turn, zero_state)
    d_maps = jnp.einsum("nhdf,hef->nhde", d_block_states, incoming, precision=PRECISE)
    d_product = jnp.einsum("hdf,hef->hde", outgoing, incoming, precision=PRECISE)
    d_queries, d_key_rows, d_values, d_strength = rule_back(
        (d_blocks, d_reach, d_maps, outgoing, d_product)
    )
    grad_extended, d_logits, grad_taps = inputs_back((d_queries, d_key_rows, d_values, d_strength))
    from_next = passed_along(grad_extended[:edge_count], "seq", -1)
    d_projected = grad_extended[edge_count:].at[row_count - edge_count :].add(from_next)
    d_projected_low = d_projected.astype(jnp.bfloat16)
    d_logits_low = d_logits.astype(jnp.bfloat16)
    grad_qkv = jnp.einsum(
        "td,tc->dc", normed_in, d_projected_low, preferred_element_type=jnp.float32
    )
    grad_beta = jnp.einsum("td,th->dh", normed_in, d_logits_low, preferred_element_type=jnp.float32)
    d_normed_in_part = jnp.einsum(
        "tc,dc->td", d_projected_low, qkv_mat, preferred_element_type=jnp.float32
    ) + jnp.einsum("th,dh->td", d_logits_low, beta_full, preferred_element_type=jnp.float32)
    d_normed_in, grad_gain_out = lax.psum((d_normed_in_part, grad_gain_out), "shard")
    d_input_norm, grad_gain_in = norm_in_back(d_normed_in)
    d_input = d_residual + d_input_norm
    red_qkv, red_beta, red_gate_up, red_out, red_down = (
        lax.psum_scatter(
            grad_qkv.reshape(model_width, 3, inner_width), "seq", scatter_dimension=0, tiled=True
        ),
        lax.psum_scatter(grad_beta, "seq", scatter_dimension=0, tiled=True),
        lax.psum_scatter(
            grad_gate_up.reshape(model_width, 2, unit_count), "seq", scatter_dimension=0, tiled=True
        ),
        lax.psum_scatter(grad_out, "seq", scatter_dimension=1, tiled=True),
        lax.psum_scatter(grad_down, "seq", scatter_dimension=1, tiled=True),
    )
    grad_gains = jnp.concatenate([grad_gain_in, grad_gain_ff, grad_gain_out])
    red_gains, red_conv = lax.psum((grad_gains, grad_taps.reshape(TAPS, 3, inner_width)), "seq")
    qkv_new = adamw(qkv_weight, qkv_first, qkv_second, red_qkv, RATE_WIDE, SHRINK)
    beta_new = adamw(beta_weight, beta_first, beta_second, red_beta, RATE_WIDE, SHRINK)
    out_new = adamw(out_weight, out_first, out_second, red_out, RATE_WIDE, SHRINK)
    gate_up_new = adamw(
        gate_up_weight, gate_up_first, gate_up_second, red_gate_up, RATE_WIDE, SHRINK
    )
    down_new = adamw(down_weight, down_first, down_second, red_down, RATE_DOWN, SHRINK)
    conv_new = adamw(conv_weight, conv_first, conv_second, red_conv, RATE_CONV, 0.0)
    gains_new = adamw(gains, gains_first, gains_second, red_gains, RATE_GAIN, 0.0)
    back_out, back_grad = (
        lax.all_to_all(
            result.astype(jnp.bfloat16)[got_place], "seq", split_axis=0, concat_axis=0, tiled=True
        ),
        lax.all_to_all(
            d_input.astype(jnp.bfloat16)[got_place], "seq", split_axis=0, concat_axis=0, tiled=True
        ),
    )
    restore = jnp.argsort(order)
    return (
        back_out[restore],
        back_grad[restore],
        qkv_new[0],
        qkv_new[1],
        qkv_new[2],
        beta_new[0],
        beta_new[1],
        beta_new[2],
        out_new[0],
        out_new[1],
        out_new[2],
        gate_up_new[0],
        gate_up_new[1],
        gate_up_new[2],
        down_new[0],
        down_new[1],
        down_new[2],
        conv_new[0],
        conv_new[1],
        conv_new[2],
        gains_new[0],
        gains_new[1],
        gains_new[2],
    )


def solution(mesh):
    return jax.shard_map(
        per_device,
        mesh=mesh,
        in_specs=(
            P("seq", None),
            P("seq", None),
            P("seq"),
            P(),
            P("seq", None, "shard"),
            P("seq", None, "shard"),
            P("seq", None, "shard"),
            P("seq", "shard"),
            P("seq", "shard"),
            P("seq", "shard"),
            P("shard", "seq"),
            P("shard", "seq"),
            P("shard", "seq"),
            P("seq", None, "shard"),
            P("seq", None, "shard"),
            P("seq", None, "shard"),
            P("shard", "seq"),
            P("shard", "seq"),
            P("shard", "seq"),
            P(None, None, "shard"),
            P(None, None, "shard"),
            P(None, None, "shard"),
            P(),
            P(),
            P(),
        ),
        out_specs=(
            P("seq", None),
            P("seq", None),
            P("seq", None, "shard"),
            P("seq", None, "shard"),
            P("seq", None, "shard"),
            P("seq", "shard"),
            P("seq", "shard"),
            P("seq", "shard"),
            P("shard", "seq"),
            P("shard", "seq"),
            P("shard", "seq"),
            P("seq", None, "shard"),
            P("seq", None, "shard"),
            P("seq", None, "shard"),
            P("shard", "seq"),
            P("shard", "seq"),
            P("shard", "seq"),
            P(None, None, "shard"),
            P(None, None, "shard"),
            P(None, None, "shard"),
            P(),
            P(),
            P(),
        ),
        check_vma=False,
    )
```

profile of v0, /device:TPU:0, one launch (start us, length us, event | category | flops | bytes accessed | tf_op | source)
XLA Modules:
  0.0 4234.4 jit_solution(12107768504949259279)
XLA Ops:
  43.2 62.6 %all_gather.21 = bf16[2048,4]{0,1:T(4,128)(2,1)S(1)} all-gather(bf16[256,4]{0,1:T(4,128)(2,1)S(1)} %convert_element_type.155), channel_id=1, replica_groups=mesh['seq'=8,'shard'=4] {'seq'}, dimensions={0}, use_global_device_ids=true | all-gather | bytes 18432 | tf_op jit(solution)/shard_map/all_gather | solution.py:188
  111.4 11.6 gather_fusion.2
  182.1 716.5 %while.95 = (s32[]{:T(128)}, f32[4,128,128]{2,1,0:T(8,128)S(1)}, f32[4,128,128]{2,1,0:T(8,128)S(1)}, f32[16,64,4,128]{3,1,2,0:T(8,128)}, f32[16,64,4,128]{3,1,2,...) while((s32[]{:T(128)}, f32[4,128,128]{2,1,0:T(8,128)S(1)}, ...), condition=%wide.region_8.9_spmd.clone.clone, body=%wide.region_7.8_spmd.clone.clone.sunk | while | flops 454299712 | bytes 10483474 | solution.py:115
  185.2 19.7 custom-call.56
  230.0 19.7 custom-call.56
  274.7 19.7 custom-call.56
  319.6 19.7 custom-call.56
  364.3 19.7 custom-call.56
  409.1 19.7 custom-call.56
  453.9 19.7 custom-call.56
  498.7 19.7 custom-call.56
  543.5 19.7 custom-call.56
  588.2 19.7 custom-call.56
  633.0 19.7 custom-call.56
  677.8 19.7 custom-call.56
  722.6 19.7 custom-call.56
  767.4 19.7 custom-call.56
  812.1 19.7 custom-call.56
  856.9 19.7 custom-call.56
  898.7 60.6 %while.92 = (s32[]{:T(128)}, f32[4,128,128]{2,1,0:T(8,128)S(1)}, f32[4,128,128]{2,1,0:T(8,128)S(1)}, f32[4,128,128]{2,1,0:T(8,128)S(1)}, s32[]{:T(128)}) while((s32[]{:T(128)}, f32[4,128,128]{2,1,0:T(8,128)S(1)}, f32[4,128,128]{2,1,0:T(8,128)S(1)}, f32[4,128,128]{2,1,0:T(8,128)S(1)}, s32[]{:T(128)}) %tuple.202), condition=%wide.region_10.11_spmd, body=%wide.region_9.10_spmd.sunk | while | flops 100728832 | bytes 2097253 | solution.py:226
  995.7 11.6 gather_fusion.5
  1007.3 65.5 %all_to_all.60 = bf16[8,128,2048]{2,1,0:T(8,128)(2,1)} all-to-all(bf16[8,128,2048]{2,1,0:T(8,128)(2,1)} %bitcast.605), channel_id=1, replica_groups=mesh['seq'=8,'shard'=4] {'seq'}, dimensions={0} | all-to-all | bytes 8388608 | tf_op jit(solution)/shard_map/all_to_all | solution.py:174
  1072.8 11.6 gather_fusion.6
  1084.3 209.6 %all-reduce.23.cloned.1.call-done = f32[1024,2048]{1,0:T(8,128)} async-done(((f32[1024,2048]{1,0:T(8,128)}), f32[1024,2048]{1,0:T(8,128)}) %all-reduce.23.cloned.1.call-update) | async-done | bytes 8388624 | tf_op jit(solution)/shard_map/psum | solution.py:124
  1303.1 59.8 %all-gather.9.cloned.1.call-done = bf16[2048,2,1408]{2,1,0:T(2,128)(2,1)} async-done(((bf16[256,2,1408]{2,1,0:T(2,128)(2,1)}), bf16[2048,2,1408]{2,1,0:T(2,128)(2,1)}) %all-gather.9.cloned.1.call-update) | async-done | bytes 11534352 | tf_op jit(solution)/shard_map/all_gather | solution.py:189
  1375.3 15.2 fusion.245
  1390.5 19.2 all-gather.11.cloned.1.call-done
  1409.6 17.4 fusion.223
  1427.1 19.8 fusion.222
  1449.8 11.6 fusion.263
  1461.4 276.5 %all-reduce.25.cloned.1.call-done = f32[1024,2048]{1,0:T(8,128)} async-done(((f32[1024,2048]{1,0:T(8,128)}), f32[1024,2048]{1,0:T(8,128)}) %all-reduce.25.cloned.1.call-update) | async-done | bytes 8388624 | tf_op jit(solution)/shard_map/psum | solution.py:124
  1792.0 51.8 %while.93 = (s32[]{:T(128)}, f32[4,128,128]{2,1,0:T(8,128)S(1)}, f32[4,128,128]{2,1,0:T(8,128)S(1)}, f32[4,128,128]{2,1,0:T(8,128)S(1)}, s32[]{:T(128)}) while((s32[]{:T(128)}, f32[4,128,128]{2,1,0:T(8,128)S(1)}, f32[4,128,128]{2,1,0:T(8,128)S(1)}, f32[4,128,128]{2,1,0:T(8,128)S(1)}, s32[]{:T(128)}) %tuple.205), condition=%wide.region_20.21_spmd, body=%wide.region_19.20_spmd.sunk | while | flops 100728832 | bytes 2097253 | solution.py:284
  1850.7 1045.9 %while.94 = (s32[]{:T(128)}, f32[4,128,128]{2,1,0:T(8,128)S(1)}, f32[4,128,128]{2,1,0:T(8,128)}, f32[16,64,4,128]{3,1,2,0:T(8,128)}, f32[16,64,4,128]{3,1,2,0:T(...) while((s32[]{:T(128)}, f32[4,128,128]{2,1,0:T(8,128)S(1)}, ...), condition=%wide.region_25.26_spmd.clone, body=%wide.region_21.25_spmd.clone.sunk | while | flops 920170304 | bytes 16140669 | solution.py:115
  1861.4 19.7 custom-call.55
  1926.8 19.7 custom-call.55
  1992.1 19.7 custom-call.55
  2057.5 19.7 custom-call.55
  2122.8 19.7 custom-call.55
  2188.2 19.7 custom-call.55
  2253.5 19.7 custom-call.55
  2318.8 19.7 custom-call.55
  2384.2 19.7 custom-call.55
  2449.6 19.7 custom-call.55
  2514.9 19.7 custom-call.55
  2580.2 19.7 custom-call.55
  2645.6 19.7 custom-call.55
  2710.9 19.7 custom-call.55
  2776.3 19.7 custom-call.55
  2841.6 19.7 custom-call.55
  2967.5 13.8 convolution_add_fusion.12
  2986.9 22.8 fusion.221
  3009.6 26.9 reshape.573
  3059.7 12.2 fusion.214
  3071.9 12.7 copy.287
  3085.3 470.3 %all-reduce.29.cloned.1.call-done = (f32[1024,2048]{1,0:T(8,128)}, f32[1024,2048]{1,0:T(8,128)}) async-done(((f32[1024,2048]{1,0:T(8,128)}, f32[1024,2048]{1,0:T(8,128)}), (f32[1024,2048]{1,0:T(8,128)}, f32[1024,2048]{1,0:T(8,128)})) %all-reduce.29.cloned.1.call-update) | async-done | bytes 16777232 | tf_op jit(solution)/shard_map/psum | solution.py:124
  3570.2 11.6 gather_fusion.7
  3613.3 11.8 gather_fusion.3
  3625.1 34.3 all-to-all-done.4
  3664.5 293.1 %all-reduce.27.cloned.1.call-done = f32[2048,2,1408]{2,1,0:T(2,128)} async-done(((f32[2048,2,1408]{2,1,0:T(2,128)}), f32[2048,2,1408]{2,1,0:T(2,128)}) %all-reduce.27.cloned.1.call-update) | async-done | bytes 23068688
  3957.6 12.6 multiply_subtract_fusion
  3970.2 42.4 %reduce-scatter.9.cloned.1.call-done = f32[512,256]{1,0:T(8,128)} async-done(((f32[512,2048]{1,0:T(8,128)}), f32[512,256]{1,0:T(8,128)}) %reduce-scatter.9.cloned.1.call-update) | async-done | bytes 524304 | tf_op jit(solution)/shard_map/reduce_scatter | solution.py:313
  4015.4 87.5 %reduce-scatter.11.cloned.1.call-done = f32[1408,256]{1,0:T(8,128)} async-done(((f32[1408,2048]{1,0:T(8,128)}), f32[1408,256]{1,0:T(8,128)}) %reduce-scatter.11.cloned.1.call-update) | async-done | bytes 1441808 | tf_op jit(solution)/shard_map/reduce_scatter | solution.py:314
  4107.8 23.6 all-reduce.16
  4132.7 65.9 %reduce-scatter.7.cloned.1.call-done = f32[256,3,512]{2,0,1:T(8,128)} async-done(((f32[2048,3,512]{2,0,1:T(8,128)}), f32[256,3,512]{2,0,1:T(8,128)}) %reduce-scatter.7.cloned.1.call-update) | async-done | bytes 1572880 | tf_op jit(solution)/shard_map/reduce_scatter | solution.py:306
  (1594 shorter events, 1639.6 us)
Async XLA Ops:
  7.2 119.6 %all-gather.5.cloned.1.call-start = ((), (), s32[]{:S(2)}) async-start(), calls=%async_computation.9 | async-start | bytes 7077888 | tf_op jit(solution)/shard_map/all_gather | solution.py:187
  14.9 21.9 copy-start.117
  14.9 21.9 copy-start.94
  20.1 16.7 all-to-all-start.1
  36.8 70.3 %copy-start.102 = (s32[8,128,1]{1,2,0:T(1,128)}, s32[8,128,1]{1,2,0:T(1,128)S(1)}, u32[]{:S(2)}) copy-start(s32[8,128,1]{1,2,0:T(1,128)S(1)} %all-to-all-done.1) | copy-start | bytes 12292
  36.9 74.6 %all-to-all-start = ((bf16[8,128,2048]{2,1,0:T(8,128)(2,1)}), bf16[8,128,2048]{2,1,0:T(8,128)(2,1)}, u32[]{:S(2)}, u32[]{:S(2)}) async-start(bf16[8,128,2048]{2,1,0:T(8,128)(2,1)} %bitcast.602), calls=%async_computation | async-start | bytes 8388608 | tf_op jit(solution)/shard_map/all_to_all | solution.py:173
  41.6 941.4 %all-gather.7.cloned.1.call-start = ((), (), s32[]{:S(2)}) async-start(), calls=%async_computation.10 | async-start | bytes 2359296 | tf_op jit(solution)/shard_map/all_gather | solution.py:190
  42.4 1251.5 %all-reduce.23.cloned.1.call-start = ((), (), s32[]{:S(2)}) async-start(), calls=%async_computation.11 | async-start | bytes 16777216 | tf_op jit(solution)/shard_map/psum | solution.py:124
  42.9 102.7 %copy-start.73 = (f32[1536]{0:T(1024)}, f32[1536]{0:T(1024)S(1)}, u32[]{:S(2)}) copy-start(f32[1536]{0:T(1024)S(1)} %mul.975) | copy-start | bytes 18436
  42.9 102.7 %copy-start.75 = (f32[1536]{0:T(1024)}, f32[1536]{0:T(1024)S(1)}, u32[]{:S(2)}) copy-start(f32[1536]{0:T(1024)S(1)} %mul.985) | copy-start | bytes 18436
  42.9 102.7 %copy-start.77 = (f32[1536]{0:T(1024)}, f32[1536]{0:T(1024)S(1)}, u32[]{:S(2)}) copy-start(f32[1536]{0:T(1024)S(1)} %mul.990) | copy-start | bytes 18436
  43.0 102.6 %copy-start.79 = (f32[1536]{0:T(1024)}, f32[1536]{0:T(1024)S(1)}, u32[]{:S(2)}) copy-start(f32[1536]{0:T(1024)S(1)} %mul.995) | copy-start | bytes 18436
  43.1 102.5 %copy-start.83 = (f32[1024]{0:T(1024)}, f32[1024]{0:T(1024)S(1)}, u32[]{:S(2)}) copy-start(f32[1024]{0:T(1024)S(1)} %get-tuple-element.1498) | copy-start | bytes 12292
  43.2 63.7 %copy-start.121 = (f32[128]{0:T(128)}, f32[128]{0:T(128)S(1)}, u32[]{:S(2)}) copy-start(f32[128]{0:T(128)S(1)} %slice.122) | copy-start | bytes 1540
  105.8 34.7 copy-start.91
  107.0 38.6 copy-start.85
  107.0 38.6 copy-start.87
  107.0 38.6 copy-start.89
  107.0 33.5 copy-start.71
  107.0 1263.8 %copy-start.68 = (f32[2048]{0:T(1024)}, f32[2048]{0:T(1024)S(1)}, u32[]{:S(2)}) copy-start(f32[2048]{0:T(1024)S(1)} %get-tuple-element.1541) | copy-start | bytes 24580
  137.7 6.2 collective-permute-start.2
  898.7 66.3 %copy-start.26 = (f32[16,64,4,128]{3,1,2,0:T(8,128)}, f32[16,64,4,128]{3,1,2,0:T(8,128)S(1)}, u32[]{:S(2)}) copy-start(f32[16,64,4,128]{3,1,2,0:T(8,128)S(1)} %get-tuple-element.794) | copy-start | bytes 6291460
  910.0 2.8 collective-permute-start
  913.2 5.7 collective-permute-start
  919.3 7.7 collective-permute-start
  927.4 7.7 collective-permute-start
  935.5 7.7 collective-permute-start
  943.5 7.7 collective-permute-start
  951.6 7.7 collective-permute-start
  990.6 372.4 %all-gather.9.cloned.1.call-start = ((), (), s32[]{:S(2)}) async-start(), calls=%async_computation.12 | async-start | bytes 12976128 | tf_op jit(solution)/shard_map/all_gather | solution.py:189
  994.6 415.0 %all-gather.11.cloned.1.call-start = ((), (), s32[]{:S(2)}) async-start(), calls=%async_computation.13 | async-start | bytes 6488064 | tf_op jit(solution)/shard_map/all_gather | solution.py:191
  995.6 742.2 %all-reduce.25.cloned.1.call-start = ((), (), s32[]{:S(2)}) async-start(), calls=%async_computation.14 | async-start | bytes 16777216 | tf_op jit(solution)/shard_map/psum | solution.py:124
  1007.3 65.5 %copy-start.99 = (s32[1024]{0:T(1024)S(1)}, s32[1024]{0:T(1024)}, u32[]{:S(2)}) copy-start(s32[1024]{0:T(1024)} %copy-done.98) | copy-start | bytes 12292
  1303.1 442.5 %copy-start.96 = (f32[1024]{0:T(1024)}, f32[1024]{0:T(1024)S(1)}, u32[]{:S(2)}) copy-start(f32[1024]{0:T(1024)S(1)} %fusion.241) | copy-start | bytes 12292
  1446.9 2108.7 %all-reduce.29.cloned.1.call-start = ((), (), s32[]{:S(2)}) async-start(), calls=%async_computation.20 | async-start | bytes 33554432 | tf_op jit(solution)/shard_map/psum | solution.py:124
  1449.8 288.1 %copy-start.69 = (f32[2048]{0:T(1024)S(1)}, f32[2048]{0:T(1024)}, u32[]{:S(2)}) copy-start(f32[2048]{0:T(1024)} %copy-done.68) | copy-start | bytes 24580
  1792.4 3.4 collective-permute-start.1
  1796.2 7.1 collective-permute-start.1
  1803.7 7.7 collective-permute-start.1
  1811.8 7.7 collective-permute-start.1
  1819.9 7.7 collective-permute-start.1
  1828.0 7.7 collective-permute-start.1
  1836.0 7.7 collective-permute-start.1
  2954.3 9.4 collective-permute-start.3
  2981.4 620.6 %reduce-scatter.13.cloned.1.call-start = ((), (), s32[]{:S(2)}) async-start(), calls=%async_computation.18 | async-start | bytes 1179648
  2986.8 970.8 %all-reduce.27.cloned.1.call-start = ((), (), s32[]{:S(2)}) async-start(), calls=%async_computation.19 | async-start | bytes 46137344
  3036.5 976.0 %reduce-scatter.9.cloned.1.call-start = ((), (), s32[]{:S(2)}) async-start(), calls=%async_computation.16 | async-start | bytes 4718592 | tf_op jit(solution)/shard_map/reduce_scatter | solution.py:313
  3045.5 1057.3 %reduce-scatter.11.cloned.1.call-start = ((), (), s32[]{:S(2)}) async-start(), calls=%async_computation.17 | async-start | bytes 12976128 | tf_op jit(solution)/shard_map/reduce_scatter | solution.py:314
  3057.7 1140.9 %reduce-scatter.7.cloned.1.call-start = ((), (), s32[]{:S(2)}) async-start(), calls=%async_computation.15 | async-start | bytes 14155776 | tf_op jit(solution)/shard_map/reduce_scatter | solution.py:306
  3581.8 21.1 copy-start.116
  3581.8 77.6 %all-to-all-start.4 = ((bf16[8,128,2048]{2,1,0:T(8,128)(2,1)}), bf16[8,128,2048]{2,1,0:T(8,128)(2,1)}, u32[]{:S(2)}, u32[]{:S(2)}) async-start(bf16[8,128,2048]{2,1,0:T(8,128)(2,1)} %bitcast.604), calls=%async_computation.4 | async-start | bytes 8388608 | tf_op jit(solution)/shard_map/all_to_all | solution.py:331
  3659.4 298.2 %copy-start.33 = (f32[256,2,1408]{2,1,0:T(2,128)S(1)}, f32[256,2,1408]{2,1,0:T(2,128)}, u32[]{:S(2)}) copy-start(f32[256,2,1408]{2,1,0:T(2,128)} %param.48) | copy-start | bytes 8650756
  3659.4 556.2 %all-to-all-start.2 = ((bf16[8,128,2048]{2,1,0:T(8,128)(2,1)}), bf16[8,128,2048]{2,1,0:T(8,128)(2,1)}, u32[]{:S(2)}, u32[]{:S(2)}) async-start(bf16[8,128,2048]{2,1,0:T(8,128)(2,1)} %bitcast.603), calls=%async_computation.2 | async-start | bytes 8388608 | tf_op jit(solution)/shard_map/all_to_all | solution.py:328
  3664.5 348.0 %copy-start.49 = (f32[512,256]{1,0:T(8,128)S(1)}, f32[512,256]{1,0:T(8,128)}, u32[]{:S(2)}) copy-start(f32[512,256]{1,0:T(8,128)} %param.45) | copy-start | bytes 1572868
  3970.2 132.7 %copy-start.43 = (f32[1408,256]{1,0:T(8,128)S(1)}, f32[1408,256]{1,0:T(8,128)}, u32[]{:S(2)}) copy-start(f32[1408,256]{1,0:T(8,128)} %param.51) | copy-start | bytes 4325380
  4015.3 92.5 %copy-start.110 = (f32[2048]{0:T(1024)S(1)}, f32[2048]{0:T(1024)}, u32[]{:S(2)}) copy-start(f32[2048]{0:T(1024)} %get-tuple-element.1340) | copy-start | bytes 24580
  4015.3 92.5 %copy-start.65 = (f32[4,1536]{1,0:T(4,128)S(1)}, f32[4,1536]{1,0:T(4,128)}, u32[]{:S(2)}) copy-start(f32[4,1536]{1,0:T(4,128)} %pad_add_fusion.5) | copy-start | bytes 73732
  4015.3 116.1 %copy-start.82 = (f32[4224]{0:T(1024)S(1)}, f32[4224]{0:T(1024)}, u32[]{:S(2)}) copy-start(f32[4224]{0:T(1024)} %param.57) | copy-start | bytes 50692
  4015.3 116.1 %copy-start.113 = (f32[4224]{0:T(1024)S(1)}, f32[4224]{0:T(1024)}, u32[]{:S(2)}) copy-start(f32[4224]{0:T(1024)} %param.58) | copy-start | bytes 50692
  4015.3 116.1 %copy-start.114 = (f32[4224]{0:T(1024)S(1)}, f32[4224]{0:T(1024)}, u32[]{:S(2)}) copy-start(f32[4224]{0:T(1024)} %param.59) | copy-start | bytes 50692
  4015.3 116.7 %copy-start.67 = (f32[4,3,512]{2,0,1:T(4,128)S(1)}, f32[4,3,512]{2,0,1:T(4,128)}, u32[]{:S(2)}) copy-start(f32[4,3,512]{2,0,1:T(4,128)} %param.54) | copy-start | bytes 73732
  4015.3 116.7 %copy-start.111 = (f32[4,3,512]{2,0,1:T(4,128)S(1)}, f32[4,3,512]{2,0,1:T(4,128)}, u32[]{:S(2)}) copy-start(f32[4,3,512]{2,0,1:T(4,128)} %param.55) | copy-start | bytes 73732
  4015.3 116.7 %copy-start.112 = (f32[4,3,512]{2,0,1:T(4,128)S(1)}, f32[4,3,512]{2,0,1:T(4,128)}, u32[]{:S(2)}) copy-start(f32[4,3,512]{2,0,1:T(4,128)} %param.56) | copy-start | bytes 73732
  4015.4 183.3 %copy-start.41 = (f32[256,3,512]{2,0,1:T(8,128)S(1)}, f32[256,3,512]{2,0,1:T(8,128)}, u32[]{:S(2)}) copy-start(f32[256,3,512]{2,0,1:T(8,128)} %param.39) | copy-start | bytes 4718596
  (120 other events, 806.5 us)
Sparse Core Ops, SparseCore 0:
  10.5 62.6 all-gather.4
  75.7 49.6 all-gather.6
  990.7 303.1 all-reduce.22
  1296.2 66.6 all-gather.8
  1365.2 44.3 all-gather.10
  1447.0 290.8 all-reduce.24
  2981.4 574.1 all-reduce.28
  3559.4 36.4 reduce-scatter.12
  3599.7 357.9 all-reduce.26
  3961.2 51.3 reduce-scatter.8
  4016.1 86.7 reduce-scatter.10
  4106.2 92.3 reduce-scatter.6
where the time goes:
time: 4260 us; the launch traced here: 4230 us
  waiting for transfers between devices  1610 us (38%)
  matrix products  989 us (23%)
  other arithmetic  891 us (21%)
  local copies, waits for them, and re-layouts  482 us (11%)
  blocking collectives  161 us (4%)
  starting transfers between devices  72.3 us (2%)
    psum x3, waiting for transfers between devices, shard_total(): return lax.psum(values, 'shard')  956 us
    another operation x144, other arithmetic, group_step(): jax.scipy.linalg.solve_triangular(system, right_side, lower=True, unit_di...  648 us
    unnamed x14, waiting for transfers between devices  293 us
    dynamic_slice x144, local copies, waits for them, and re-layouts, local_rule(): lax.scan(group_step, (zero_state, identity), (to_groups(queries), to_grou...  128 us
    dot_general x48, matrix products, group_step(): jnp.einsum('hcd,hde->hce', queries, state_start, precision=PRECISE)  101 us
    dynamic_update_slice x80, local copies, waits for them, and re-layouts, local_rule(): lax.scan(group_step, (zero_state, identity), (to_groups(queries), to_grou...  94.7 us
    dot_general x48, matrix products, group_step(): jnp.einsum('hcd,hce->hde', key_rows, fresh_values, precision=PRECISE)  89.7 us
    dot_general x48, matrix products, group_step(): product = jnp.einsum('hde,hef->hdf', factor, start_map, precision=PRECISE)  88.8 us
  transfers between devices with their start and end apart: 32, of which 24 were waited for; matrix products, arithmetic and copies ran while one was open for 26% of the time, Pallas kernels for 0%

commit v1 on v0

v1 whole, which is shorter than its diff:
```python
import functools

import jax
import jax.numpy as jnp
from jax import lax
from jax.experimental import pallas as pl
from jax.experimental.pallas import tpu as pltpu
from jax.sharding import PartitionSpec as P

HEAD = 128
TAPS = 4
GROUP = 64
STEP = 10


EPSILON = 1e-06
PRECISE = lax.Precision.HIGHEST
FIRST_DECAY = 0.9
SECOND_DECAY = 0.95
ADAM_EPSILON = 1e-08
RATE_WIDE = 0.044
RATE_DOWN = 0.027
RATE_CONV = 0.8
RATE_GAIN = 0.3
SHRINK = 0.1


def halves(value):
    high = value.astype(jnp.bfloat16)
    return high, (value - high.astype(jnp.float32)).astype(jnp.bfloat16)


def mul(left, right, dims=((1,), (0,))):
    def one(a, b):
        return lax.dot_general(a, b, (dims, ((), ())), preferred_element_type=jnp.float32)

    left_high, left_low = halves(left)
    right_high, right_low = halves(right)
    return one(left_high, right_high) + (one(left_high, right_low) + one(left_low, right_high))


def mul_nt(left, right):
    return mul(left, right, ((1,), (1,)))


def grid_indices(size):
    return (
        lax.broadcasted_iota(jnp.int32, (size, size), 0),
        lax.broadcasted_iota(jnp.int32, (size, size), 1),
    )


def unit_lower_inverse(strict_part):
    size = strict_part.shape[0]
    rows, cols = grid_indices(size)
    inverse = (rows == cols).astype(jnp.float32)
    level = 0
    while (1 << level) < size:
        corner = (
            ((rows >> (level + 1)) == (cols >> (level + 1)))
            & (((rows >> level) & 1) == 1)
            & (((cols >> level) & 1) == 0)
        )
        part = jnp.where(corner, strict_part, 0.0)
        if level == 0:
            inverse = inverse - part
        else:
            inverse = inverse - mul(inverse, mul(part, inverse))
        level += 1
    return inverse


def sigmoid(value):
    return 1.0 / (1.0 + jnp.exp(-value))


def unit_scale(act):
    return lax.rsqrt(jnp.sum(act * act, axis=-1, keepdims=True) + EPSILON)


def maps_kernel(
    heads,
    keep_ref,
    pre_ref,
    edge_ref,
    logit_ref,
    taps_ref,
    conv_ref,
    solved_ref,
    square_ref,
    step_ref,
    fresh_ref,
    reach_ref,
    zero_out_ref,
    total_ref,
    history,
    running,
):
    block = pl.program_id(0)
    keep = keep_ref[block]
    scale = HEAD**-0.5

    @pl.when(block == 0)
    def _():
        history[0:8, :] = edge_ref[...] * keep
        rows, cols = grid_indices(HEAD)
        start = jnp.where(rows == cols, 1.0, 0.0)
        for head in range(heads):
            running[head, :, 0:HEAD] = start
            running[head, :, HEAD : 2 * HEAD] = jnp.zeros((HEAD, HEAD), jnp.float32)

    @pl.when(block > 0)
    def _():
        history[0:8, :] = history[GROUP : GROUP + 8, :] * keep

    history[8 : GROUP + 8, :] = pre_ref[...].astype(jnp.float32)

    def conv_of(column):
        cols = slice(column * HEAD, (column + 1) * HEAD)
        total = taps_ref[0:1, cols] * history[5 : 5 + GROUP, cols]
        for tap in range(1, TAPS):
            total = total + taps_ref[tap : tap + 1, cols] * history[5 + tap : 5 + tap + GROUP, cols]
        conv_ref[:, cols] = total
        return total * sigmoid(total)

    rows, cols = grid_indices(GROUP)
    for head in range(heads):
        lanes = slice(head * HEAD, (head + 1) * HEAD)
        query = conv_of(head)
        query = query * unit_scale(query)
        key = conv_of(heads + head)
        key = key * unit_scale(key)
        value = conv_of(2 * heads + head)
        strength = sigmoid(logit_ref[:, head : head + 1])
        overlap = mul_nt(key, key)
        scores = jnp.where(rows >= cols, mul_nt(query, key), 0.0)
        inverse = unit_lower_inverse(jnp.where(rows > cols, strength * overlap, 0.0))
        solved = mul(inverse, jnp.concatenate([strength * key, strength * value], axis=1))
        solved_ref[head] = solved
        square_ref[head, :, 0:GROUP] = inverse
        square_ref[head, :, GROUP : 2 * GROUP] = scores
        mixed = mul(scores, solved)
        reach_ref[:, lanes] = scale * (query - mixed[:, 0:HEAD])
        zero_out_ref[:, lanes] = scale * mixed[:, HEAD:]
        pushed = mul(key.T, solved)
        big_rows, big_cols = grid_indices(HEAD)
        step = jnp.where(big_rows == big_cols, 1.0, 0.0) - pushed[:, 0:HEAD]
        step_ref[head] = step
        fresh_ref[head] = pushed[:, HEAD:]
        moved = mul(step, running[head] * keep)
        running[head, :, 0:HEAD] = moved[:, 0:HEAD]
        running[head, :, HEAD:] = moved[:, HEAD:] + pushed[:, HEAD:]
    total_ref[...] = running[...]


def outputs_kernel(
    heads,
    keep_ref,
    incoming_ref,
    step_ref,
    fresh_ref,
    reach_ref,
    zero_out_ref,
    gain_ref,
    state_ref,
    mixed_ref,
    normed_ref,
    running,
):
    block = pl.program_id(0)
    keep = keep_ref[block]

    @pl.when(block == 0)
    def _():
        running[...] = incoming_ref[...]

    for head in range(heads):
        lanes = slice(head * HEAD, (head + 1) * HEAD)
        state = running[head] * keep
        state_ref[head] = state
        running[head] = mul(step_ref[head], state) + fresh_ref[head]
        mixed = mul(reach_ref[:, lanes], state) + zero_out_ref[:, lanes]
        mixed_ref[:, lanes] = mixed
        inverse_rms = lax.rsqrt(jnp.mean(mixed * mixed, axis=-1, keepdims=True) + EPSILON)
        normed_ref[:, lanes] = (mixed * inverse_rms * gain_ref[...]).astype(jnp.bfloat16)


def tail_kernel(
    heads,
    keep_ref,
    d_normed_ref,
    mixed_ref,
    gain_ref,
    step_ref,
    reach_ref,
    d_mixed_ref,
    d_state_ref,
    d_gain_ref,
    running,
):
    block = pl.num_programs(0) - 1 - pl.program_id(0)
    keep = keep_ref[block]

    @pl.when(pl.program_id(0) == 0)
    def _():
        running[...] = jnp.zeros_like(running)
        d_gain_ref[...] = jnp.zeros_like(d_gain_ref)

    gain_sum = jnp.zeros((1, HEAD), jnp.float32)
    for head in range(heads):
        lanes = slice(head * HEAD, (head + 1) * HEAD)
        mixed = mixed_ref[:, lanes]
        d_normed = d_normed_ref[:, lanes]
        inverse_rms = lax.rsqrt(jnp.mean(mixed * mixed, axis=-1, keepdims=True) + EPSILON)
        unit = mixed * inverse_rms
        gain_sum = gain_sum + jnp.sum(d_normed * unit, axis=0, keepdims=True)
        d_unit = d_normed * gain_ref[...]
        d_mixed = inverse_rms * (d_unit - unit * jnp.mean(d_unit * unit, axis=-1, keepdims=True))
        d_mixed_ref[:, lanes] = d_mixed
        running[head] = keep * (
            mul(step_ref[head].T, running[head]) + mul(reach_ref[:, lanes].T, d_mixed)
        )
    d_gain_ref[...] += gain_sum
    d_state_ref[...] = running[...]


def back_kernel(
    heads,
    keep_ref,
    outgoing_ref,
    pre_ref,
    edge_ref,
    logit_ref,
    taps_ref,
    conv_ref,
    solved_ref,
    square_ref,
    step_ref,
    reach_ref,
    state_ref,
    d_mixed_ref,
    d_pre_ref,
    d_tail_ref,
    d_edge_ref,
    d_logit_ref,
    d_taps_ref,
    d_history,
    edge_history,
    running,
):
    count = pl.num_programs(0)
    block = count - 1 - pl.program_id(0)
    keep = keep_ref[block]
    scale = HEAD**-0.5
    rows, cols = grid_indices(GROUP)

    @pl.when(pl.program_id(0) == 0)
    def _():
        running[...] = outgoing_ref[...]
        d_history[GROUP : GROUP + 8, :] = jnp.zeros((8, d_history.shape[1]), jnp.float32)
        d_taps_ref[...] = jnp.zeros_like(d_taps_ref)

    @pl.when(pl.program_id(0) > 0)
    def _():
        d_history[GROUP : GROUP + 8, :] = d_history[0:8, :] * keep_ref[block + 1]

    def act_of(column):
        conv = conv_ref[:, column * HEAD : (column + 1) * HEAD]
        gate = sigmoid(conv)
        return conv * gate, gate * (1.0 + conv * (1.0 - gate))

    def d_unit(unit, inverse_norm, grad):
        return inverse_norm * (grad - unit * jnp.sum(unit * grad, axis=-1, keepdims=True))

    for head in range(heads):
        lanes = slice(head * HEAD, (head + 1) * HEAD)
        query, query_slope = act_of(head)
        query_scale = unit_scale(query)
        query = query * query_scale
        key, key_slope = act_of(heads + head)
        key_scale = unit_scale(key)
        key = key * key_scale
        value, value_slope = act_of(2 * heads + head)
        strength = sigmoid(logit_ref[:, head : head + 1])
        solved = solved_ref[head]
        inverse = square_ref[head, :, 0:GROUP]
        scores = square_ref[head, :, GROUP : 2 * GROUP]
        state = state_ref[head]
        d_state = running[head]
        d_mixed = d_mixed_ref[:, lanes]
        d_out = scale * d_mixed
        running[head] = keep * (
            mul(step_ref[head].T, d_state) + mul(reach_ref[:, lanes].T, d_mixed)
        )
        overlap = mul_nt(key, key)
        fresh = solved[:, HEAD:] - mul(solved[:, 0:HEAD], state)
        d_fresh = mul(scores.T, d_out) + mul(key, d_state)
        d_scores = jnp.where(rows >= cols, mul_nt(d_out, fresh), 0.0)
        d_query = mul_nt(d_out, state) + mul(d_scores, key)
        d_key = mul(d_scores.T, query) + mul_nt(fresh, d_state)
        d_solved = jnp.concatenate([-mul_nt(d_fresh, state), d_fresh], axis=1)
        d_right = mul(inverse.T, d_solved)
        d_strict = jnp.where(rows > cols, -mul_nt(d_right, solved), 0.0)
        d_overlap = strength * d_strict
        d_key = (
            d_key + strength * d_right[:, 0:HEAD] + mul(d_overlap + d_overlap.T, key)
        )
        d_value = strength * d_right[:, HEAD:]
        d_strength = (
            jnp.sum(d_right[:, 0:HEAD] * key, axis=-1, keepdims=True)
            + jnp.sum(d_right[:, HEAD:] * value, axis=-1, keepdims=True)
            + jnp.sum(d_strict * overlap, axis=-1, keepdims=True)
        )
        d_logit_ref[:, head : head + 1] = d_strength * strength * (1.0 - strength)
        for column, d_conv in (
            (head, d_unit(query, query_scale, d_query) * query_slope),
            (heads + head, d_unit(key, key_scale, d_key) * key_slope),
            (2 * heads + head, d_value * value_slope),
        ):
            d_history[0:GROUP, column * HEAD : (column + 1) * HEAD] = d_conv

    for column in range(3 * heads):
        lanes = slice(column * HEAD, (column + 1) * HEAD)
        pre = pre_ref[:, lanes].astype(jnp.float32)
        total = jnp.zeros((GROUP, HEAD), jnp.float32)
        for tap in range(TAPS):
            part = d_history[TAPS - 1 - tap : TAPS - 1 - tap + GROUP, lanes]
            total = total + taps_ref[tap : tap + 1, lanes] * part
            d_taps_ref[tap : tap + 1, lanes] += jnp.sum(pre * part, axis=0, keepdims=True)
        d_pre_ref[:, lanes] = total.astype(jnp.bfloat16)

        @pl.when(block == count - 1)
        def _(total=total, lanes=lanes):
            d_tail_ref[:, lanes] = total[GROUP - 8 :, :]

    @pl.when(block == 0)
    def _():
        edge_history[0:8, :] = jnp.zeros((8, edge_history.shape[1]), jnp.float32)
        edge_history[8:16, :] = d_history[0:8, :] * keep
        total = jnp.zeros(d_edge_ref.shape, jnp.float32)
        for tap in range(TAPS):
            part = edge_history[TAPS - 1 - tap : TAPS - 1 - tap + 8, :]
            total = total + taps_ref[tap : tap + 1, :] * part
            d_taps_ref[tap : tap + 1, :] += jnp.sum(edge_ref[...] * part, axis=0, keepdims=True)
        d_edge_ref[...] = total


def passed_along(value, axis, by):
    count = lax.axis_size(axis)
    pairs = [(i, i + by) for i in range(count) if 0 <= i + by < count]
    return lax.ppermute(value, axis, pairs)


def adamw(weight, first, second, grad, rate, decay):
    first = FIRST_DECAY * first + (1.0 - FIRST_DECAY) * grad
    second = SECOND_DECAY * second + (1.0 - SECOND_DECAY) * grad * grad
    stepped = (
        first
        / (1.0 - FIRST_DECAY**STEP)
        / (jnp.sqrt(second / (1.0 - SECOND_DECAY**STEP)) + ADAM_EPSILON)
    )
    return (weight - rate * (stepped + decay * weight), first, second)


def f32(*shape):
    return jax.ShapeDtypeStruct(shape, jnp.float32)


def bf16(*shape):
    return jax.ShapeDtypeStruct(shape, jnp.bfloat16)


class Rule:
    def __init__(self, keep, heads, row_count):
        self.keep, self.heads, self.rows = keep, heads, row_count
        self.count = row_count // GROUP
        self.params = pltpu.CompilerParams(
            dimension_semantics=("arbitrary",), vmem_limit_bytes=48 * 1024 * 1024
        )

    def rows_spec(self, width, back=False):
        last = self.count - 1
        if back:
            return pl.BlockSpec((GROUP, width), lambda n: (last - n, 0))
        return pl.BlockSpec((GROUP, width), lambda n: (n, 0))

    def block_spec(self, shape, back=False):
        last = self.count - 1
        if back:
            return pl.BlockSpec((None,) + shape, lambda n: (last - n, 0, 0, 0))
        return pl.BlockSpec((None,) + shape, lambda n: (n, 0, 0, 0))

    def whole(self, *shape):
        return pl.BlockSpec(shape, lambda n: (0,) * len(shape))

    def smem(self):
        return pl.BlockSpec(memory_space=pltpu.SMEM)

    def maps(self, pre, edge, logits, taps):
        heads, rows, count, inner = self.heads, self.rows, self.count, self.heads * HEAD
        return pl.pallas_call(
            functools.partial(maps_kernel, heads),
            grid=(count,),
            in_specs=[
                self.smem(),
                self.rows_spec(3 * inner),
                self.whole(8, 3 * inner),
                self.rows_spec(heads),
                self.whole(TAPS, 3 * inner),
            ],
            out_specs=[
                self.rows_spec(3 * inner),
                self.block_spec((heads, GROUP, 2 * HEAD)),
                self.block_spec((heads, GROUP, 2 * GROUP)),
                self.block_spec((heads, HEAD, HEAD)),
                self.block_spec((heads, HEAD, HEAD)),
                self.rows_spec(inner),
                self.rows_spec(inner),
                self.whole(heads, HEAD, 2 * HEAD),
            ],
            out_shape=[
                f32(rows, 3 * inner),
                f32(count, heads, GROUP, 2 * HEAD),
                f32(count, heads, GROUP, 2 * GROUP),
                f32(count, heads, HEAD, HEAD),
                f32(count, heads, HEAD, HEAD),
                f32(rows, inner),
                f32(rows, inner),
                f32(heads, HEAD, 2 * HEAD),
            ],
            scratch_shapes=[
                pltpu.VMEM((GROUP + 8, 3 * inner), jnp.float32),
                pltpu.VMEM((heads, HEAD, 2 * HEAD), jnp.float32),
            ],
            compiler_params=self.params,
            name="delta_maps",
        )(self.keep, pre, edge, logits, taps)

    def outputs(self, incoming, step, fresh, reach, zero_out, gain):
        heads, rows, count, inner = self.heads, self.rows, self.count, self.heads * HEAD
        return pl.pallas_call(
            functools.partial(outputs_kernel, heads),
            grid=(count,),
            in_specs=[
                self.smem(),
                self.whole(heads, HEAD, HEAD),
                self.block_spec((heads, HEAD, HEAD)),
                self.block_spec((heads, HEAD, HEAD)),
                self.rows_spec(inner),
                self.rows_spec(inner),
                self.whole(1, HEAD),
            ],
            out_specs=[
                self.block_spec((heads, HEAD, HEAD)),
                self.rows_spec(inner),
                self.rows_spec(inner),
            ],
            out_shape=[f32(count, heads, HEAD, HEAD), f32(rows, inner), bf16(rows, inner)],
            scratch_shapes=[pltpu.VMEM((heads, HEAD, HEAD), jnp.float32)],
            compiler_params=self.params,
            name="delta_outputs",
        )(self.keep, incoming, step, fresh, reach, zero_out, gain)

    def tail(self, d_normed, mixed, gain, step, reach):
        heads, rows, count, inner = self.heads, self.rows, self.count, self.heads * HEAD
        return pl.pallas_call(
            functools.partial(tail_kernel, heads),
            grid=(count,),
            in_specs=[
                self.smem(),
                self.rows_spec(inner, True),
                self.rows_spec(inner, True),
                self.whole(1, HEAD),
                self.block_spec((heads, HEAD, HEAD), True),
                self.rows_spec(inner, True),
            ],
            out_specs=[
                self.rows_spec(inner, True),
                self.whole(heads, HEAD, HEAD),
                self.whole(1, HEAD),
            ],
            out_shape=[f32(rows, inner), f32(heads, HEAD, HEAD), f32(1, HEAD)],
            scratch_shapes=[pltpu.VMEM((heads, HEAD, HEAD), jnp.float32)],
            compiler_params=self.params,
            name="delta_tail",
        )(self.keep, d_normed, mixed, gain, step, reach)

    def back(self, outgoing, pre, edge, logits, taps, conv, solved, square, step, reach, state, d_mixed):
        heads, rows, count, inner = self.heads, self.rows, self.count, self.heads * HEAD
        return pl.pallas_call(
            functools.partial(back_kernel, heads),
            grid=(count,),
            in_specs=[
                self.smem(),
                self.whole(heads, HEAD, HEAD),
                self.rows_spec(3 * inner, True),
                self.whole(8, 3 * inner),
                self.rows_spec(heads, True),
                self.whole(TAPS, 3 * inner),
                self.rows_spec(3 * inner, True),
                self.block_spec((heads, GROUP, 2 * HEAD), True),
                self.block_spec((heads, GROUP, 2 * GROUP), True),
                self.block_spec((heads, HEAD, HEAD), True),
                self.rows_spec(inner, True),
                self.block_spec((heads, HEAD, HEAD), True),
                self.rows_spec(inner, True),
            ],
            out_specs=[
                self.rows_spec(3 * inner, True),
                self.whole(8, 3 * inner),
                self.whole(8, 3 * inner),
                self.rows_spec(heads, True),
                self.whole(TAPS, 3 * inner),
            ],
            out_shape=[
                bf16(rows, 3 * inner),
                f32(8, 3 * inner),
                f32(8, 3 * inner),
                f32(rows, heads),
                f32(TAPS, 3 * inner),
            ],
            scratch_shapes=[
                pltpu.VMEM((GROUP + 8, 3 * inner), jnp.float32),
                pltpu.VMEM((16, 3 * inner), jnp.float32),
                pltpu.VMEM((heads, HEAD, HEAD), jnp.float32),
            ],
            compiler_params=self.params,
            name="delta_back",
        )(
            self.keep, outgoing, pre, edge, logits, taps, conv, solved, square, step, reach, state,
            d_mixed,
        )


def rms_unit(values):
    return values * lax.rsqrt(jnp.mean(values * values, axis=-1, keepdims=True) + EPSILON)


def rms_back(values, gain_vec, grad):
    inverse_rms = lax.rsqrt(jnp.mean(values * values, axis=-1, keepdims=True) + EPSILON)
    unit = values * inverse_rms
    d_unit = grad * gain_vec
    d_values = inverse_rms * (d_unit - unit * jnp.mean(d_unit * unit, axis=-1, keepdims=True))
    return d_values, jnp.sum(grad * unit, axis=0)


def low(values):
    return values.astype(jnp.bfloat16)


def product(left, right, dims=((1,), (0,))):
    return lax.dot_general(left, right, (dims, ((), ())), preferred_element_type=jnp.float32)


def rows_summed(partial):
    return lax.psum_scatter(low(partial), "shard", scatter_dimension=0, tiled=True)


def rows_joined(rows):
    return lax.all_gather(rows, "shard", axis=0, tiled=True)


def per_device(
    hidden_in,
    out_grad,
    deal,
    lengths,
    qkv_weight,
    qkv_first,
    qkv_second,
    beta_weight,
    beta_first,
    beta_second,
    out_weight,
    out_first,
    out_second,
    gate_up_weight,
    gate_up_first,
    gate_up_second,
    down_weight,
    down_first,
    down_second,
    conv_weight,
    conv_first,
    conv_second,
    gains,
    gains_first,
    gains_second,
):
    row_count, model_width = hidden_in.shape
    heads = beta_weight.shape[1]
    inner = qkv_weight.shape[2]
    units = down_weight.shape[0]
    longest = {4: 4096, 16: 8192}[lengths.shape[0]]
    hops = min(lax.axis_size("seq") - 1, -(-longest // row_count))
    target = deal // row_count
    order = jnp.argsort(target, stable=True)
    got_x, got_dy, got_place = (
        lax.all_to_all(hidden_in[order], "seq", split_axis=0, concat_axis=0, tiled=True),
        lax.all_to_all(out_grad[order], "seq", split_axis=0, concat_axis=0, tiled=True),
        lax.all_to_all(deal[order] % row_count, "seq", split_axis=0, concat_axis=0, tiled=True),
    )
    arranged = jnp.argsort(got_place)
    chain_x = got_x[arranged].astype(jnp.float32)
    chain_dy = got_dy[arranged]
    first_place = lax.axis_index("seq") * row_count
    places = first_place + jnp.arange(0, row_count, GROUP, dtype=jnp.int32)
    starts = jnp.cumsum(lengths) - lengths
    keep = jnp.all(starts[None, :] != places[:, None], axis=1).astype(jnp.float32)
    quarter = row_count // lax.axis_size("shard")
    first_row = lax.axis_index("shard") * quarter

    def own_rows(values):
        return lax.dynamic_slice_in_dim(values, first_row, quarter, 0)

    qkv_mat = lax.all_gather(low(qkv_weight).reshape(-1, 3 * inner), "seq", axis=0, tiled=True)
    beta_mat = lax.all_gather(low(beta_weight), "seq", axis=0, tiled=True)
    gate_up_mat = lax.all_gather(
        low(gate_up_weight).reshape(-1, 2 * units), "seq", axis=0, tiled=True
    )
    out_mat = lax.all_gather(low(out_weight), "seq", axis=1, tiled=True)
    down_mat = lax.all_gather(low(down_weight), "seq", axis=1, tiled=True)
    gain_in = gains[:model_width]
    gain_ff = gains[model_width : 2 * model_width]
    gain_out = gains[2 * model_width :].reshape(1, HEAD)
    conv_mat = conv_weight.reshape(TAPS, 3 * inner)

    normed_in = low(rms_unit(chain_x) * gain_in)
    projected = low(product(normed_in, qkv_mat))
    logits = product(normed_in, beta_mat)
    edge_rows = passed_along(projected[row_count - 8 :], "seq", 1).astype(jnp.float32)
    edge_rows = edge_rows * (jnp.arange(8) >= 8 - (TAPS - 1)).astype(jnp.float32)[:, None]
    rule = Rule(keep, heads, row_count)
    conv, solved, square, step, fresh, reach, zero_out, total = rule.maps(
        projected, edge_rows, logits, conv_mat
    )
    whole_step, whole_fresh = total[:, :, :HEAD], total[:, :, HEAD:]
    incoming = jnp.zeros((heads, HEAD, HEAD), jnp.float32)
    for hop in range(hops):
        advanced = whole_fresh
        if hop:
            advanced = advanced + jnp.einsum(
                "hde,hef->hdf", whole_step, incoming, precision=PRECISE
            )
        incoming = passed_along(advanced, "seq", 1)
    state, mixed, normed = rule.outputs(incoming, step, fresh, reach, zero_out, gain_out)

    residual = own_rows(chain_x) + rows_summed(product(normed, out_mat)).astype(jnp.float32)
    normed_ff = rows_joined(low(rms_unit(residual) * gain_ff))
    gate_up_out = product(normed_ff, gate_up_mat)
    gate, up = gate_up_out[:, :units], gate_up_out[:, units:]
    opened = jax.nn.sigmoid(gate)
    hidden_units = low(gate * opened * up)
    result = residual + rows_summed(product(hidden_units, down_mat)).astype(jnp.float32)
    result = rows_joined(low(result))

    d_hidden = product(chain_dy, down_mat, ((1,), (1,)))
    d_gate = low(d_hidden * up * (opened * (1.0 + gate * (1.0 - opened))))
    d_up = low(d_hidden * (gate * opened))
    d_gate_up = jnp.concatenate([d_gate, d_up], axis=1)
    d_normed_ff = rows_summed(product(d_gate_up, gate_up_mat, ((1,), (1,)))).astype(jnp.float32)
    d_residual, grad_gain_ff = rms_back(residual, gain_ff, d_normed_ff)
    d_residual = own_rows(chain_dy).astype(jnp.float32) + d_residual
    d_mix = rows_joined(low(d_residual))
    grad_down = product(hidden_units, chain_dy, ((0,), (0,)))
    grad_gate_up = product(normed_ff, d_gate_up, ((0,), (0,)))
    grad_out = product(normed, d_mix, ((0,), (0,)))
    d_normed = product(d_mix, out_mat, ((1,), (1,)))
    d_mixed, d_first_state, grad_gain_out = rule.tail(d_normed, mixed, gain_out, step, reach)
    flipped = jnp.swapaxes(whole_step, 1, 2)
    outgoing = jnp.zeros((heads, HEAD, HEAD), jnp.float32)
    for hop in range(hops):
        advanced = d_first_state
        if hop:
            advanced = advanced + jnp.einsum("hde,hef->hdf", flipped, outgoing, precision=PRECISE)
        outgoing = passed_along(advanced, "seq", -1)
    d_pre, d_tail, d_edge, d_logits, grad_taps = rule.back(
        outgoing, projected, edge_rows, logits, conv_mat, conv, solved, square, step, reach, state,
        d_mixed,
    )
    d_tail = low(d_tail + passed_along(d_edge, "seq", -1))
    d_pre = lax.dynamic_update_slice(d_pre, d_tail, (row_count - 8, 0))
    d_logits = low(d_logits)
    grad_qkv = product(normed_in, d_pre, ((0,), (0,)))
    grad_beta = product(normed_in, d_logits, ((0,), (0,)))
    d_normed_in = rows_summed(
        product(d_pre, qkv_mat, ((1,), (1,))) + product(d_logits, beta_mat, ((1,), (1,)))
    ).astype(jnp.float32)
    d_input, grad_gain_in = rms_back(own_rows(chain_x), gain_in, d_normed_in)
    d_input = rows_joined(low(d_residual + d_input))

    def seq_summed(grad, dim):
        return lax.psum_scatter(low(grad), "seq", scatter_dimension=dim, tiled=True).astype(
            jnp.float32
        )

    red_qkv = seq_summed(grad_qkv, 0).reshape(qkv_weight.shape)
    red_beta = lax.psum_scatter(grad_beta, "seq", scatter_dimension=0, tiled=True)
    red_gate_up = seq_summed(grad_gate_up, 0).reshape(gate_up_weight.shape)
    red_out = seq_summed(grad_out, 1)
    red_down = seq_summed(grad_down, 1)
    grad_gains = jnp.concatenate([grad_gain_in, grad_gain_ff, grad_gain_out.reshape(HEAD)])
    red_gains = lax.psum(grad_gains, ("seq", "shard"))
    red_conv = lax.psum(grad_taps.reshape(conv_weight.shape), "seq")
    qkv_new = adamw(qkv_weight, qkv_first, qkv_second, red_qkv, RATE_WIDE, SHRINK)
    beta_new = adamw(beta_weight, beta_first, beta_second, red_beta, RATE_WIDE, SHRINK)
    out_new = adamw(out_weight, out_first, out_second, red_out, RATE_WIDE, SHRINK)
    gate_up_new = adamw(
        gate_up_weight, gate_up_first, gate_up_second, red_gate_up, RATE_WIDE, SHRINK
    )
    down_new = adamw(down_weight, down_first, down_second, red_down, RATE_DOWN, SHRINK)
    conv_new = adamw(conv_weight, conv_first, conv_second, red_conv, RATE_CONV, 0.0)
    gains_new = adamw(gains, gains_first, gains_second, red_gains, RATE_GAIN, 0.0)
    back_out, back_grad = (
        lax.all_to_all(result[got_place], "seq", split_axis=0, concat_axis=0, tiled=True),
        lax.all_to_all(d_input[got_place], "seq", split_axis=0, concat_axis=0, tiled=True),
    )
    restore = jnp.argsort(order)
    return (
        back_out[restore],
        back_grad[restore],
        *qkv_new,
        *beta_new,
        *out_new,
        *gate_up_new,
        *down_new,
        *conv_new,
        *gains_new,
    )


def solution(mesh):
    return jax.shard_map(
        per_device,
        mesh=mesh,
        in_specs=(
            P("seq", None),
            P("seq", None),
            P("seq"),
            P(),
            P("seq", None, "shard"),
            P("seq", None, "shard"),
            P("seq", None, "shard"),
            P("seq", "shard"),
            P("seq", "shard"),
            P("seq", "shard"),
            P("shard", "seq"),
            P("shard", "seq"),
            P("shard", "seq"),
            P("seq", None, "shard"),
            P("seq", None, "shard"),
            P("seq", None, "shard"),
            P("shard", "seq"),
            P("shard", "seq"),
            P("shard", "seq"),
            P(None, None, "shard"),
            P(None, None, "shard"),
            P(None, None, "shard"),
            P(),
            P(),
            P(),
        ),
        out_specs=(
            P("seq", None),
            P("seq", None),
            P("seq", None, "shard"),
            P("seq", None, "shard"),
            P("seq", None, "shard"),
            P("seq", "shard"),
            P("seq", "shard"),
            P("seq", "shard"),
            P("shard", "seq"),
            P("shard", "seq"),
            P("shard", "seq"),
            P("seq", None, "shard"),
            P("seq", None, "shard"),
            P("seq", None, "shard"),
            P("shard", "seq"),
            P("shard", "seq"),
            P("shard", "seq"),
            P(None, None, "shard"),
            P(None, None, "shard"),
            P(None, None, "shard"),
            P(),
            P(),
            P(),
        ),
        check_vma=False,
    )
```

time: 4260 us -> 1730 us (0.41)
  matrix products: 989 us -> 152 us
  other arithmetic: 891 us -> 74.1 us
  waiting for transfers between devices: 1610 us -> 841 us
  local copies, waits for them, and re-layouts: 482 us -> 132 us
  Pallas kernels: 0 us -> 245 us
  blocking collectives: 161 us -> 210 us
    psum x3 -> x0, waiting for transfers between devices: 956 us -> none  [shard_total(): return lax.psum(values, 'shard')]
    dot_general x483 -> x20, matrix products: 939 us -> 147 us  [the longest x14 144 us: product(): lax.dot_general(left, right, (dims, ((), ())), preferred_element_type=jnp...]
    another operation x157 -> x1, other arithmetic: 649 us -> 0.18 us  [the longest x144 648 us: group_step(): jax.scipy.linalg.solve_triangular(system, right_side, lower=True, unit_di...]
    reduce_scatter x3 -> x8, waiting for transfers between devices: 196 us -> 506 us  [the longest x4 300 us: rows_summed(): lax.psum_scatter(low(partial), 'shard', scatter_dimension=0, tiled=True)]
    unnamed x14 -> x18, waiting for transfers between devices: 293 us -> 12.2 us
    pallas_call x0 -> x4, Pallas kernels: none -> 245 us  [the longest x1 132 us: maps(): pl.pallas_call(functools.partial(maps_kernel, heads), grid=(count,), in_s...]
    all_gather x4 -> x8, waiting for transfers between devices: 79 us -> 293 us  [the longest x4 266 us: rows_joined(): return lax.all_gather(rows, 'shard', axis=0, tiled=True)]
    dynamic_slice x144 -> x0, local copies, waits for them, and re-layouts: 128 us -> none  [local_rule(): lax.scan(group_step, (zero_state, identity), (to_groups(queries), to_grou...]
  transfers between devices with their start and end apart: 32 -> 31, of which waited for: 24 -> 23; matrix products, arithmetic and copies ran while one was open for 26% -> 15% of each run, Pallas kernels for 0% -> 8%
where the time goes in v1:
time: 1730 us; the launch traced here: 1720 us
  waiting for transfers between devices  841 us (49%)
  Pallas kernels  245 us (14%)
  blocking collectives  210 us (12%)
  matrix products  152 us (9%)
  local copies, waits for them, and re-layouts  132 us (8%)
  other arithmetic  74.1 us (4%)
  starting transfers between devices  52.2 us (3%)
    reduce_scatter x4, waiting for transfers between devices, rows_summed(): lax.psum_scatter(low(partial), 'shard', scatter_dimension=0, tiled=True)  300 us
    all_gather x4, waiting for transfers between devices, rows_joined(): return lax.all_gather(rows, 'shard', axis=0, tiled=True)  266 us
    reduce_scatter x4, waiting for transfers between devices, seq_summed(): lax.psum_scatter(low(grad), 'seq', scatter_dimension=dim, tiled=True)  206 us
    dot_general x14, matrix products, product(): lax.dot_general(left, right, (dims, ((), ())), preferred_element_type=jnp...  144 us
    pallas_call x1, Pallas kernels, maps(): pl.pallas_call(functools.partial(maps_kernel, heads), grid=(count,), in_s...  132 us
    pallas_call x1, Pallas kernels, back(): pl.pallas_call(functools.partial(back_kernel, heads), grid=(count,), in_s...  84.3 us
    all_to_all x1, blocking collectives, per_device(): lax.all_to_all(out_grad[order], 'seq', split_axis=0, concat_axis=0, tiled...  82.7 us
    all_gather x1, blocking collectives, per_device(): beta_mat = lax.all_gather(low(beta_weight), 'seq', axis=0, tiled=True)  63.4 us
  transfers between devices with their start and end apart: 31, of which 23 were waited for; matrix products, arithmetic and copies ran while one was open for 15% of the time, Pallas kernels for 8%

profile of v1, /device:TPU:0, one launch (start us, length us, event | category | flops | bytes accessed | tf_op | source)
XLA Modules:
  0.0 1721.0 jit_solution(6086053795331943421)
XLA Ops:
  10.2 4.4 sort.48
  14.6 4.5 gather_fusion.1
  19.8 5.2 all-to-all-start.1
  24.9 11.5 gather_fusion
  36.5 4.7 all-to-all-start
  42.5 63.4 %all_gather.28 = bf16[2048,4]{0,1:T(4,128)(2,1)S(1)} all-gather(bf16[256,4]{0,1:T(4,128)(2,1)S(1)} %convert_element_type.118), channel_id=1, replica_groups=mesh['seq'=8,'shard'=4] {'seq'}, dimensions={0}, use_global_device_ids=true | all-gather | bytes 18432 | tf_op jit(solution)/shard_map/all_gather | solution.py:617
  105.9 4.4 sort.49
  110.3 11.5 gather_fusion.2
  125.0 10.3 convolution_convert_fusion.4.pre_ref
  139.6 132.2 %delta_maps.1 = (f32[1024,1536]{1,0:T(8,128)}, f32[16,4,64,256]{3,2,1,0:T(8,128)}, f32[16,4,64,128]{3,2,1,0:T(8,128)S(1)}, f32[16,4,128,128]{3,2,1,0:T(8,128)}, ...) custom-call(f32[16]{0:T(128)S(1)} %convert_element_type.112.keep_ref, ...), custom_call_target="tpu_custom_call" | custom-call | tf_op jit(solution)/shard_map/delta_maps/pallas_call | solution.py:401
  277.6 5.5 collective-permute-start.2
  284.6 6.6 collective-permute-start.3
  292.7 6.6 collective-permute-start.4
  300.4 13.7 delta_outputs.1
  316.4 6.2 convolution_convert_fusion.6
  326.8 6.6 convert_element_type.111
  333.4 76.1 %reduce-scatter.12.cloned.1.call-done = bf16[256,2048]{1,0:T(8,128)(2,1)} async-done(((bf16[1024,2048]{1,0:T(8,128)(2,1)}), bf16[256,2048]{1,0:T(8,128)(2,1)}) %reduce-scatter.12.cloned.1.call-update) | async-done | bytes 1048592 | tf_op jit(solution)/shard_map/reduce_scatter | solution.py:556
  415.6 11.5 gather_fusion.5
  427.1 82.7 %all_to_all.60 = bf16[8,128,2048]{2,1,0:T(8,128)(2,1)} all-to-all(bf16[8,128,2048]{2,1,0:T(8,128)(2,1)} %bitcast.66), channel_id=1, replica_groups=mesh['seq'=8,'shard'=4] {'seq'}, dimensions={0} | all-to-all | bytes 8388608 | tf_op jit(solution)/shard_map/all_to_all | solution.py:600
  509.8 11.5 gather_fusion.6
  521.3 79.0 %all-gather.13.cloned.1.call-done = bf16[1024,2048]{1,0:T(8,128)(2,1)} async-done(((bf16[256,2048]{1,0:T(8,128)(2,1)}), bf16[1024,2048]{1,0:T(8,128)(2,1)}) %all-gather.13.cloned.1.call-update) | async-done | bytes 4194320 | tf_op jit(solution)/shard_map/all_gather | solution.py:560
  600.4 18.7 %fusion.54 = f32[1024,2816]{1,0:T(8,128)} fusion(bf16[1024,2048]{1,0:T(8,128)(2,1)} %all-gather.13.cloned.1.call-done, bf16[2048,2816]{1,0:T(8,128)(2,1)} %all-gather.15.cloned.1.call-done), kind=kOutput, calls=%fused_computation.132 | convolution fusion | flops 11811160064 | bytes 27262976 | tf_op jit(solution)/shard_map/dot_general | solution.py:552
  619.1 26.6 %all-gather.17.cloned.1.call-done = bf16[1408,2048]{1,0:T(8,128)(2,1)} async-done(((bf16[1408,256]{1,0:T(8,128)(2,1)}), bf16[1408,2048]{1,0:T(8,128)(2,1)}) %all-gather.17.cloned.1.call-update) | async-done | bytes 5767184 | tf_op jit(solution)/shard_map/all_gather | solution.py:622
  645.8 16.1 multiply_convert_fusion.2
  664.4 16.3 convolution_convert_fusion.3
  681.0 76.7 %reduce-scatter.16.cloned.1.call-done = bf16[256,2048]{1,0:T(8,128)(2,1)} async-done(((bf16[1024,2048]{1,0:T(8,128)(2,1)}), bf16[256,2048]{1,0:T(8,128)(2,1)}) %reduce-scatter.16.cloned.1.call-update) | async-done | bytes 1048592 | tf_op jit(solution)/shard_map/reduce_scatter | solution.py:556
  762.8 81.4 %all-gather.21.cloned.1.call-done = bf16[1024,2048]{1,0:T(8,128)(2,1)} async-done(((bf16[256,2048]{1,0:T(8,128)(2,1)}), bf16[1024,2048]{1,0:T(8,128)(2,1)}) %all-gather.21.cloned.1.call-update) | async-done | bytes 4194320 | tf_op jit(solution)/shard_map/all_gather | solution.py:560
  844.2 5.2 fusion.55.d_normed_ref
  849.4 14.5 delta_tail.1
  870.8 5.8 collective-permute-done.6
  878.5 6.4 collective-permute-done.7
  886.8 6.4 collective-permute-done.8.outgoing_ref
  893.2 84.3 %delta_back.1 = (bf16[1024,1536]{1,0:T(8,128)(2,1)}, f32[8,1536]{1,0:T(8,128)S(1)}, f32[8,1536]{1,0:T(8,128)S(1)}, f32[1024,4]{1,0:T(8,128)S(1)}, f32[4,1536]{1,0:T(4,128)S(1)}) custom-call(f32[16]{0:T(128)S(1)} %convert_element_type.112.keep_ref, f32[4,128,128]{2,1,0:T(8,128)S(1)} %collective-permute-done.8.outgoing_ref, bf16[1024,1536]{1,0:T(8,128)(2,1)} %copy-done.13, ...), custom_call_target="tpu_custom_call" | custom-call | tf_op jit(solution)/shard_map/delta_back/pallas_call | solution.py:490
  980.4 4.5 collective-permute-done.9
  986.5 11.3 add_convert_fusion
  997.9 10.9 convolution_convert_fusion.5
  1008.9 70.4 %reduce-scatter.18.cloned.1.call-done = bf16[256,2048]{1,0:T(8,128)(2,1)} async-done(((bf16[1024,2048]{1,0:T(8,128)(2,1)}), bf16[256,2048]{1,0:T(8,128)(2,1)}) %reduce-scatter.18.cloned.1.call-update) | async-done | bytes 1048592 | tf_op jit(solution)/shard_map/reduce_scatter | solution.py:556
  1082.0 76.8 %reduce-scatter.14.cloned.1.call-done = bf16[256,2048]{1,0:T(8,128)(2,1)} async-done(((bf16[1024,2048]{1,0:T(8,128)(2,1)}), bf16[256,2048]{1,0:T(8,128)(2,1)}) %reduce-scatter.14.cloned.1.call-update) | async-done | bytes 1048592 | tf_op jit(solution)/shard_map/reduce_scatter | solution.py:556
  1158.9 5.4 fusion.9
  1164.3 10.5 convolution_convert_fusion.1
  1175.6 4.8 fusion.26
  1180.4 18.3 %convolution_convert_fusion = bf16[2048,2816]{1,0:T(8,128)(2,1)} fusion(bf16[1024,2048]{1,0:T(8,128)(2,1)} %all-gather.13.cloned.1.call-done, bf16[1024,1408]{1,0:T(8,128)(2,1)} %copy-done.44, bf16[1024,1408]{1,0:T(8,128)(2,1)} %copy-done.43), kind=kOutput, calls=%fused_computation.9 | convolution fusion | flops 11828461568 | bytes 21495808 | tf_op jit(solution)/shard_map/dot_general | solution.py:552
  1199.9 5.9 convolution_convert_fusion.7
  1206.1 11.6 convolution_convert_fusion.2
  1218.4 27.3 %all-gather.23.cloned.1.call-done = bf16[1024,2048]{1,0:T(8,128)(2,1)} async-done(((bf16[256,2048]{1,0:T(8,128)(2,1)}), bf16[1024,2048]{1,0:T(8,128)(2,1)}) %all-gather.23.cloned.1.call-update) | async-done | bytes 4194320 | tf_op jit(solution)/shard_map/all_gather | solution.py:560
  1245.7 11.5 gather_fusion.7
  1257.3 4.6 all-to-all-start.4
  1268.2 4.4 sort.50
  1272.6 62.7 %reduce-scatter.26.cloned.1.call-done = bf16[1408,256]{1,0:T(8,128)(2,1)} async-done(((bf16[1408,2048]{1,0:T(8,128)(2,1)}), bf16[1408,256]{1,0:T(8,128)(2,1)}) %reduce-scatter.26.cloned.1.call-update) | async-done | bytes 720912 | tf_op jit(solution)/shard_map/reduce_scatter | solution.py:693
  1335.3 4.4 multiply_subtract_fusion.2
  1339.8 22.5 %psum.14 = f32[4,3,512]{2,0,1:T(4,128)S(1)} all-reduce(f32[4,3,512]{2,0,1:T(4,128)S(1)} %bitcast.60), channel_id=1, replica_groups=mesh['seq'=8,'shard'=4] {'seq'}, use_global_device_ids=true, to_apply=%region_19.20 | all-reduce | flops 6144 | bytes 49152 | tf_op jit(solution)/shard_map/psum | solution.py:704
  1362.9 11.4 reduce-scatter.28.cloned.1.call-done
  1375.9 88.9 %reduce-scatter.24.cloned.1.call-done = bf16[256,2816]{1,0:T(8,128)(2,1)} async-done(((bf16[2048,2816]{1,0:T(8,128)(2,1)}), bf16[256,2816]{1,0:T(8,128)(2,1)}) %reduce-scatter.24.cloned.1.call-update) | async-done | bytes 1441808 | tf_op jit(solution)/shard_map/reduce_scatter | solution.py:693
  1464.9 4.3 reshape.252
  1469.2 78.5 %all-gather.19.cloned.1.call-done = bf16[1024,2048]{1,0:T(8,128)(2,1)} async-done(((bf16[256,2048]{1,0:T(8,128)(2,1)}), bf16[1024,2048]{1,0:T(8,128)(2,1)}) %all-gather.19.cloned.1.call-update) | async-done | bytes 4194320 | tf_op jit(solution)/shard_map/all_gather | solution.py:560
  1547.7 11.5 gather_fusion.3
  1559.3 5.1 all-to-all-start.2
  1564.4 12.6 multiply_subtract_fusion
  1577.0 32.9 %reduce-scatter.22.cloned.1.call-done = bf16[512,256]{1,0:T(8,128)(2,1)} async-done(((bf16[512,2048]{1,0:T(8,128)(2,1)}), bf16[512,256]{1,0:T(8,128)(2,1)}) %reduce-scatter.22.cloned.1.call-update) | async-done | bytes 262160 | tf_op jit(solution)/shard_map/reduce_scatter | solution.py:693
  1612.8 41.8 %psum.15 = f32[4224]{0:T(1024)S(1)} all-reduce(f32[4224]{0:T(1024)S(1)} %pad_maximum_fusion.3), channel_id=1, replica_groups=mesh['seq'=8,'shard'=4] {'seq','shard'}, use_global_device_ids=true, to_apply=%region_22.23 | all-reduce | flops 4224 | bytes 33792 | tf_op jit(solution)/shard_map/psum | solution.py:703
  1655.3 21.8 %reduce-scatter.20.cloned.1.call-done = bf16[256,1536]{1,0:T(8,128)(2,1)} async-done(((bf16[2048,1536]{1,0:T(8,128)(2,1)}), bf16[256,1536]{1,0:T(8,128)(2,1)}) %reduce-scatter.20.cloned.1.call-update) | async-done | bytes 786448 | tf_op jit(solution)/shard_map/reduce_scatter | solution.py:693
  1679.7 4.9 multiply_subtract_fusion.1
  1690.9 11.5 gather_fusion.8
  1702.5 11.5 gather_fusion.4
  (204 shorter events, 84.5 us)
Async XLA Ops:
  7.2 117.7 %all-gather.9.cloned.1.call-start = ((), (), s32[]{:S(2)}) async-start(), calls=%async_computation.14 | async-start | bytes 7077888 | tf_op jit(solution)/shard_map/all_gather | solution.py:616
  9.1 10.0 copy-start.11
  14.6 21.9 %copy-start.34 = (s32[1024]{0:T(1024)}, s32[1024]{0:T(1024)S(1)}, u32[]{:S(2)}) copy-start(s32[1024]{0:T(1024)S(1)} %get-tuple-element.45) | copy-start | bytes 12292
  19.8 16.7 all-to-all-start.1
  36.5 69.4 %copy-start.26 = (s32[8,128,1]{1,2,0:T(1,128)}, s32[8,128,1]{1,2,0:T(1,128)S(1)}, u32[]{:S(2)}) copy-start(s32[8,128,1]{1,2,0:T(1,128)S(1)} %all-to-all-done.1) | copy-start | bytes 12292
  36.5 4.8 copy-start.20
  36.5 5.6 copy-start.32
  36.5 5.6 copy-start.42
  36.5 69.3 %copy-start.24 = (f32[4224]{0:T(1024)S(1)}, f32[4224]{0:T(1024)}, u32[]{:S(2)}) copy-start(f32[4224]{0:T(1024)} %param.47) | copy-start | bytes 50692
  36.5 73.7 %all-to-all-start = ((bf16[8,128,2048]{2,1,0:T(8,128)(2,1)}), bf16[8,128,2048]{2,1,0:T(8,128)(2,1)}, u32[]{:S(2)}, u32[]{:S(2)}) async-start(bf16[8,128,2048]{2,1,0:T(8,128)(2,1)} %bitcast.64), calls=%async_computation | async-start | bytes 8388608 | tf_op jit(solution)/shard_map/all_to_all | solution.py:599
  41.3 275.1 %all-gather.11.cloned.1.call-start = ((), (), s32[]{:S(2)}) async-start(), calls=%async_computation.15 | async-start | bytes 2359296 | tf_op jit(solution)/shard_map/all_gather | solution.py:621
  42.1 367.4 %reduce-scatter.12.cloned.1.call-start = ((), (), s32[]{:S(2)}) async-start(), calls=%async_computation.16 | async-start | bytes 5242880 | tf_op jit(solution)/shard_map/reduce_scatter | solution.py:556
  105.9 32.2 %copy-start.22 = (f32[2048]{0:T(1024)}, f32[2048]{0:T(1024)S(1)}, u32[]{:S(2)}) copy-start(f32[2048]{0:T(1024)S(1)} %get-tuple-element.170) | copy-start | bytes 24580
  124.9 13.2 copy-start.38
  124.9 13.2 copy-start.10
  135.2 4.2 copy-start.13
  135.2 4.3 copy-start.6
  135.3 4.2 collective-permute-start
  273.1 41.0 %copy-start = (f32[1024,512]{1,0:T(8,128)}, f32[1024,512]{1,0:T(8,128)S(1)}, u32[]{:S(2)}) copy-start(f32[1024,512]{1,0:T(8,128)S(1)} %get-tuple-element.50.reach_ref) | copy-start | bytes 6291460
  273.1 4.1 collective-permute-start.1
  277.6 6.6 collective-permute-start.2
  284.6 7.7 collective-permute-start.3
  292.7 7.7 collective-permute-start.4
  322.6 198.7 %all-gather.15.cloned.1.call-start = ((), (), s32[]{:S(2)}) async-start(), calls=%async_computation.18 | async-start | bytes 12976128 | tf_op jit(solution)/shard_map/all_gather | solution.py:618
  326.7 273.6 %all-gather.13.cloned.1.call-start = ((), (), s32[]{:S(2)}) async-start(), calls=%async_computation.17 | async-start | bytes 5242880 | tf_op jit(solution)/shard_map/all_gather | solution.py:560
  413.2 232.6 %all-gather.17.cloned.1.call-start = ((), (), s32[]{:S(2)}) async-start(), calls=%async_computation.19 | async-start | bytes 6488064 | tf_op jit(solution)/shard_map/all_gather | solution.py:622
  415.5 342.1 %reduce-scatter.16.cloned.1.call-start = ((), (), s32[]{:S(2)}) async-start(), calls=%async_computation.22 | async-start | bytes 5242880 | tf_op jit(solution)/shard_map/reduce_scatter | solution.py:556
  680.7 163.4 %all-gather.21.cloned.1.call-start = ((), (), s32[]{:S(2)}) async-start(), calls=%async_computation.23 | async-start | bytes 5242880 | tf_op jit(solution)/shard_map/all_gather | solution.py:560
  762.7 316.6 %reduce-scatter.18.cloned.1.call-start = ((), (), s32[]{:S(2)}) async-start(), calls=%async_computation.24 | async-start | bytes 5242880 | tf_op jit(solution)/shard_map/reduce_scatter | solution.py:556
  849.4 43.8 %copy-start.3 = (f32[16,4,64,128]{3,2,1,0:T(8,128)S(1)}, f32[16,4,64,128]{3,2,1,0:T(8,128)}, u32[]{:S(2)}) copy-start(f32[16,4,64,128]{3,2,1,0:T(8,128)} %copy-done.2) | copy-start | bytes 6291460
  865.3 27.9 %copy-start.1 = (f32[1024,512]{1,0:T(8,128)S(1)}, f32[1024,512]{1,0:T(8,128)}, u32[]{:S(2)}) copy-start(f32[1024,512]{1,0:T(8,128)} %copy-done) | copy-start | bytes 6291460
  865.3 3.5 collective-permute-start.5
  869.5 7.1 collective-permute-start.6
  877.2 7.7 collective-permute-start.7
  885.5 7.7 collective-permute-start.8
  977.5 7.4 collective-permute-start.9
  979.2 5.7 copy-start.40
  997.8 161.1 %reduce-scatter.14.cloned.1.call-start = ((), (), s32[]{:S(2)}) async-start(), calls=%async_computation.20 | async-start | bytes 5242880 | tf_op jit(solution)/shard_map/reduce_scatter | solution.py:556
  1008.8 70.5 %copy-start.23 = (f32[2048]{0:T(1024)S(1)}, f32[2048]{0:T(1024)}, u32[]{:S(2)}) copy-start(f32[2048]{0:T(1024)} %copy-done.22) | copy-start | bytes 24580
  1008.8 236.9 %all-gather.23.cloned.1.call-start = ((), (), s32[]{:S(2)}) async-start(), calls=%async_computation.25 | async-start | bytes 5242880 | tf_op jit(solution)/shard_map/all_gather | solution.py:560
  1164.3 171.0 %reduce-scatter.26.cloned.1.call-start = ((), (), s32[]{:S(2)}) async-start(), calls=%async_computation.29 | async-start | bytes 6488064 | tf_op jit(solution)/shard_map/reduce_scatter | solution.py:693
  1174.9 199.4 %reduce-scatter.28.cloned.1.call-start = ((), (), s32[]{:S(2)}) async-start(), calls=%async_computation.30 | async-start | bytes 1179648
  1180.4 284.5 %reduce-scatter.24.cloned.1.call-start = ((), (), s32[]{:S(2)}) async-start(), calls=%async_computation.28 | async-start | bytes 12976128 | tf_op jit(solution)/shard_map/reduce_scatter | solution.py:693
  1198.7 349.0 %all-gather.19.cloned.1.call-start = ((), (), s32[]{:S(2)}) async-start(), calls=%async_computation.21 | async-start | bytes 5242880 | tf_op jit(solution)/shard_map/all_gather | solution.py:560
  1199.3 410.6 %reduce-scatter.22.cloned.1.call-start = ((), (), s32[]{:S(2)}) async-start(), calls=%async_computation.27 | async-start | bytes 2359296 | tf_op jit(solution)/shard_map/reduce_scatter | solution.py:693
  1205.8 471.3 %reduce-scatter.20.cloned.1.call-start = ((), (), s32[]{:S(2)}) async-start(), calls=%async_computation.26 | async-start | bytes 7077888 | tf_op jit(solution)/shard_map/reduce_scatter | solution.py:693
  1257.3 302.0 %all-to-all-start.4 = ((bf16[8,128,2048]{2,1,0:T(8,128)(2,1)}), bf16[8,128,2048]{2,1,0:T(8,128)(2,1)}, u32[]{:S(2)}, u32[]{:S(2)}) async-start(bf16[8,128,2048]{2,1,0:T(8,128)(2,1)} %bitcast.65), calls=%async_computation.8 | async-start | bytes 8388608 | tf_op jit(solution)/shard_map/all_to_all | solution.py:716
  1261.9 6.3 copy-start.35
  1261.9 73.4 %copy-start.19 = (f32[1408,256]{1,0:T(8,128)S(1)}, f32[1408,256]{1,0:T(8,128)}, u32[]{:S(2)}) copy-start(f32[1408,256]{1,0:T(8,128)} %param.41) | copy-start | bytes 4325380
  1261.9 73.4 %copy-start.21 = (f32[1408,256]{1,0:T(8,128)S(1)}, f32[1408,256]{1,0:T(8,128)}, u32[]{:S(2)}) copy-start(f32[1408,256]{1,0:T(8,128)} %param.42) | copy-start | bytes 4325380
  1272.6 89.7 %copy-start.28 = (f32[4,3,512]{2,0,1:T(4,128)S(1)}, f32[4,3,512]{2,0,1:T(4,128)}, u32[]{:S(2)}) copy-start(f32[4,3,512]{2,0,1:T(4,128)} %param.45) | copy-start | bytes 73732
  1272.6 89.7 %copy-start.29 = (f32[4,3,512]{2,0,1:T(4,128)S(1)}, f32[4,3,512]{2,0,1:T(4,128)}, u32[]{:S(2)}) copy-start(f32[4,3,512]{2,0,1:T(4,128)} %param.46) | copy-start | bytes 73732
  1272.6 102.7 %copy-start.33 = (f32[256,4]{0,1:T(4,128)S(1)}, f32[256,4]{0,1:T(4,128)}, u32[]{:S(2)}) copy-start(f32[256,4]{0,1:T(4,128)} %param.32) | copy-start | bytes 12292
  1272.6 102.7 %copy-start.36 = (f32[256,4]{0,1:T(4,128)S(1)}, f32[256,4]{0,1:T(4,128)}, u32[]{:S(2)}) copy-start(f32[256,4]{0,1:T(4,128)} %param.33) | copy-start | bytes 12292
  1272.6 102.7 %copy-start.37 = (f32[256,4]{0,1:T(4,128)S(1)}, f32[256,4]{0,1:T(4,128)}, u32[]{:S(2)}) copy-start(f32[256,4]{0,1:T(4,128)} %param.34) | copy-start | bytes 12292
  1559.3 5.1 copy-start.14
  1559.3 143.2 %all-to-all-start.2 = ((bf16[8,128,2048]{2,1,0:T(8,128)(2,1)}), bf16[8,128,2048]{2,1,0:T(8,128)(2,1)}, u32[]{:S(2)}, u32[]{:S(2)}) async-start(bf16[8,128,2048]{2,1,0:T(8,128)(2,1)} %bitcast.63), calls=%async_computation.4 | async-start | bytes 8388608 | tf_op jit(solution)/shard_map/all_to_all | solution.py:715
  1577.0 77.6 %copy-start.25 = (f32[4224]{0:T(1024)S(1)}, f32[4224]{0:T(1024)}, u32[]{:S(2)}) copy-start(f32[4224]{0:T(1024)} %param.47) | copy-start | bytes 50692
  1577.0 77.6 %copy-start.30 = (f32[4224]{0:T(1024)S(1)}, f32[4224]{0:T(1024)}, u32[]{:S(2)}) copy-start(f32[4224]{0:T(1024)} %param.48) | copy-start | bytes 50692
  1577.0 77.6 %copy-start.31 = (f32[4224]{0:T(1024)S(1)}, f32[4224]{0:T(1024)}, u32[]{:S(2)}) copy-start(f32[4224]{0:T(1024)} %param.49) | copy-start | bytes 50692
  1577.0 102.7 %copy-start.12 = (f32[256,3,512]{0,2,1:T(8,128)S(1)}, f32[256,3,512]{0,2,1:T(8,128)}, u32[]{:S(2)}) copy-start(f32[256,3,512]{0,2,1:T(8,128)} %copy-done.11) | copy-start | bytes 4718596
  1577.0 102.6 %copy-start.16 = (f32[256,3,512]{0,2,1:T(8,128)S(1)}, f32[256,3,512]{0,2,1:T(8,128)}, u32[]{:S(2)}) copy-start(f32[256,3,512]{0,2,1:T(8,128)} %copy.90) | copy-start | bytes 4718596
  1684.5 3.2 copy-start.18
  1684.5 4.8 copy-start.17
  (12 other events, 18.5 us)
Sparse Core Ops, SparseCore 0:
  10.5 73.2 all-gather.8
  86.2 39.2 all-gather.10
  322.7 86.7 reduce-scatter.11
  412.0 105.4 all-gather.14
  519.6 80.7 all-gather.12
  602.8 42.8 all-gather.16
  680.8 76.7 reduce-scatter.15
  762.8 81.2 all-gather.20
  997.9 81.3 reduce-scatter.17
  1081.6 77.2 reduce-scatter.13
  1164.4 81.2 all-gather.22
  1249.0 86.2 reduce-scatter.25
  1339.4 34.8 reduce-scatter.27
  1378.1 86.7 reduce-scatter.23
  1466.9 80.7 all-gather.18
  1551.2 58.7 reduce-scatter.21
  1613.2 63.8 reduce-scatter.19

commit v2 on v1

v2 whole, which is shorter than its diff:
```python
import functools

import jax
import jax.numpy as jnp
from jax import lax
from jax.experimental import pallas as pl
from jax.experimental.pallas import tpu as pltpu
from jax.sharding import PartitionSpec as P

HEAD = 128
TAPS = 4
GROUP = 64
BUSY_FLOPS = 10_000_000
MAPS_BATCH = 4
CHAIN_BATCH = 4
BACK_BATCH = 2
STEP = 10


EPSILON = 1e-06
PRECISE = lax.Precision.HIGHEST
MESH = pl.DeviceIdType.MESH
FIRST_DECAY = 0.9
SECOND_DECAY = 0.95
ADAM_EPSILON = 1e-08
RATE_WIDE = 0.044
RATE_DOWN = 0.027
RATE_CONV = 0.8
RATE_GAIN = 0.3
SHRINK = 0.1


def halves(value):
    high = value.astype(jnp.bfloat16)
    return high, (value - high.astype(jnp.float32)).astype(jnp.bfloat16)


def mul(left, right, dims=((1,), (0,))):
    def one(a, b):
        return lax.dot_general(a, b, (dims, ((), ())), preferred_element_type=jnp.float32)

    left_high, left_low = halves(left)
    right_high, right_low = halves(right)
    return one(left_high, right_high) + (one(left_high, right_low) + one(left_low, right_high))


def mul_nt(left, right):
    return mul(left, right, ((1,), (1,)))


def grid_indices(size):
    return (
        lax.broadcasted_iota(jnp.int32, (size, size), 0),
        lax.broadcasted_iota(jnp.int32, (size, size), 1),
    )


def unit_lower_inverses(strict_parts):
    size = strict_parts[0].shape[0]
    rows, cols = grid_indices(size)
    inverses = [jnp.where(rows == cols, 1.0, 0.0) for _ in strict_parts]
    level = 0
    while (1 << level) < size:
        corner = (
            ((rows >> (level + 1)) == (cols >> (level + 1)))
            & (((rows >> level) & 1) == 1)
            & (((cols >> level) & 1) == 0)
        )
        parts = [jnp.where(corner, strict, 0.0) for strict in strict_parts]
        if level == 0:
            inverses = [inverse - part for inverse, part in zip(inverses, parts)]
        else:
            inner = [mul(part, inverse) for inverse, part in zip(inverses, parts)]
            outer = [mul(inverse, part) for inverse, part in zip(inverses, inner)]
            inverses = [inverse - part for inverse, part in zip(inverses, outer)]
        level += 1
    return inverses


def sigmoid(value):
    return 1.0 / (1.0 + jnp.exp(-value))


def unit_scale(act):
    return lax.rsqrt(jnp.sum(act * act, axis=-1, keepdims=True) + EPSILON)


def head_lanes(column):
    return slice(column * HEAD, (column + 1) * HEAD)


def maps_kernel(
    heads,
    batch,
    keep_ref,
    pre_ref,
    edge_ref,
    logit_ref,
    taps_ref,
    conv_ref,
    solved_ref,
    square_ref,
    step_ref,
    fresh_ref,
    reach_ref,
    zero_out_ref,
    total_ref,
    history,
    running,
):
    turn = pl.program_id(0)
    scale = HEAD**-0.5
    pairs = [(item, head) for item in range(batch) for head in range(heads)]
    keeps = [keep_ref[turn * batch + item] for item in range(batch)]

    @pl.when(turn == 0)
    def _():
        history[0, 0:8, :] = edge_ref[...] * keeps[0]
        rows, cols = grid_indices(HEAD)
        start = jnp.where(rows == cols, 1.0, 0.0)
        for head in range(heads):
            running[head, :, 0:HEAD] = start
            running[head, :, HEAD : 2 * HEAD] = jnp.zeros((HEAD, HEAD), jnp.float32)

    @pl.when(turn > 0)
    def _():
        history[0, 0:8, :] = history[batch - 1, GROUP : GROUP + 8, :] * keeps[0]

    for item in range(batch):
        history[item, 8 : GROUP + 8, :] = pre_ref[
            item * GROUP : (item + 1) * GROUP, :
        ].astype(jnp.float32)
        if item:
            history[item, 0:8, :] = history[item - 1, GROUP : GROUP + 8, :] * keeps[item]

    def conv_of(item, column):
        cols = head_lanes(column)
        total = taps_ref[0:1, cols] * history[item, 5 : 5 + GROUP, cols]
        for tap in range(1, TAPS):
            shifted = history[item, 5 + tap : 5 + tap + GROUP, cols]
            total = total + taps_ref[tap : tap + 1, cols] * shifted
        conv_ref[item * GROUP : (item + 1) * GROUP, cols] = total
        return total * sigmoid(total)

    rows, cols = grid_indices(GROUP)
    big_rows, big_cols = grid_indices(HEAD)
    keys = [conv_of(item, heads + head) for item, head in pairs]
    keys = [key * unit_scale(key) for key in keys]
    strengths = [
        sigmoid(logit_ref[item * GROUP : (item + 1) * GROUP, head : head + 1])
        for item, head in pairs
    ]
    overlaps = [mul_nt(key, key) for key in keys]
    inverses = unit_lower_inverses(
        [
            jnp.where(rows > cols, strength * overlap, 0.0)
            for strength, overlap in zip(strengths, overlaps)
        ]
    )
    queries = [conv_of(item, head) for item, head in pairs]
    queries = [query * unit_scale(query) for query in queries]
    scores = [
        jnp.where(rows >= cols, mul_nt(query, key), 0.0) for query, key in zip(queries, keys)
    ]
    values = [conv_of(item, 2 * heads + head) for item, head in pairs]
    solved = [
        mul(inverse, jnp.concatenate([strength * key, strength * value], axis=1))
        for inverse, strength, key, value in zip(inverses, strengths, keys, values)
    ]
    pushed = [mul(key.T, part) for key, part in zip(keys, solved)]
    mixed = [mul(score, part) for score, part in zip(scores, solved)]
    steps = [jnp.where(big_rows == big_cols, 1.0, 0.0) - part[:, 0:HEAD] for part in pushed]
    for index, (item, head) in enumerate(pairs):
        here = slice(item * GROUP, (item + 1) * GROUP)
        solved_ref[item, head] = solved[index]
        square_ref[item, head, :, 0:GROUP] = inverses[index]
        square_ref[item, head, :, GROUP : 2 * GROUP] = scores[index]
        reach_ref[here, head_lanes(head)] = scale * (queries[index] - mixed[index][:, 0:HEAD])
        zero_out_ref[here, head_lanes(head)] = scale * mixed[index][:, HEAD:]
        step_ref[item, head] = steps[index]
        fresh_ref[item, head] = pushed[index][:, HEAD:]
    now = [running[head] for head in range(heads)]
    for item in range(batch):
        first = item * heads
        moved = [mul(steps[first + head], now[head] * keeps[item]) for head in range(heads)]
        now = [
            jnp.concatenate(
                [moved[head][:, 0:HEAD], moved[head][:, HEAD:] + pushed[first + head][:, HEAD:]],
                axis=1,
            )
            for head in range(heads)
        ]
    for head in range(heads):
        running[head] = now[head]
    total_ref[...] = running[...]


def outputs_kernel(
    heads,
    batch,
    keep_ref,
    incoming_ref,
    step_ref,
    fresh_ref,
    reach_ref,
    zero_out_ref,
    gain_ref,
    state_ref,
    mixed_ref,
    normed_ref,
    running,
):
    turn = pl.program_id(0)

    @pl.when(turn == 0)
    def _():
        running[...] = incoming_ref[...]

    now = [running[head] for head in range(heads)]
    states = []
    for item in range(batch):
        keep = keep_ref[turn * batch + item]
        now = [state * keep for state in now]
        states.append(now)
        now = [
            mul(step_ref[item, head], now[head]) + fresh_ref[item, head] for head in range(heads)
        ]
    for head in range(heads):
        running[head] = now[head]
    for item in range(batch):
        here = slice(item * GROUP, (item + 1) * GROUP)
        outs = [
            mul(reach_ref[here, head_lanes(head)], states[item][head])
            + zero_out_ref[here, head_lanes(head)]
            for head in range(heads)
        ]
        for head, mixed in enumerate(outs):
            state_ref[item, head] = states[item][head]
            mixed_ref[here, head_lanes(head)] = mixed
            inverse_rms = lax.rsqrt(jnp.mean(mixed * mixed, axis=-1, keepdims=True) + EPSILON)
            normed_ref[here, head_lanes(head)] = (mixed * inverse_rms * gain_ref[...]).astype(
                jnp.bfloat16
            )


def tail_kernel(
    heads,
    batch,
    keep_ref,
    d_normed_ref,
    mixed_ref,
    gain_ref,
    step_ref,
    reach_ref,
    d_mixed_ref,
    d_state_ref,
    d_gain_ref,
    running,
):
    turn = pl.num_programs(0) - 1 - pl.program_id(0)

    @pl.when(pl.program_id(0) == 0)
    def _():
        running[...] = jnp.zeros_like(running)
        d_gain_ref[...] = jnp.zeros_like(d_gain_ref)

    gain_sum = jnp.zeros((1, HEAD), jnp.float32)
    pulled = []
    for item in range(batch):
        here = slice(item * GROUP, (item + 1) * GROUP)
        grads = []
        for head in range(heads):
            mixed = mixed_ref[here, head_lanes(head)]
            d_normed = d_normed_ref[here, head_lanes(head)]
            inverse_rms = lax.rsqrt(jnp.mean(mixed * mixed, axis=-1, keepdims=True) + EPSILON)
            unit = mixed * inverse_rms
            gain_sum = gain_sum + jnp.sum(d_normed * unit, axis=0, keepdims=True)
            d_unit = d_normed * gain_ref[...]
            d_mixed = inverse_rms * (
                d_unit - unit * jnp.mean(d_unit * unit, axis=-1, keepdims=True)
            )
            d_mixed_ref[here, head_lanes(head)] = d_mixed
            grads.append(d_mixed)
        pulled.append(
            [mul(reach_ref[here, head_lanes(head)].T, grads[head]) for head in range(heads)]
        )
    now = [running[head] for head in range(heads)]
    for item in reversed(range(batch)):
        keep = keep_ref[turn * batch + item]
        now = [
            keep * (mul(step_ref[item, head].T, now[head]) + pulled[item][head])
            for head in range(heads)
        ]
    for head in range(heads):
        running[head] = now[head]
    d_gain_ref[...] += gain_sum
    d_state_ref[...] = running[...]


def back_kernel(
    heads,
    batch,
    keep_ref,
    outgoing_ref,
    pre_ref,
    edge_ref,
    logit_ref,
    taps_ref,
    conv_ref,
    solved_ref,
    square_ref,
    step_ref,
    reach_ref,
    state_ref,
    d_mixed_ref,
    d_pre_ref,
    d_tail_ref,
    d_edge_ref,
    d_taps_ref,
    d_history,
    edge_history,
    running,
):
    count = pl.num_programs(0)
    turn = count - 1 - pl.program_id(0)
    scale = HEAD**-0.5
    rows, cols = grid_indices(GROUP)
    pairs = [(item, head) for item in range(batch) for head in range(heads)]
    indices = range(len(pairs))
    keeps = [keep_ref[turn * batch + item] for item in range(batch)]

    @pl.when(pl.program_id(0) == 0)
    def _():
        running[...] = outgoing_ref[...]
        d_history[batch - 1, GROUP : GROUP + 8, :] = jnp.zeros(
            (8, d_history.shape[2]), jnp.float32
        )
        d_taps_ref[...] = jnp.zeros_like(d_taps_ref)

    @pl.when(pl.program_id(0) > 0)
    def _():
        d_history[batch - 1, GROUP : GROUP + 8, :] = (
            d_history[0, 0:8, :] * keep_ref[(turn + 1) * batch]
        )

    def spot(item):
        return slice(item * GROUP, (item + 1) * GROUP)

    def act_of(item, column):
        conv = conv_ref[spot(item), head_lanes(column)]
        return conv * sigmoid(conv)

    def slope_of(item, column):
        conv = conv_ref[spot(item), head_lanes(column)]
        gate = sigmoid(conv)
        return gate * (1.0 + conv * (1.0 - gate))

    def d_unit(unit, inverse_norm, grad):
        return inverse_norm * (grad - unit * jnp.sum(unit * grad, axis=-1, keepdims=True))

    d_mixed = [d_mixed_ref[spot(item), head_lanes(head)] for item, head in pairs]
    pulled = [
        mul(reach_ref[spot(item), head_lanes(head)].T, d_mixed[index])
        for index, (item, head) in enumerate(pairs)
    ]
    d_states = [None] * len(pairs)
    now = [running[head] for head in range(heads)]
    for item in reversed(range(batch)):
        first = item * heads
        d_states[first : first + heads] = now
        now = [
            keeps[item] * (mul(step_ref[item, head].T, now[head]) + pulled[first + head])
            for head in range(heads)
        ]
    for head in range(heads):
        running[head] = now[head]

    d_out = [scale * grad for grad in d_mixed]
    states = [state_ref[item, head] for item, head in pairs]
    solved = [solved_ref[item, head] for item, head in pairs]
    scores = [square_ref[item, head, :, GROUP : 2 * GROUP] for item, head in pairs]
    acts = [act_of(item, heads + head) for item, head in pairs]
    key_scales = [unit_scale(act) for act in acts]
    keys = [act * size for act, size in zip(acts, key_scales)]
    fresh = [
        solved[index][:, HEAD:] - mul(solved[index][:, 0:HEAD], states[index])
        for index in indices
    ]
    d_fresh = [
        mul(scores[index].T, d_out[index]) + mul(keys[index], d_states[index])
        for index in indices
    ]
    d_scores = [
        jnp.where(rows >= cols, mul_nt(d_out[index], fresh[index]), 0.0) for index in indices
    ]
    d_solved = [
        jnp.concatenate([-mul_nt(d_fresh[index], states[index]), d_fresh[index]], axis=1)
        for index in indices
    ]
    d_right = [
        mul(square_ref[item, head, :, 0:GROUP].T, d_solved[index])
        for index, (item, head) in enumerate(pairs)
    ]
    d_queries = [
        mul_nt(d_out[index], states[index]) + mul(d_scores[index], keys[index])
        for index in indices
    ]
    acts = [act_of(item, head) for item, head in pairs]
    query_scales = [unit_scale(act) for act in acts]
    queries = [act * size for act, size in zip(acts, query_scales)]
    d_keys = [
        mul(d_scores[index].T, queries[index]) + mul_nt(fresh[index], d_states[index])
        for index in indices
    ]
    d_strict = [
        jnp.where(rows > cols, -mul_nt(d_right[index], solved[index]), 0.0) for index in indices
    ]
    strengths = [
        sigmoid(logit_ref[spot(item), head : head + 1]) for item, head in pairs
    ]
    overlaps = [mul_nt(key, key) for key in keys]
    both = [
        strengths[index] * d_strict[index] + (strengths[index] * d_strict[index]).T
        for index in indices
    ]
    d_keys = [
        d_keys[index]
        + strengths[index] * d_right[index][:, 0:HEAD]
        + mul(both[index], keys[index])
        for index in indices
    ]
    d_logits = []
    for index, (item, head) in enumerate(pairs):
        strength = strengths[index]
        value = act_of(item, 2 * heads + head)
        d_strength = (
            jnp.sum(d_right[index][:, 0:HEAD] * keys[index], axis=-1, keepdims=True)
            + jnp.sum(d_right[index][:, HEAD:] * value, axis=-1, keepdims=True)
            + jnp.sum(d_strict[index] * overlaps[index], axis=-1, keepdims=True)
        )
        d_logits.append(d_strength * strength * (1.0 - strength))
        for column, grad in (
            (head, d_unit(queries[index], query_scales[index], d_queries[index])),
            (heads + head, d_unit(keys[index], key_scales[index], d_keys[index])),
            (2 * heads + head, strength * d_right[index][:, HEAD:]),
        ):
            d_history[item, 0:GROUP, head_lanes(column)] = grad * slope_of(item, column)

    spread = lax.broadcasted_iota(jnp.int32, (GROUP, HEAD), 1)
    for item in range(batch):
        placed = jnp.zeros((GROUP, HEAD), jnp.float32)
        for head in range(heads):
            placed = jnp.where(spread == head, d_logits[item * heads + head], placed)
        d_pre_ref[spot(item), 3 * heads * HEAD :] = placed.astype(jnp.bfloat16)

    for item in reversed(range(batch - 1)):
        d_history[item, GROUP : GROUP + 8, :] = d_history[item + 1, 0:8, :] * keeps[item + 1]
    for column in range(3 * heads):
        lanes = head_lanes(column)
        for item in range(batch):
            pre = pre_ref[spot(item), lanes].astype(jnp.float32)
            total = jnp.zeros((GROUP, HEAD), jnp.float32)
            for tap in range(TAPS):
                part = d_history[item, TAPS - 1 - tap : TAPS - 1 - tap + GROUP, lanes]
                total = total + taps_ref[tap : tap + 1, lanes] * part
                d_taps_ref[tap : tap + 1, lanes] += jnp.sum(pre * part, axis=0, keepdims=True)
            d_pre_ref[spot(item), lanes] = total.astype(jnp.bfloat16)
        d_tail_ref[:, lanes] = jnp.where(
            turn == count - 1, total[GROUP - 8 :, :], d_tail_ref[:, lanes]
        )

    @pl.when(turn == 0)
    def _():
        edge_history[0:8, :] = jnp.zeros((8, edge_history.shape[1]), jnp.float32)
        edge_history[8:16, :] = d_history[0, 0:8, :] * keeps[0]
        total = jnp.zeros(d_edge_ref.shape, jnp.float32)
        for tap in range(TAPS):
            part = edge_history[TAPS - 1 - tap : TAPS - 1 - tap + 8, :]
            total = total + taps_ref[tap : tap + 1, :] * part
            d_taps_ref[tap : tap + 1, :] += jnp.sum(edge_ref[...] * part, axis=0, keepdims=True)
        d_edge_ref[...] = total


def passed_along(value, axis, by):
    count = lax.axis_size(axis)
    pairs = [(i, i + by) for i in range(count) if 0 <= i + by < count]
    return lax.ppermute(value, axis, pairs)


def adamw(weight, first, second, grad, rate, decay):
    first = FIRST_DECAY * first + (1.0 - FIRST_DECAY) * grad
    second = SECOND_DECAY * second + (1.0 - SECOND_DECAY) * grad * grad
    stepped = (
        first
        / (1.0 - FIRST_DECAY**STEP)
        / (jnp.sqrt(second / (1.0 - SECOND_DECAY**STEP)) + ADAM_EPSILON)
    )
    return (weight - rate * (stepped + decay * weight), first, second)


def f32(*shape):
    return jax.ShapeDtypeStruct(shape, jnp.float32)


def bf16(*shape):
    return jax.ShapeDtypeStruct(shape, jnp.bfloat16)


class Rule:
    def __init__(self, keep, heads, row_count):
        self.keep, self.heads, self.rows = keep, heads, row_count
        self.count = row_count // GROUP
        self.params = pltpu.CompilerParams(
            dimension_semantics=("arbitrary",), vmem_limit_bytes=48 * 1024 * 1024
        )

    def rows_spec(self, width, batch, back=False):
        last = self.count // batch - 1
        if back:
            return pl.BlockSpec((batch * GROUP, width), lambda n: (last - n, 0))
        return pl.BlockSpec((batch * GROUP, width), lambda n: (n, 0))

    def block_spec(self, shape, batch, back=False):
        last = self.count // batch - 1
        if back:
            return pl.BlockSpec((batch,) + shape, lambda n: (last - n, 0, 0, 0))
        return pl.BlockSpec((batch,) + shape, lambda n: (n, 0, 0, 0))

    def whole(self, *shape):
        return pl.BlockSpec(shape, lambda n: (0,) * len(shape))

    def smem(self):
        return pl.BlockSpec(memory_space=pltpu.SMEM)

    def maps(self, pre, edge, logits, taps):
        heads, rows, count, inner = self.heads, self.rows, self.count, self.heads * HEAD
        return pl.pallas_call(
            functools.partial(maps_kernel, heads, MAPS_BATCH),
            grid=(count // MAPS_BATCH,),
            in_specs=[
                self.smem(),
                self.rows_spec(3 * inner, MAPS_BATCH),
                self.whole(8, 3 * inner),
                self.rows_spec(heads, MAPS_BATCH),
                self.whole(TAPS, 3 * inner),
            ],
            out_specs=[
                self.rows_spec(3 * inner, MAPS_BATCH),
                self.block_spec((heads, GROUP, 2 * HEAD), MAPS_BATCH),
                self.block_spec((heads, GROUP, 2 * GROUP), MAPS_BATCH),
                self.block_spec((heads, HEAD, HEAD), MAPS_BATCH),
                self.block_spec((heads, HEAD, HEAD), MAPS_BATCH),
                self.rows_spec(inner, MAPS_BATCH),
                self.rows_spec(inner, MAPS_BATCH),
                self.whole(heads, HEAD, 2 * HEAD),
            ],
            out_shape=[
                f32(rows, 3 * inner),
                f32(count, heads, GROUP, 2 * HEAD),
                f32(count, heads, GROUP, 2 * GROUP),
                f32(count, heads, HEAD, HEAD),
                f32(count, heads, HEAD, HEAD),
                f32(rows, inner),
                f32(rows, inner),
                f32(heads, HEAD, 2 * HEAD),
            ],
            scratch_shapes=[
                pltpu.VMEM((MAPS_BATCH, GROUP + 8, 3 * inner), jnp.float32),
                pltpu.VMEM((heads, HEAD, 2 * HEAD), jnp.float32),
            ],
            compiler_params=self.params,
            cost_estimate=busy(35),
            name="delta_maps",
        )(self.keep, pre, edge, logits, taps)

    def outputs(self, incoming, step, fresh, reach, zero_out, gain):
        heads, rows, count, inner = self.heads, self.rows, self.count, self.heads * HEAD
        return pl.pallas_call(
            functools.partial(outputs_kernel, heads, CHAIN_BATCH),
            grid=(count // CHAIN_BATCH,),
            in_specs=[
                self.smem(),
                self.whole(heads, HEAD, HEAD),
                self.block_spec((heads, HEAD, HEAD), CHAIN_BATCH),
                self.block_spec((heads, HEAD, HEAD), CHAIN_BATCH),
                self.rows_spec(inner, CHAIN_BATCH),
                self.rows_spec(inner, CHAIN_BATCH),
                self.whole(1, HEAD),
            ],
            out_specs=[
                self.block_spec((heads, HEAD, HEAD), CHAIN_BATCH),
                self.rows_spec(inner, CHAIN_BATCH),
                self.rows_spec(inner, CHAIN_BATCH),
            ],
            out_shape=[f32(count, heads, HEAD, HEAD), f32(rows, inner), bf16(rows, inner)],
            scratch_shapes=[pltpu.VMEM((heads, HEAD, HEAD), jnp.float32)],
            compiler_params=self.params,
            cost_estimate=busy(9),
            name="delta_outputs",
        )(self.keep, incoming, step, fresh, reach, zero_out, gain)

    def tail(self, d_normed, mixed, gain, step, reach):
        heads, rows, count, inner = self.heads, self.rows, self.count, self.heads * HEAD
        return pl.pallas_call(
            functools.partial(tail_kernel, heads, CHAIN_BATCH),
            grid=(count // CHAIN_BATCH,),
            in_specs=[
                self.smem(),
                self.rows_spec(inner, CHAIN_BATCH, True),
                self.rows_spec(inner, CHAIN_BATCH, True),
                self.whole(1, HEAD),
                self.block_spec((heads, HEAD, HEAD), CHAIN_BATCH, True),
                self.rows_spec(inner, CHAIN_BATCH, True),
            ],
            out_specs=[
                self.rows_spec(inner, CHAIN_BATCH, True),
                self.whole(heads, HEAD, HEAD),
                self.whole(1, HEAD),
            ],
            out_shape=[f32(rows, inner), f32(heads, HEAD, HEAD), f32(1, HEAD)],
            scratch_shapes=[pltpu.VMEM((heads, HEAD, HEAD), jnp.float32)],
            compiler_params=self.params,
            cost_estimate=busy(11),
            name="delta_tail",
        )(self.keep, d_normed, mixed, gain, step, reach)

    def back(self, outgoing, pre, edge, logits, taps, conv, solved, square, step, reach, state, d_mixed):
        heads, rows, count, inner = self.heads, self.rows, self.count, self.heads * HEAD
        return pl.pallas_call(
            functools.partial(back_kernel, heads, BACK_BATCH),
            grid=(count // BACK_BATCH,),
            in_specs=[
                self.smem(),
                self.whole(heads, HEAD, HEAD),
                self.rows_spec(3 * inner, BACK_BATCH, True),
                self.whole(8, 3 * inner),
                self.rows_spec(heads, BACK_BATCH, True),
                self.whole(TAPS, 3 * inner),
                self.rows_spec(3 * inner, BACK_BATCH, True),
                self.block_spec((heads, GROUP, 2 * HEAD), BACK_BATCH, True),
                self.block_spec((heads, GROUP, 2 * GROUP), BACK_BATCH, True),
                self.block_spec((heads, HEAD, HEAD), BACK_BATCH, True),
                self.rows_spec(inner, BACK_BATCH, True),
                self.block_spec((heads, HEAD, HEAD), BACK_BATCH, True),
                self.rows_spec(inner, BACK_BATCH, True),
            ],
            out_specs=[
                self.rows_spec(3 * inner + HEAD, BACK_BATCH, True),
                self.whole(8, 3 * inner),
                self.whole(8, 3 * inner),
                self.whole(TAPS, 3 * inner),
            ],
            out_shape=[
                bf16(rows, 3 * inner + HEAD),
                f32(8, 3 * inner),
                f32(8, 3 * inner),
                f32(TAPS, 3 * inner),
            ],
            scratch_shapes=[
                pltpu.VMEM((BACK_BATCH, GROUP + 8, 3 * inner), jnp.float32),
                pltpu.VMEM((16, 3 * inner), jnp.float32),
                pltpu.VMEM((heads, HEAD, HEAD), jnp.float32),
            ],
            compiler_params=self.params,
            cost_estimate=busy(45),
            name="delta_back",
        )(
            self.keep, outgoing, pre, edge, logits, taps, conv, solved, square, step, reach, state,
            d_mixed,
        )


def rms_unit(values):
    return values * lax.rsqrt(jnp.mean(values * values, axis=-1, keepdims=True) + EPSILON)


def rms_back(values, gain_vec, grad):
    inverse_rms = lax.rsqrt(jnp.mean(values * values, axis=-1, keepdims=True) + EPSILON)
    unit = values * inverse_rms
    d_unit = grad * gain_vec
    d_values = inverse_rms * (d_unit - unit * jnp.mean(d_unit * unit, axis=-1, keepdims=True))
    return d_values, jnp.sum(grad * unit, axis=0)


def low(values):
    return values.astype(jnp.bfloat16)


def product(left, right, dims=((1,), (0,))):
    return lax.dot_general(left, right, (dims, ((), ())), preferred_element_type=jnp.float32)


def rows_summed(partial):
    return lax.psum_scatter(low(partial), "shard", scatter_dimension=0, tiled=True)


def rows_joined(rows):
    return lax.all_gather(rows, "shard", axis=0, tiled=True)


def seq_summed(grad, dim):
    return lax.psum_scatter(grad, "seq", scatter_dimension=dim, tiled=True)


def one_hot(indices, size):
    return (jnp.arange(size, dtype=jnp.int32)[:, None] == indices[None, :]).astype(jnp.bfloat16)


def moved(matrix, values):
    return low(product(matrix, values))


def moved_back(matrix, values):
    return low(product(matrix, values, ((0,), (0,))))


def busy(micros):
    return pl.CostEstimate(flops=micros * BUSY_FLOPS, bytes_accessed=0, transcendentals=0)


def ends(count):
    me = lax.axis_index("shard")
    return me, me > 0, me < count - 1


def meet_neighbours(count):
    me, has_left, has_right = ends(count)
    barrier = pltpu.get_barrier_semaphore()

    @pl.when(has_left)
    def _():
        pl.semaphore_signal(barrier, inc=1, device_id={"shard": me - 1}, device_id_type=MESH)

    @pl.when(has_right)
    def _():
        pl.semaphore_signal(barrier, inc=1, device_id={"shard": me + 1}, device_id_type=MESH)

    pl.semaphore_wait(barrier, has_left.astype(jnp.int32) + has_right.astype(jnp.int32))


def join_kernel(count, parts, own_ref, out_ref, own_sem, send_sem, recv_sem):
    me, has_left, has_right = ends(count)
    size = own_ref.shape[0] // parts
    meet_neighbours(count)
    own_copy = pltpu.make_async_copy(own_ref, out_ref.at[me], own_sem)
    own_copy.start()

    def piece_copy(way, block, part, source, target):
        rows = pl.ds(part * size, size)
        return pltpu.make_async_remote_copy(
            src_ref=source.at[rows] if source is own_ref else source.at[block, rows],
            dst_ref=out_ref.at[block, rows],
            send_sem=send_sem.at[way, block, part],
            recv_sem=recv_sem.at[block, part],
            device_id={"shard": target},
            device_id_type=MESH,
        )

    def each(action):
        for far in range(count):
            for part in range(parts):
                for way, present, onward, block, target in (
                    (0, me >= far, has_right, me - far, me + 1),
                    (1, me + far < count, has_left, me + far, me - 1),
                ):
                    action(far, part, way, present, onward, block, target)

    def start(far, part, way, present, onward, block, target):
        source = own_ref if far == 0 else out_ref

        if far:

            @pl.when(present)
            def _():
                piece_copy(way, block, part, out_ref, target).wait_recv()

        @pl.when(present & onward)
        def _():
            piece_copy(way, block, part, source, target).start()

    def finish(far, part, way, present, onward, block, target):
        source = own_ref if far == 0 else out_ref

        @pl.when(present & onward)
        def _():
            piece_copy(way, block, part, source, target).wait_send()

    each(start)
    each(finish)
    own_copy.wait()


def join_rows(rows, count, ident, parts=4):
    size, width = rows.shape
    return pl.pallas_call(
        functools.partial(join_kernel, count, parts),
        out_shape=jax.ShapeDtypeStruct((count, size, width), rows.dtype),
        in_specs=[pl.BlockSpec(memory_space=pl.ANY)],
        out_specs=pl.BlockSpec(memory_space=pl.ANY),
        scratch_shapes=[
            pltpu.SemaphoreType.DMA(()),
            pltpu.SemaphoreType.DMA((2, count, parts)),
            pltpu.SemaphoreType.DMA((count, parts)),
        ],
        compiler_params=pltpu.CompilerParams(collective_id=ident, has_side_effects=True),
        cost_estimate=busy(70),
        name="join_rows",
    )(rows).reshape(count * size, width)


def swap_kernel(count, to_columns, in_ref, out_ref, own_sem, send_sem, recv_sem):
    me = lax.axis_index("shard")
    barrier = pltpu.get_barrier_semaphore()
    for hop in range(1, count):
        other = lax.rem(me + hop, count)
        pl.semaphore_signal(barrier, inc=1, device_id={"shard": other}, device_id_type=MESH)
    pl.semaphore_wait(barrier, count - 1)
    if to_columns:
        width = in_ref.shape[2]
    else:
        width = out_ref.shape[2]

    def columns(ref, index):
        return ref.at[:, pl.ds(pl.multiple_of(index * width, width), width)]

    def source(block):
        return in_ref.at[block] if to_columns else columns(in_ref, block)

    def landing(block):
        return columns(out_ref, block) if to_columns else out_ref.at[block]

    own_copy = pltpu.make_async_copy(source(me), landing(me), own_sem)
    own_copy.start()

    def block_copy(hop):
        other = lax.rem(me + hop, count)
        return pltpu.make_async_remote_copy(
            src_ref=source(other),
            dst_ref=landing(me),
            send_sem=send_sem.at[hop],
            recv_sem=recv_sem.at[hop],
            device_id={"shard": other},
            device_id_type=MESH,
        )

    for hop in range(1, count):
        block_copy(hop).start()
    for hop in range(1, count):
        block_copy(hop).wait()
    own_copy.wait()


def swap_blocks(value, count, ident, to_columns):
    if to_columns:
        _, size, width = value.shape
        shape = (size, count * width)
    else:
        size, width = value.shape[0], value.shape[1] // count
        shape = (count, size, width)
    return pl.pallas_call(
        functools.partial(swap_kernel, count, to_columns),
        out_shape=jax.ShapeDtypeStruct(shape, value.dtype),
        in_specs=[pl.BlockSpec(memory_space=pl.ANY)],
        out_specs=pl.BlockSpec(memory_space=pl.ANY),
        scratch_shapes=[
            pltpu.SemaphoreType.DMA(()),
            pltpu.SemaphoreType.DMA((count,)),
            pltpu.SemaphoreType.DMA((count,)),
        ],
        compiler_params=pltpu.CompilerParams(collective_id=ident, has_side_effects=True),
        cost_estimate=busy(23),
        name="swap_blocks",
    )(value)


def relay_kernel(heads, hops, back, total_ref, fresh_ref, out_ref, sending, landing, send_sem, recv_sem):
    count = lax.axis_size("seq")
    me = lax.axis_index("seq")
    if back:
        follows, precedes, target, origin = me < count - 1, me > 0, me - 1, me + 1
    else:
        follows, precedes, target, origin = me > 0, me < count - 1, me + 1, me - 1
    barrier = pltpu.get_barrier_semaphore()

    @pl.when(follows)
    def _():
        pl.semaphore_signal(barrier, inc=1, device_id={"seq": origin}, device_id_type=MESH)

    @pl.when(precedes)
    def _():
        pl.semaphore_signal(barrier, inc=1, device_id={"seq": target}, device_id_type=MESH)

    pl.semaphore_wait(barrier, follows.astype(jnp.int32) + precedes.astype(jnp.int32))

    def state_copy(hop, head):
        return pltpu.make_async_remote_copy(
            src_ref=sending.at[hop, head],
            dst_ref=landing.at[hop, head],
            send_sem=send_sem.at[hop, head],
            recv_sem=recv_sem.at[hop, head],
            device_id={"seq": target},
            device_id_type=MESH,
        )

    for hop in range(hops):
        for head in range(heads):
            fresh = fresh_ref[head]
            if hop == 0:
                sending[hop, head] = low(fresh)
            else:

                @pl.when(follows)
                def _():
                    state_copy(hop - 1, head).wait_recv()
                    step = total_ref[head, :, 0:HEAD]
                    step = step.T if back else step
                    sending[hop, head] = low(
                        fresh + mul(step, landing[hop - 1, head].astype(jnp.float32))
                    )

                @pl.when(jnp.logical_not(follows))
                def _():
                    sending[hop, head] = low(fresh)

            @pl.when(precedes)
            def _():
                state_copy(hop, head).start()

    for head in range(heads):

        @pl.when(follows)
        def _():
            state_copy(hops - 1, head).wait_recv()
            out_ref[head] = landing[hops - 1, head].astype(jnp.float32)

        @pl.when(jnp.logical_not(follows))
        def _():
            out_ref[head] = jnp.zeros((HEAD, HEAD), jnp.float32)

    @pl.when(precedes)
    def _():
        for hop in range(hops):
            for head in range(heads):
                state_copy(hop, head).wait_send()


def relayed(total, fresh, hops, back, ident):
    heads = fresh.shape[0]
    return pl.pallas_call(
        functools.partial(relay_kernel, heads, hops, back),
        out_shape=jax.ShapeDtypeStruct((heads, HEAD, HEAD), jnp.float32),
        in_specs=[pl.BlockSpec(memory_space=pltpu.VMEM)] * 2,
        out_specs=pl.BlockSpec(memory_space=pltpu.VMEM),
        scratch_shapes=[
            pltpu.VMEM((hops, heads, HEAD, HEAD), jnp.bfloat16),
            pltpu.VMEM((hops, heads, HEAD, HEAD), jnp.bfloat16),
            pltpu.SemaphoreType.DMA((hops, heads)),
            pltpu.SemaphoreType.DMA((hops, heads)),
        ],
        compiler_params=pltpu.CompilerParams(collective_id=ident, has_side_effects=True),
        cost_estimate=busy(15),
        name="relay_back" if back else "relay",
    )(total, fresh)


def last_join_kernel(
    count,
    parts,
    shared,
    own_ref,
    small_ref,
    out_ref,
    small_out,
    seq_slots,
    layer_slots,
    own_sem,
    send_sem,
    recv_sem,
    seq_send,
    seq_recv,
    layer_send,
    layer_recv,
):
    me, has_left, has_right = ends(count)
    size = own_ref.shape[0] // parts
    devices = lax.axis_size("seq")
    here = lax.axis_index("seq")
    barrier = pltpu.get_barrier_semaphore()
    for hop in range(1, devices):
        other = lax.rem(here + hop, devices)
        pl.semaphore_signal(barrier, inc=1, device_id={"seq": other}, device_id_type=MESH)
    for hop in range(1, count):
        other = lax.rem(me + hop, count)
        pl.semaphore_signal(barrier, inc=1, device_id={"shard": other}, device_id_type=MESH)
    pl.semaphore_wait(barrier, devices + count - 2)
    own_copy = pltpu.make_async_copy(own_ref, out_ref.at[me], own_sem)
    own_copy.start()

    def seq_copy(hop):
        return pltpu.make_async_remote_copy(
            src_ref=small_ref,
            dst_ref=seq_slots.at[here],
            send_sem=seq_send.at[hop],
            recv_sem=seq_recv.at[hop],
            device_id={"seq": lax.rem(here + hop, devices)},
            device_id_type=MESH,
        )

    def layer_copy(hop):
        return pltpu.make_async_remote_copy(
            src_ref=small_out.at[pl.ds(0, shared)],
            dst_ref=layer_slots.at[me],
            send_sem=layer_send.at[hop],
            recv_sem=layer_recv.at[hop],
            device_id={"shard": lax.rem(me + hop, count)},
            device_id_type=MESH,
        )

    def piece_copy(way, block, part, source, target):
        rows = pl.ds(part * size, size)
        return pltpu.make_async_remote_copy(
            src_ref=source.at[rows] if source is own_ref else source.at[block, rows],
            dst_ref=out_ref.at[block, rows],
            send_sem=send_sem.at[way, block, part],
            recv_sem=recv_sem.at[block, part],
            device_id={"shard": target},
            device_id_type=MESH,
        )

    def each(far, action):
        for part in range(parts):
            for way, present, onward, block, target in (
                (0, me >= far, has_right, me - far, me + 1),
                (1, me + far < count, has_left, me + far, me - 1),
            ):
                action(far, part, way, present, onward, block, target)

    def start(far, part, way, present, onward, block, target):
        if far:

            @pl.when(present)
            def _():
                piece_copy(way, block, part, out_ref, target).wait_recv()

        @pl.when(present & onward)
        def _():
            piece_copy(way, block, part, out_ref if far else own_ref, target).start()

    def finish(far, part, way, present, onward, block, target):
        @pl.when(present & onward)
        def _():
            piece_copy(way, block, part, out_ref if far else own_ref, target).wait_send()

    def seq_start(hop, carry):
        seq_copy(hop).start()
        return carry

    def seq_finish(hop, carry):
        seq_copy(hop).wait()
        return carry

    lax.fori_loop(1, devices, seq_start, 0)
    seq_slots[here] = small_ref[...]
    each(0, start)
    lax.fori_loop(1, devices, seq_finish, 0)
    total = seq_slots[0]
    for index in range(1, devices):
        total = total + seq_slots[index]
    small_out[...] = total
    for hop in range(1, count):
        layer_copy(hop).start()
    layer_slots[me] = total[0:shared]
    for far in range(1, count):
        each(far, start)
    for hop in range(1, count):
        layer_copy(hop).wait()
    total = layer_slots[0]
    for index in range(1, count):
        total = total + layer_slots[index]
    small_out[0:shared, :] = total
    for far in range(count):
        each(far, finish)
    own_copy.wait()


def join_rows_and_sum(rows, small, shared, count, ident, parts=4):
    size, width = rows.shape
    devices = lax.axis_size("seq")
    joined, summed = pl.pallas_call(
        functools.partial(last_join_kernel, count, parts, shared),
        out_shape=[jax.ShapeDtypeStruct((count, size, width), rows.dtype), f32(*small.shape)],
        in_specs=[pl.BlockSpec(memory_space=pl.ANY), pl.BlockSpec(memory_space=pltpu.VMEM)],
        out_specs=[pl.BlockSpec(memory_space=pl.ANY), pl.BlockSpec(memory_space=pltpu.VMEM)],
        scratch_shapes=[
            pltpu.VMEM((devices,) + small.shape, jnp.float32),
            pltpu.VMEM((count, shared, small.shape[1]), jnp.float32),
            pltpu.SemaphoreType.DMA(()),
            pltpu.SemaphoreType.DMA((2, count, parts)),
            pltpu.SemaphoreType.DMA((count, parts)),
            pltpu.SemaphoreType.DMA((devices,)),
            pltpu.SemaphoreType.DMA((devices,)),
            pltpu.SemaphoreType.DMA((count,)),
            pltpu.SemaphoreType.DMA((count,)),
        ],
        compiler_params=pltpu.CompilerParams(collective_id=ident, has_side_effects=True),
        cost_estimate=busy(70),
        name="join_rows_and_sum",
    )(rows, small)
    return joined.reshape(count * size, width), summed


def total_join_kernel(
    count,
    parts,
    grads_ref,
    weights_ref,
    rows_ref,
    own_ref,
    out_ref,
    joined_ref,
    weigh_ref,
    grads,
    weights,
    rows_in,
    part_ref,
    weighed,
    from_left,
    from_right,
    load_sem,
    weigh_sem,
    own_sem,
    send_sem,
    recv_sem,
    join_send,
    join_recv,
):
    me, has_left, has_right = ends(count)
    size = out_ref.shape[0] // parts
    tile = 2 * HEAD
    width = out_ref.shape[1]
    loads = [
        pltpu.make_async_copy(source, target, load_sem.at[index])
        for index, (source, target) in enumerate(
            ((grads_ref, grads), (weights_ref, weights), (rows_ref, rows_in))
        )
    ]
    for load in loads:
        load.start()
    meet_neighbours(count)
    own_copy = pltpu.make_async_copy(own_ref, joined_ref.at[me], own_sem)
    own_copy.start()

    def sum_copy(way, block, part, source, target):
        rows = pl.ds(part * size, size)
        landing = (from_left, from_right)[way]
        return pltpu.make_async_remote_copy(
            src_ref=source.at[block, rows],
            dst_ref=landing.at[block, rows],
            send_sem=send_sem.at[way, block, part],
            recv_sem=recv_sem.at[way, block, part],
            device_id={"shard": target},
            device_id_type=MESH,
        )

    def join_copy(way, block, part, source, target):
        rows = pl.ds(part * size, size)
        return pltpu.make_async_remote_copy(
            src_ref=source.at[rows] if source is own_ref else source.at[block, rows],
            dst_ref=joined_ref.at[block, rows],
            send_sem=join_send.at[way, block, part],
            recv_sem=join_recv.at[block, part],
            device_id={"shard": target},
            device_id_type=MESH,
        )

    def sum_way(way, block):
        if way == 0:
            return me < block, has_left, me + 1
        return me > block, has_right, me - 1

    def join_way(far, way):
        if way == 0:
            return me >= far, has_right, me - far, me + 1
        return me + far < count, has_left, me + far, me - 1

    def join_start(far, way, part):
        present, onward, block, target = join_way(far, way)
        if far:

            @pl.when(present)
            def _():
                join_copy(way, block, part, joined_ref, target).wait_recv()

        @pl.when(present & onward)
        def _():
            join_copy(way, block, part, joined_ref if far else own_ref, target).start()

    def sum_start(way, block, part):
        sends, receives, target = sum_way(way, block)
        landing = (from_left, from_right)[way]
        rows = pl.ds(part * size, size)

        @pl.when(sends & receives)
        def _():
            sum_copy(way, block, part, landing, target).wait_recv()
            landing[block, rows, :] = (
                landing[block, rows, :].astype(jnp.float32)
                + part_ref[block, rows, :].astype(jnp.float32)
            ).astype(jnp.bfloat16)
            sum_copy(way, block, part, landing, target).start()

    for part in range(parts):
        for way in range(2):
            join_start(0, way, part)
    loads[0].wait()
    loads[1].wait()

    def block_turn(turn, carry):
        block = jnp.int32(0)
        for place in range(count):
            by_distance = sorted(range(count), key=lambda other: -abs(other - place))
            for index, other in enumerate(by_distance):
                block = jnp.where((me == place) & (turn == index), other, block)

        def tile_turn(index, inner_carry):
            across = pl.ds(pl.multiple_of(index * tile, tile), tile)
            part_ref[block, :, across] = low(
                product(grads[block], weights[across, :], ((1,), (1,)))
            )
            return inner_carry

        lax.fori_loop(0, width // tile, tile_turn, 0)

        @pl.when((block > me) & jnp.logical_not(has_left))
        def _():
            for part in range(parts):
                sum_copy(0, block, part, part_ref, me + 1).start()

        @pl.when((block < me) & jnp.logical_not(has_right))
        def _():
            for part in range(parts):
                sum_copy(1, block, part, part_ref, me - 1).start()

        return carry

    lax.fori_loop(0, count, block_turn, 0)
    loads[2].wait()
    wide = weights.shape[1]
    rows_total = count * out_ref.shape[0]

    def weigh_store(turn):
        rows = pl.ds(pl.multiple_of(turn * tile, tile), tile)
        return pltpu.make_async_copy(weighed.at[rows], weigh_ref.at[rows], weigh_sem.at[turn])

    def weigh_turn(turn, carry):
        rows = pl.ds(pl.multiple_of(turn * tile, tile), tile)
        turned = rows_in[:, rows].T

        def weigh_tile(first, span):
            against = grads[:, :, pl.ds(first, span)].reshape(rows_total, span)
            weighed[rows, pl.ds(first, span)] = low(product(turned, against))

        def tile_turn(index, inner_carry):
            weigh_tile(pl.multiple_of(index * tile, tile), tile)
            return inner_carry

        lax.fori_loop(0, wide // tile, tile_turn, 0)
        if wide % tile:
            weigh_tile(wide // tile * tile, wide % tile)
        weigh_store(turn).start()
        return carry

    for step in range(count):
        if step == min(2, count - 1):
            lax.fori_loop(0, width // tile, weigh_turn, 0)
        for part in range(parts):
            if step:
                for way in range(2):
                    join_start(step, way, part)
            if step < count - 1:
                sum_start(0, count - 1 - step, part)
                sum_start(1, step, part)

    for block in range(count):

        @pl.when(me == block)
        def _():
            for part in range(parts):
                rows = pl.ds(part * size, size)
                total = part_ref[block, rows, :].astype(jnp.float32)
                if block > 0:
                    sum_copy(0, block, part, from_left, me).wait_recv()
                    total = total + from_left[block, rows, :].astype(jnp.float32)
                if block < count - 1:
                    sum_copy(1, block, part, from_right, me).wait_recv()
                    total = total + from_right[block, rows, :].astype(jnp.float32)
                out_ref[rows, :] = total

    for step in range(count):
        for part in range(parts):
            for way in range(2):
                present, onward, block, target = join_way(step, way)

                @pl.when(present & onward)
                def _():
                    source = joined_ref if step else own_ref
                    join_copy(way, block, part, source, target).wait_send()

            if step < count - 1:
                for way, block in ((0, count - 1 - step), (1, step)):
                    sends, _, target = sum_way(way, block)

                    @pl.when(sends)
                    def _():
                        sum_copy(way, block, part, part_ref, target).wait_send()

    own_copy.wait()

    def weigh_finish(turn, carry):
        weigh_store(turn).wait()
        return carry

    lax.fori_loop(0, width // tile, weigh_finish, 0)


def total_and_join(grads, weights, rows, own, count, ident, parts=4):
    size, width = own.shape
    wide = grads.shape[1]
    total, joined, weighed = pl.pallas_call(
        functools.partial(total_join_kernel, count, parts),
        out_shape=[
            jax.ShapeDtypeStruct((size, width), jnp.float32),
            jax.ShapeDtypeStruct((count, size, width), own.dtype),
            bf16(width, wide),
        ],
        in_specs=[pl.BlockSpec(memory_space=pl.ANY)] * 4,
        out_specs=[pl.BlockSpec(memory_space=pltpu.VMEM)] + [pl.BlockSpec(memory_space=pl.ANY)] * 2,
        scratch_shapes=[
            pltpu.VMEM((count, size, wide), jnp.bfloat16),
            pltpu.VMEM((width, wide), jnp.bfloat16),
            pltpu.VMEM((count * size, width), jnp.bfloat16),
            pltpu.VMEM((count, size, width), jnp.bfloat16),
            pltpu.VMEM((width, wide), jnp.bfloat16),
            pltpu.VMEM((count, size, width), jnp.bfloat16),
            pltpu.VMEM((count, size, width), jnp.bfloat16),
            pltpu.SemaphoreType.DMA((3,)),
            pltpu.SemaphoreType.DMA((width // (2 * HEAD),)),
            pltpu.SemaphoreType.DMA(()),
            pltpu.SemaphoreType.DMA((2, count, parts)),
            pltpu.SemaphoreType.DMA((2, count, parts)),
            pltpu.SemaphoreType.DMA((2, count, parts)),
            pltpu.SemaphoreType.DMA((count, parts)),
        ],
        compiler_params=pltpu.CompilerParams(
            collective_id=ident, has_side_effects=True, vmem_limit_bytes=60 * 1024 * 1024
        ),
        cost_estimate=busy(95),
        name="total_and_join",
    )(grads.reshape(count, size, wide), weights, rows, own)
    return total, joined.reshape(count * size, width), weighed


def feed_kernel(
    count,
    parts,
    own_ref,
    dy_ref,
    gate_up_ref,
    down_ref,
    down_part_out,
    grad_open_out,
    grad_down_out,
    total_ref,
    gate_up,
    down,
    dy,
    rows_all,
    hidden,
    d_both,
    partial,
    landing,
    down_part,
    open_stage,
    down_stage,
    load_sem,
    part_sem,
    open_sem,
    down_sem,
    join_send,
    join_recv,
    sum_send,
    sum_recv,
):
    me, has_left, has_right = ends(count)
    units, width = down.shape
    piece = own_ref.shape[0] // parts
    tile = 2 * HEAD
    loads = [
        pltpu.make_async_copy(gate_up_ref, gate_up, load_sem.at[0]),
        pltpu.make_async_copy(dy_ref, dy, load_sem.at[1]),
        pltpu.make_async_copy(down_ref, down, load_sem.at[2]),
    ]
    for load in loads:
        load.start()
    rows_all[me] = own_ref[...]
    meet_neighbours(count)

    def part_store(block):
        return pltpu.make_async_copy(
            down_part.at[block], down_part_out.at[block], part_sem.at[block]
        )

    def open_store(turn):
        slot = lax.rem(turn, 2)
        rows = pl.ds(pl.multiple_of(turn * tile, tile), tile)
        return pltpu.make_async_copy(
            open_stage.at[slot], grad_open_out.at[rows], open_sem.at[slot]
        )

    def down_store(turn, size):
        slot = lax.rem(turn, 2)
        rows = pl.ds(pl.multiple_of(turn * tile, tile), size)
        return pltpu.make_async_copy(
            down_stage.at[slot, pl.ds(0, size)], grad_down_out.at[rows], down_sem.at[slot]
        )

    def join_copy(way, block, part):
        rows = pl.ds(part * piece, piece)
        return pltpu.make_async_remote_copy(
            src_ref=rows_all.at[block, rows],
            dst_ref=rows_all.at[block, rows],
            send_sem=join_send.at[way, block, part],
            recv_sem=join_recv.at[block, part],
            device_id={"shard": me - 1 if way else me + 1},
            device_id_type=MESH,
        )

    def sum_copy(way, block, part, source):
        rows = pl.ds(part * piece, piece)
        target = me - 1 if way else me + 1
        slot = jnp.where(block == target, count, block) if way else block
        return pltpu.make_async_remote_copy(
            src_ref=source.at[block, rows],
            dst_ref=landing.at[slot, rows],
            send_sem=sum_send.at[way, block, part],
            recv_sem=sum_recv.at[way, block, part],
            device_id={"shard": target},
            device_id_type=MESH,
        )

    def open_tile(block, first, size):
        across = pl.ds(first, size)
        beyond = pl.ds(pl.multiple_of(units + first, HEAD), size)
        rows = rows_all[block]
        gate = jnp.dot(rows, gate_up[:, across], preferred_element_type=jnp.float32)
        up = jnp.dot(rows, gate_up[:, beyond], preferred_element_type=jnp.float32)
        d_hidden = product(dy[block], down[across, :], ((1,), (1,)))
        opened = sigmoid(gate)
        wave = gate * opened
        hidden[block, :, across] = low(wave * up)
        d_both[block, :, across] = low(d_hidden * up * (opened * (1.0 + gate * (1.0 - opened))))
        d_both[block, :, beyond] = low(d_hidden * wave)

    def compute(block):
        def open_turn(turn, carry):
            open_tile(block, pl.multiple_of(turn * tile, tile), tile)
            return carry

        lax.fori_loop(0, units // tile, open_turn, 0)
        if units % tile:
            open_tile(block, units // tile * tile, units % tile)

        def close_turn(turn, carry):
            across = pl.ds(pl.multiple_of(turn * tile, tile), tile)
            partial[block, :, across] = low(
                product(d_both[block], gate_up[across, :], ((1,), (1,)))
            )
            return carry

        def down_turn(turn, carry):
            across = pl.ds(pl.multiple_of(turn * tile, tile), tile)
            down_part[block, :, across] = low(product(hidden[block], down[:, across]))
            return carry

        lax.fori_loop(0, width // tile, close_turn, 0)
        lax.fori_loop(0, width // tile, down_turn, 0)

    def slot_turn(slot, carry):
        far = (slot + 1) // 2
        rightward = lax.rem(slot, 2) == 1

        @pl.when(slot == 0)
        def _():
            for part in range(parts):

                @pl.when(has_right)
                def _():
                    join_copy(0, me, part).start()

                @pl.when(has_left)
                def _():
                    join_copy(1, me, part).start()

            for load in loads:
                load.wait()

        @pl.when(rightward)
        def _():
            for part in range(parts):
                for way, present, onward, block in (
                    (0, me >= far, has_right, me - far),
                    (1, me + far < count, has_left, me + far),
                ):

                    @pl.when(present)
                    def _():
                        join_copy(way, block, part).wait_recv()

                    @pl.when(present & onward)
                    def _():
                        join_copy(way, block, part).start()

        block = jnp.where(rightward, me - far, me + far)

        @pl.when((block >= 0) & (block < count))
        def _():
            compute(block)
            part_store(block).start()

            @pl.when((block > me) & jnp.logical_not(has_left))
            def _():
                for part in range(parts):
                    sum_copy(0, block, part, partial).start()

            @pl.when((block < me) & jnp.logical_not(has_right))
            def _():
                for part in range(parts):
                    sum_copy(1, block, part, partial).start()

        return carry

    lax.fori_loop(0, 2 * count - 1, slot_turn, 0)

    def add_on(way, block, part):
        rows = pl.ds(part * piece, piece)
        sum_copy(way, block, part, landing).wait_recv()
        landing[block, rows, :] = low(
            landing[block, rows, :].astype(jnp.float32)
            + partial[block, rows, :].astype(jnp.float32)
        )
        sum_copy(way, block, part, landing).start()

    rows_total = count * own_ref.shape[0]

    def weigh(left, right, stage, across_count):
        turned = left.reshape(rows_total, left.shape[2]).T

        def turn_of(turn, carry):
            across = pl.ds(pl.multiple_of(turn * tile, tile), tile)
            against = right[:, :, across].reshape(rows_total, tile)
            stage[:, across] = low(product(turned, against))
            return carry

        lax.fori_loop(0, across_count, turn_of, 0)

    open_count = width // tile
    down_count, down_rest = units // tile, units % tile

    def late_turn(turn, carry):
        step, part = 2 + turn // parts, lax.rem(turn, parts)

        @pl.when((step < count) & (me < step) & has_left)
        def _():
            add_on(0, step, part)

        @pl.when((step < count) & (me > count - 1 - step) & has_right)
        def _():
            add_on(1, count - 1 - step, part)

        slot = lax.rem(turn, 2)
        cols = pl.ds(pl.multiple_of(turn * tile, tile), tile)

        @pl.when(turn < open_count)
        def _():
            @pl.when(turn >= 2)
            def _():
                open_store(turn - 2).wait()

            weigh(rows_all[:, :, cols], d_both, open_stage.at[slot], 2 * units // tile)
            open_store(turn).start()

        @pl.when(turn < down_count)
        def _():
            @pl.when(turn >= 2)
            def _():
                down_store(turn - 2, tile).wait()

            weigh(hidden[:, :, cols], dy, down_stage.at[slot], width // tile)
            down_store(turn, tile).start()

        return carry

    late_count = max((count - 2) * parts, open_count)
    lax.fori_loop(0, late_count, late_turn, 0)
    for turn in range(max(0, open_count - 2), open_count):
        open_store(turn).wait()
    for turn in range(max(0, down_count - 2), down_count):
        down_store(turn, tile).wait()
    if down_rest:
        weigh(
            hidden[:, :, down_count * tile :],
            dy,
            down_stage.at[down_count % 2, pl.ds(0, down_rest)],
            width // tile,
        )
        down_store(down_count, down_rest).start()

    for part in range(parts):
        rows = pl.ds(part * piece, piece)
        total_ref[rows, :] = partial[me, rows, :].astype(jnp.float32)

        @pl.when(has_left)
        def _():
            sum_copy(0, me, part, landing).wait_recv()
            total_ref[rows, :] += landing[me, rows, :].astype(jnp.float32)

        @pl.when(has_right)
        def _():
            sum_copy(1, me, part, landing).wait_recv()
            total_ref[rows, :] += landing[count, rows, :].astype(jnp.float32)

    for block in range(count):
        for part in range(parts):

            @pl.when((me >= block) & has_right)
            def _():
                join_copy(0, block, part).wait_send()

            @pl.when((me <= block) & has_left)
            def _():
                join_copy(1, block, part).wait_send()

            @pl.when(me < block)
            def _():
                sum_copy(0, block, part, partial).wait_send()

            @pl.when(me > block)
            def _():
                sum_copy(1, block, part, partial).wait_send()

        part_store(block).wait()

    if down_rest:
        down_store(down_count, down_rest).wait()


def feed_forward(own, dy, gate_up_mat, down_mat, count, ident, parts=4):
    size, width = own.shape
    units = down_mat.shape[0]
    dma = pltpu.SemaphoreType.DMA
    down_part, grad_open, grad_down, total = pl.pallas_call(
        functools.partial(feed_kernel, count, parts),
        out_shape=[
            bf16(count, size, width),
            bf16(width, 2 * units),
            bf16(units, width),
            f32(size, width),
        ],
        in_specs=[pl.BlockSpec(memory_space=pltpu.VMEM)] + [pl.BlockSpec(memory_space=pl.ANY)] * 3,
        out_specs=[pl.BlockSpec(memory_space=pl.ANY)] * 3 + [pl.BlockSpec(memory_space=pltpu.VMEM)],
        scratch_shapes=[
            pltpu.VMEM((width, 2 * units), jnp.bfloat16),
            pltpu.VMEM((units, width), jnp.bfloat16),
            pltpu.VMEM((count, size, width), jnp.bfloat16),
            pltpu.VMEM((count, size, width), jnp.bfloat16),
            pltpu.VMEM((count, size, units), jnp.bfloat16),
            pltpu.VMEM((count, size, 2 * units), jnp.bfloat16),
            pltpu.VMEM((count, size, width), jnp.bfloat16),
            pltpu.VMEM((count + 1, size, width), jnp.bfloat16),
            pltpu.VMEM((count, size, width), jnp.bfloat16),
            pltpu.VMEM((2, 2 * HEAD, 2 * units), jnp.bfloat16),
            pltpu.VMEM((2, 2 * HEAD, width), jnp.bfloat16),
            dma((3,)),
            dma((count,)),
            dma((2,)),
            dma((2,)),
            dma((2, count, parts)),
            dma((count, parts)),
            dma((2, count, parts)),
            dma((2, count, parts)),
        ],
        compiler_params=pltpu.CompilerParams(
            collective_id=ident, has_side_effects=True, vmem_limit_bytes=63 * 1024 * 1024
        ),
        cost_estimate=busy(120),
        name="feed_forward",
    )(own, dy.reshape(count, size, width), gate_up_mat, down_mat)
    return down_part.reshape(count * size, width), grad_open, grad_down, total


def per_device(
    hidden_in,
    out_grad,
    deal,
    lengths,
    qkv_weight,
    qkv_first,
    qkv_second,
    beta_weight,
    beta_first,
    beta_second,
    out_weight,
    out_first,
    out_second,
    gate_up_weight,
    gate_up_first,
    gate_up_second,
    down_weight,
    down_first,
    down_second,
    conv_weight,
    conv_first,
    conv_second,
    gains,
    gains_first,
    gains_second,
):
    row_count, model_width = hidden_in.shape
    heads = beta_weight.shape[1]
    inner = qkv_weight.shape[2]
    units = down_weight.shape[0]
    devices = lax.axis_size("seq")
    layers = lax.axis_size("shard")
    place = lax.axis_index("shard")
    longest = {4: 4096, 16: 8192}[lengths.shape[0]]
    hops = min(devices - 1, -(-longest // row_count))
    share = row_count // devices // layers
    quarter = devices * share
    _, order, sent_place = lax.sort(
        (deal // row_count, jnp.arange(row_count, dtype=jnp.int32), deal % row_count), num_keys=1
    )
    ordered = order.reshape(devices, layers, share)
    own_order = lax.dynamic_index_in_dim(ordered, place, 1, keepdims=False).reshape(quarter)
    by_layer = jnp.swapaxes(ordered, 0, 1).reshape(row_count)
    chosen = one_hot(own_order, row_count)
    sorting = one_hot(by_layer, row_count)

    def exchanged(rows):
        width = rows.shape[-1]
        return lax.all_to_all(
            rows.reshape(devices, share, width), "seq", split_axis=0, concat_axis=0, tiled=True
        ).reshape(quarter, width)

    own_x = exchanged(moved_back(chosen, hidden_in)).astype(jnp.float32)
    got_place = lax.all_to_all(
        sent_place.reshape(devices, layers * share, 1),
        "seq",
        split_axis=0,
        concat_axis=0,
        tiled=True,
    )
    got_place = jnp.swapaxes(got_place.reshape(devices, layers, share), 0, 1).reshape(row_count)
    to_chain = one_hot(got_place, row_count)

    sorted_dy, own_x = lax.optimization_barrier(
        (moved_back(one_hot(order, row_count), out_grad), own_x)
    )
    all_dy = lax.all_to_all(
        sorted_dy.reshape(devices, layers, share, model_width),
        "seq",
        split_axis=0,
        concat_axis=0,
        tiled=True,
    )

    first_place = lax.axis_index("seq") * row_count
    places = first_place + jnp.arange(0, row_count, GROUP, dtype=jnp.int32)
    starts = jnp.cumsum(lengths) - lengths
    keep = jnp.all(starts[None, :] != places[:, None], axis=1).astype(jnp.float32)

    beta_pad = jnp.zeros((beta_weight.shape[0], HEAD - heads), jnp.bfloat16)
    mixer_mat = lax.all_gather(
        jnp.concatenate(
            [low(qkv_weight).reshape(-1, 3 * inner), low(beta_weight), beta_pad], axis=1
        ),
        "seq",
        axis=0,
        tiled=True,
    )
    out_low = low(out_weight)
    out_rows = lax.all_to_all(
        jnp.broadcast_to(out_low[None], (layers,) + out_low.shape),
        "shard",
        split_axis=0,
        concat_axis=0,
        tiled=True,
    ).reshape(layers * inner, out_low.shape[1])
    out_rows, own_x = lax.optimization_barrier((out_rows, own_x))
    out_mat = lax.all_gather(out_rows, "seq", axis=1, tiled=True)
    gate_up_mat = lax.all_gather(
        low(gate_up_weight).reshape(-1, 2 * units), "seq", axis=0, tiled=True
    )
    down_mat = lax.all_gather(low(down_weight), "seq", axis=1, tiled=True)
    gain_in = gains[:model_width]
    gain_ff = gains[model_width : 2 * model_width]
    gain_out = gains[2 * model_width :].reshape(1, HEAD)
    conv_mat = conv_weight.reshape(TAPS, 3 * inner)

    normed_in = join_rows(low(rms_unit(own_x) * gain_in), layers, 0)
    normed_in, all_dy = lax.optimization_barrier((normed_in, all_dy))
    all_dy = jnp.swapaxes(all_dy, 0, 1).reshape(row_count, model_width)
    own_dy = lax.dynamic_slice_in_dim(all_dy, place * quarter, quarter, 0)
    mixed_in = product(normed_in, mixer_mat)
    logits = mixed_in[:, 3 * inner :]
    logits_high = low(logits)
    logits_low = low(logits - logits_high.astype(jnp.float32))
    chain_in = product(
        to_chain,
        jnp.concatenate([low(mixed_in[:, : 3 * inner]), logits_high, logits_low], axis=1),
    )
    projected = low(chain_in[:, : 3 * inner])
    logits = (
        chain_in[:, 3 * inner : 3 * inner + heads]
        + chain_in[:, 3 * inner + HEAD : 3 * inner + HEAD + heads]
    )
    edge_rows = passed_along(projected[row_count - 8 :], "seq", 1).astype(jnp.float32)
    edge_rows = edge_rows * (jnp.arange(8) >= 8 - (TAPS - 1)).astype(jnp.float32)[:, None]
    rule = Rule(keep, heads, row_count)
    conv, solved, square, step, fresh, reach, zero_out, total = rule.maps(
        projected, edge_rows, logits, conv_mat
    )
    incoming = relayed(total, total[:, :, HEAD:], hops, False, 7)
    state, mixed, normed = rule.outputs(incoming, step, fresh, reach, zero_out, gain_out)

    normed = moved_back(to_chain, normed)
    own_normed = swap_blocks(normed.reshape(layers, quarter, inner), layers, 1, True)
    residual = own_x + product(own_normed, out_mat)
    result, grad_gate_up, grad_down, d_normed_ff = feed_forward(
        low(rms_unit(residual) * gain_ff), all_dy, gate_up_mat, down_mat, layers, 2
    )
    red_gate_up = seq_summed(grad_gate_up, 0)
    d_residual, grad_gain_ff = rms_back(residual, gain_ff, d_normed_ff)
    d_residual = own_dy.astype(jnp.float32) + d_residual
    own_mix = low(d_residual)
    all_mix = join_rows(own_mix, layers, 4)
    out_own = lax.dynamic_slice_in_dim(out_mat, place * inner, inner, 0)
    d_normed = low(product(all_mix, out_own, ((1,), (1,))))
    grad_out = low(product(normed, all_mix, ((0,), (0,))))
    d_normed, grad_out, result = lax.optimization_barrier((d_normed, grad_out, result))
    result = lax.psum_scatter(result, "shard", scatter_dimension=0, tiled=True)
    red_down = seq_summed(grad_down, 1)
    red_out = seq_summed(grad_out, 1)
    d_normed = product(to_chain, d_normed)
    d_mixed, d_first_state, grad_gain_out = rule.tail(d_normed, mixed, gain_out, step, reach)
    d_mixed, red_gate_up = lax.optimization_barrier((d_mixed, red_gate_up))
    outgoing = relayed(total, d_first_state, hops, True, 8)
    d_pre, d_tail, d_edge, grad_taps = rule.back(
        outgoing, projected, edge_rows, logits, conv_mat, conv, solved, square, step, reach, state,
        d_mixed,
    )
    d_tail = low(d_tail + passed_along(d_edge, "seq", -1))
    d_pre = lax.dynamic_update_slice(d_pre, d_tail, (row_count - 8, 0))
    d_mixed_in = moved_back(to_chain, d_pre)
    d_mixed_in, result, red_gate_up = lax.optimization_barrier((d_mixed_in, result, red_gate_up))
    result = exchanged(low(residual + result.astype(jnp.float32)))
    red_gate_up = red_gate_up.astype(jnp.float32).reshape(gate_up_weight.shape)
    gate_up_new = adamw(
        gate_up_weight, gate_up_first, gate_up_second, red_gate_up, RATE_WIDE, SHRINK
    )
    result, *gate_up_new = lax.optimization_barrier((result, *gate_up_new))
    d_normed_in, result, grad_mixer = total_and_join(
        d_mixed_in, mixer_mat, normed_in, result, layers, 5
    )
    red_mixer = seq_summed(grad_mixer, 0)
    d_normed_in, red_down, red_out = lax.optimization_barrier((d_normed_in, red_down, red_out))
    d_input, grad_gain_in = rms_back(own_x, gain_in, d_normed_in)
    d_input = exchanged(low(d_residual + d_input))
    shared = -(-gains.shape[0] // (8 * HEAD)) * 8
    small = jnp.concatenate(
        [
            grad_gain_in,
            grad_gain_ff,
            grad_gain_out.reshape(HEAD),
            jnp.zeros((shared * HEAD - gains.shape[0],), jnp.float32),
            grad_taps.reshape(-1),
        ]
    ).reshape(-1, HEAD)
    d_input, small_sum = join_rows_and_sum(d_input, small, shared, layers, 6)
    d_input, red_mixer = lax.optimization_barrier((d_input, red_mixer))


    red_mixer = red_mixer.astype(jnp.float32)
    red_qkv = red_mixer[:, : 3 * inner].reshape(qkv_weight.shape)
    red_beta = red_mixer[:, 3 * inner : 3 * inner + heads]
    red_out = red_out.astype(jnp.float32)
    red_down = red_down.astype(jnp.float32)
    red_conv = small_sum[shared:].reshape(conv_weight.shape)
    red_gains = small_sum[:shared].reshape(-1)[: gains.shape[0]]
    qkv_new = adamw(qkv_weight, qkv_first, qkv_second, red_qkv, RATE_WIDE, SHRINK)
    beta_new = adamw(beta_weight, beta_first, beta_second, red_beta, RATE_WIDE, SHRINK)
    out_new = adamw(out_weight, out_first, out_second, red_out, RATE_WIDE, SHRINK)
    down_new = adamw(down_weight, down_first, down_second, red_down, RATE_DOWN, SHRINK)
    conv_new = adamw(conv_weight, conv_first, conv_second, red_conv, RATE_CONV, 0.0)
    gains_new = adamw(gains, gains_first, gains_second, red_gains, RATE_GAIN, 0.0)
    return (
        moved(sorting, result),
        moved(sorting, d_input),
        *qkv_new,
        *beta_new,
        *out_new,
        *gate_up_new,
        *down_new,
        *conv_new,
        *gains_new,
    )


def solution(mesh):
    return jax.shard_map(
        per_device,
        mesh=mesh,
        in_specs=(
            P("seq", None),
            P("seq", None),
            P("seq"),
            P(),
            P("seq", None, "shard"),
            P("seq", None, "shard"),
            P("seq", None, "shard"),
            P("seq", "shard"),
            P("seq", "shard"),
            P("seq", "shard"),
            P("shard", "seq"),
            P("shard", "seq"),
            P("shard", "seq"),
            P("seq", None, "shard"),
            P("seq", None, "shard"),
            P("seq", None, "shard"),
            P("shard", "seq"),
            P("shard", "seq"),
            P("shard", "seq"),
            P(None, None, "shard"),
            P(None, None, "shard"),
            P(None, None, "shard"),
            P(),
            P(),
            P(),
        ),
        out_specs=(
            P("seq", None),
            P("seq", None),
            P("seq", None, "shard"),
            P("seq", None, "shard"),
            P("seq", None, "shard"),
            P("seq", "shard"),
            P("seq", "shard"),
            P("seq", "shard"),
            P("shard", "seq"),
            P("shard", "seq"),
            P("shard", "seq"),
            P("seq", None, "shard"),
            P("seq", None, "shard"),
            P("seq", None, "shard"),
            P("shard", "seq"),
            P("shard", "seq"),
            P("shard", "seq"),
            P(None, None, "shard"),
            P(None, None, "shard"),
            P(None, None, "shard"),
            P(),
            P(),
            P(),
        ),
        check_vma=False,
    )
```

time: 1730 us -> 950 us (0.55)
  waiting for transfers between devices: 841 us -> 77.3 us
  Pallas kernels: 245 us -> 630 us
  blocking collectives: 210 us -> 9.42 us
  matrix products: 152 us -> 69 us
  local copies, waits for them, and re-layouts: 132 us -> 56.1 us
  starting transfers between devices: 52.2 us -> 26.3 us
    reduce_scatter x8 -> x5, waiting for transfers between devices: 506 us -> 2.64 us  [the longest x1 2.58 us: per_device(): result = lax.psum_scatter(result, 'shard', scatter_dimension=0, tiled=True)]
    pallas_call x4 -> x12, Pallas kernels: 245 us -> 630 us  [the longest x1 167 us: feed_forward(): pl.pallas_call(functools.partial(feed_kernel, count, parts), out_shape=[b...]
    all_gather x6 -> x2, waiting for transfers between devices: 266 us -> 0.02 us  [the longest x1 0.02 us: per_device(): out_mat = lax.all_gather(out_rows, 'seq', axis=1, tiled=True)]
    gather x9 -> x0, local copies, waits for them, and re-layouts: 96.9 us -> none  [the longest x1 11.5 us: per_device(): chain_x = got_x[arranged].astype(jnp.float32)]
    dot_general x14 -> x12, matrix products: 144 us -> 69 us  [product(): lax.dot_general(left, right, (dims, ((), ())), preferred_element_type=jnp...]
    all_to_all x1, blocking collectives: 82.7 us -> 9.42 us  [per_device(): lax.all_to_all(sent_place.reshape(devices, layers * share, 1), 'seq', spl...]
    psum x2 -> x0, blocking collectives: 64.3 us -> none  [the longest x1 41.8 us: per_device(): red_gains = lax.psum(grad_gains, ('seq', 'shard'))]
    all_gather x1 -> x0, blocking collectives: 63.4 us -> none  [per_device(): beta_mat = lax.all_gather(low(beta_weight), 'seq', axis=0, tiled=True)]
  transfers between devices with their start and end apart: 31 -> 16, of which waited for: 23 -> 7; matrix products, arithmetic and copies ran while one was open for 15% -> 14% of each run, Pallas kernels for 8% -> 49%
where the time goes in v2:
time: 950 us; the launch traced here: 942 us
  Pallas kernels  630 us (66%)
  waiting for transfers between devices  77.3 us (8%)
  matrix products  69 us (7%)
  other arithmetic  58.7 us (6%)
  local copies, waits for them, and re-layouts  56.1 us (6%)
  starting transfers between devices  26.3 us (3%)
  between operations  14.9 us (2%)
    pallas_call x1, Pallas kernels, feed_forward(): pl.pallas_call(functools.partial(feed_kernel, count, parts), out_shape=[b...  167 us
    pallas_call x2, Pallas kernels, join_rows(): pl.pallas_call(functools.partial(join_kernel, count, parts), out_shape=ja...  132 us
    pallas_call x1, Pallas kernels, total_and_join(): pl.pallas_call(functools.partial(total_join_kernel, count, parts), out_sh...  127 us
    pallas_call x1, Pallas kernels, join_rows_and_sum(): pl.pallas_call(functools.partial(last_join_kernel, count, parts, shared),...  71.3 us
    dot_general x12, matrix products, product(): lax.dot_general(left, right, (dims, ((), ())), preferred_element_type=jnp...  69 us
    pallas_call x1, Pallas kernels, back(): pl.pallas_call(functools.partial(back_kernel, heads, BACK_BATCH), grid=(c...  44.9 us
    all_to_all x3, waiting for transfers between devices, exchanged(): lax.all_to_all(rows.reshape(devices, share, width), 'seq', split_axis=0,...  35.7 us
    unnamed x126, local copies, waits for them, and re-layouts  34 us
  transfers between devices with their start and end apart: 16, of which 7 were waited for; matrix products, arithmetic and copies ran while one was open for 14% of the time, Pallas kernels for 49%

profile of v2, /device:TPU:0, one launch (start us, length us, event | category | flops | bytes accessed | tf_op | source)
XLA Modules:
  0.0 941.9 jit_solution(6422899809532462856)
XLA Ops:
  7.2 1.9 copy.213
  11.2 4.4 sort.21
  15.8 4.5 convolution_convert_fusion.1
  20.2 5.3 all-to-all-start.2
  25.6 20.0 %all-to-all-done.2 = bf16[8,32,2048]{2,1,0:T(8,128)(2,1)S(1)} async-done(((bf16[8,32,2048]{2,1,0:T(8,128)(2,1)}), bf16[8,32,2048]{2,1,0:T(8,128)(2,1)S(1)}, u32[]{:S(2)}, u32[]{:S(2)}) %all-to-all-start.2) | async-done | bytes 1048608 | tf_op jit(solution)/shard_map/all_to_all | solution.py:1750
  46.7 4.6 all-to-all-start.1
  51.3 8.3 fusion.7
  59.6 1.6 bitcast_convert_fusion
  61.2 13.4 %all-to-all-done.1 = bf16[4,512,256]{2,1,0:T(8,128)(2,1)} async-done(((bf16[4,512,256]{2,1,0:T(8,128)(2,1)}), bf16[4,512,256]{2,1,0:T(8,128)(2,1)}, u32[]{:S(2)}, u32[]{:S(2)}) %all-to-all-start.1) | async-done | bytes 1048608 | tf_op jit(solution)/shard_map/all_to_all | solution.py:1791
  75.7 2.8 convert_element_type.124
  79.8 9.4 all_to_all.30
  89.3 4.7 all-to-all-start.3
  97.2 71.1 %join_rows.2 = bf16[4,256,2048]{2,1,0:T(8,128)(2,1)} custom-call(bf16[256,2048]{1,0:T(8,128)(2,1)} %multiply_convert_fusion.1.own_ref), custom_call_target="tpu_custom_call" | custom-call | flops 700000000 | tf_op jit(solution)/shard_map/join_rows/pallas_call | solution.py:795
  168.3 4.8 copy.216
  173.1 11.5 %fusion.62 = f32[1024,1664]{1,0:T(8,128)S(1)} fusion(bf16[1024,2048]{1,0:T(8,128)(2,1)} %bitcast.65, bf16[2048,1664]{1,0:T(8,128)(2,1)} %all-gather.5.cloned.1.call-done.weights_ref), kind=kOutput, calls=%fused_computation.122 | convolution fusion | flops 6979321856 | bytes 17825792 | tf_op jit(solution)/shard_map/dot_general | solution.py:690
  185.0 4.1 fusion.61
  189.1 1.8 collective-permute-start
  191.0 1.9 slice.67.pre_ref
  193.1 32.4 %delta_maps.1 = (f32[1024,1536]{1,0:T(8,128)}, f32[16,4,64,256]{3,2,1,0:T(8,128)}, f32[16,4,64,128]{3,2,1,0:T(8,128)S(1)}, f32[16,4,128,128]{3,2,1,0:T(8,128)}, ...) custom-call(f32[16]{0:T(128)S(1)} %convert_element_type.107.keep_ref, ...), custom_call_target="tpu_custom_call" | custom-call | flops 350000000 | tf_op jit(solution)/shard_map/delta_maps/pallas_call | solution.py:537
  228.3 5.8 relay.1.incoming_ref
  235.1 8.8 delta_outputs.1
  243.9 2.3 fusion.30
  246.2 13.3 %swap_blocks.1 = bf16[256,2048]{1,0:T(8,128)(2,1)} custom-call(bf16[4,256,512]{2,1,0:T(8,128)(2,1)} %bitcast.79), custom_call_target="tpu_custom_call" | custom-call | flops 230000000 | tf_op jit(solution)/shard_map/swap_blocks/pallas_call | solution.py:860
  259.5 6.2 multiply_reduce_fusion.4
  265.8 1.5 copy-done.14
  268.5 22.0 %all-gather.9.cloned.1.call-done.gate_up_ref = bf16[2048,2816]{1,0:T(8,128)(2,1)} async-done(((bf16[256,2816]{1,0:T(8,128)(2,1)}), bf16[2048,2816]{1,0:T(8,128)(2,1)}) %all-gather.9.cloned.1.call-update) | async-done | bytes 11534352 | tf_op jit(solution)/shard_map/all_gather | solution.py:1800
  290.5 167.1 %feed_forward.1 = (bf16[4,256,2048]{2,1,0:T(8,128)(2,1)}, bf16[2048,2816]{1,0:T(8,128)(2,1)}, bf16[1408,2048]{1,0:T(8,128)(2,1)}, f32[256,2048]{1,0:T(8,128)}) custom-call(bf16[256,2048]{1,0:T(8,128)(2,1)} %multiply_convert_fusion.own_ref, bf16[4,256,2048]{2,1,0:T(8,128)(2,1)} %bitcast.62, bf16[2048,2816]{1,0:T(8,128)(2,1)} %all-gather.9.cloned.1.call-done.gate_up_ref, ...), custom_call_target="tpu_custom_call" | custom-call | flops 1200000000 | tf_op jit(solution)/shard_map/feed_forward/pallas_call | solution.py:1661
  457.7 1.5 copy-done.15
  459.2 2.3 multiply_reduce_fusion
  461.6 2.9 fusion.48.own_ref
  464.4 60.9 %join_rows.3 = bf16[4,256,2048]{2,1,0:T(8,128)(2,1)} custom-call(bf16[256,2048]{1,0:T(8,128)(2,1)} %fusion.48.own_ref), custom_call_target="tpu_custom_call" | custom-call | flops 700000000 | tf_op jit(solution)/shard_map/join_rows/pallas_call | solution.py:795
  525.4 5.4 fusion.27
  530.8 3.9 convolution_convert_fusion
  537.5 10.1 %delta_tail.1 = (f32[1024,512]{1,0:T(8,128)S(1)}, f32[4,128,128]{2,1,0:T(8,128)S(1)}, f32[1,128]{1,0:T(1,128)S(1)}) custom-call(f32[16]{0:T(128)S(1)} %convert_element_type.107.keep_ref, f32[1024,512]{1,0:T(8,128)S(1)} %fusion.1.d_normed_ref, f32[1024,512]{1,0:T(8,128)} %copy-done.6, f32[1,128]{1,0:T(1,128)S(1)} %slice_bitcast_fusion.gain_ref, ...), custom_call_target="tpu_custom_call" | custom-call | flops 110000000 | tf_op jit(solution)/shard_map/delta_tail/pallas_call | solution.py:604
  549.6 17.1 %relay_back.1.outgoing_ref = f32[4,128,128]{2,1,0:T(8,128)} custom-call(f32[4,128,256]{2,1,0:T(8,128)} %copy-done.2, f32[4,128,128]{2,1,0:T(8,128)} %copy-done.9), custom_call_target="tpu_custom_call" | custom-call | flops 150000000 | tf_op jit(solution)/shard_map/relay_back/pallas_call | solution.py:949
  566.7 1.6 copy-done.4
  569.2 44.9 %delta_back.1 = (bf16[1024,1664]{1,0:T(8,128)(2,1)}, f32[8,1536]{1,0:T(8,128)S(1)}, f32[8,1536]{1,0:T(8,128)S(1)}, f32[4,1536]{1,0:T(4,128)S(1)}) custom-call(f32[16]{0:T(128)S(1)} %convert_element_type.107.keep_ref, f32[4,128,128]{2,1,0:T(8,128)S(1)} %copy-done.7, bf16[1024,1536]{1,0:T(8,128)(2,1)} %slice.67.pre_ref, ...), custom_call_target="tpu_custom_call" | custom-call | flops 450000000 | tf_op jit(solution)/shard_map/delta_back/pallas_call | solution.py:629
  615.5 1.9 collective-permute-done.1
  618.0 7.4 fusion.10
  625.4 2.6 reduce-scatter.8.cloned.1.call-done
  627.9 4.3 reshape.240
  632.3 2.5 add_convert_fusion.1
  634.8 3.6 all-to-all-start.4
  638.5 13.1 %multiply_subtract_fusion = (f32[256,2,1408]{2,1,0:T(2,128)}, f32[256,2,1408]{2,1,0:T(2,128)}, f32[256,2,1408]{2,1,0:T(2,128)}) fusion(f32[256,2,1408]{2,1,0:T(2,128)} %param.38, f32[256,2,1408]{2,1,0:T(2,128)} %reshape.240, f32[256,2,1408]{2,1,0:T(2,128)} %param.39, f32[256,2,1408]{2,1,0:T(2,128)} %param.40), kind=kLoop, calls=%fused_computation.23 | loop fusion | flops 10813440 | bytes 20185088 | tf_op jit(solution)/shard_map/sub | solution.py:498
  651.6 2.3 all-to-all-done.4
  654.8 127.5 %total_and_join.1 = (f32[256,2048]{1,0:T(8,128)}, bf16[4,256,2048]{2,1,0:T(8,128)(2,1)}, bf16[2048,1664]{1,0:T(8,128)(2,1)}) custom-call(bf16[4,256,1664]{2,1,0:T(8,128)(2,1)} %bitcast.77, bf16[2048,1664]{1,0:T(8,128)(2,1)} %all-gather.5.cloned.1.call-done.weights_ref, bf16[1024,2048]{1,0:T(8,128)(2,1)} %bitcast.66, bf16[256,2048]{1,0:T(8,128)(2,1)} %bitcast.76), custom_call_target="tpu_custom_call" | custom-call | flops 950000000 | tf_op jit(solution)/shard_map/total_and_join/pallas_call | solution.py:1329
  784.7 1.6 copy.218
  786.4 3.5 copy.220
  790.0 2.8 multiply_reduce_fusion.1
  793.8 4.2 add_convert_fusion
  798.0 4.6 all-to-all-start.5
  802.7 2.9 multiply_subtract_fusion.3
  805.6 4.3 multiply_subtract_fusion.2
  809.9 6.0 fusion.8
  815.9 13.4 %all-to-all-done.5 = bf16[8,32,2048]{2,1,0:T(8,128)(2,1)} async-done(((bf16[8,32,2048]{2,1,0:T(8,128)(2,1)}), bf16[8,32,2048]{2,1,0:T(8,128)(2,1)}, u32[]{:S(2)}, u32[]{:S(2)}) %all-to-all-start.5) | async-done | bytes 1048608 | tf_op jit(solution)/shard_map/all_to_all | solution.py:1750
  829.3 71.3 %join_rows_and_sum.1 = (bf16[4,256,2048]{2,1,0:T(8,128)(2,1)}, f32[88,128]{1,0:T(8,128)}) custom-call(bf16[256,2048]{1,0:T(8,128)(2,1)} %bitcast.25.own_ref, f32[88,128]{1,0:T(8,128)} %bitcast.83), custom_call_target="tpu_custom_call" | custom-call | flops 700000000 | tf_op jit(solution)/shard_map/join_rows_and_sum/pallas_call | solution.py:1089
  903.3 1.4 multiply_subtract_fusion.4
  910.8 1.6 copy.238
  912.4 1.6 copy.219
  914.0 5.2 multiply_subtract_fusion.1
  919.2 3.1 copy.235
  922.4 1.6 copy.236
  924.0 1.6 copy.237
  925.6 8.2 fusion.9
  (205 shorter events, 36.8 us)
Async XLA Ops:
  7.2 165.9 %all-gather.5.cloned.1.call-start = ((), (), s32[]{:S(2)}) async-start(), calls=%async_computation.11 | async-start | bytes 7667712 | tf_op jit(solution)/shard_map/all_gather | solution.py:1782
  9.1 2.0 copy-start.20
  9.2 1.9 copy-start.47
  20.2 5.3 copy-start.29
  20.2 25.3 %all-to-all-start.2 = ((bf16[8,32,2048]{2,1,0:T(8,128)(2,1)}), bf16[8,32,2048]{2,1,0:T(8,128)(2,1)S(1)}, u32[]{:S(2)}, u32[]{:S(2)}) async-start(bf16[8,32,2048]{2,1,0:T(8,128)(2,1)} %bitcast.7), calls=%async_computation.2 | async-start | bytes 2097152 | tf_op jit(solution)/shard_map/all_to_all | solution.py:1750
  45.6 5.7 copy-start.27
  46.7 28.0 %all-to-all-start.1 = ((bf16[4,512,256]{2,1,0:T(8,128)(2,1)}), bf16[4,512,256]{2,1,0:T(8,128)(2,1)}, u32[]{:S(2)}, u32[]{:S(2)}) async-start(bf16[4,512,256]{2,1,0:T(8,128)(2,1)} %broadcast_in_dim.6), calls=%async_computation.1 | async-start | bytes 2097152 | tf_op jit(solution)/shard_map/all_to_all | solution.py:1791
  51.3 208.3 %all-gather.7.cloned.1.call-start = ((), (), s32[]{:S(2)}) async-start(), calls=%async_computation.12 | async-start | bytes 9437184 | tf_op jit(solution)/shard_map/all_gather | solution.py:1799
  59.6 15.1 %copy-start.24 = (f32[1408,256]{1,0:T(8,128)S(1)}, f32[1408,256]{1,0:T(8,128)}, u32[]{:S(2)}) copy-start(f32[1408,256]{1,0:T(8,128)} %param.41) | copy-start | bytes 4325380
  61.2 34.7 %copy-start.11 = (f32[256,2048]{1,0:T(8,128)}, f32[256,2048]{1,0:T(8,128)S(1)}, u32[]{:S(2)}) copy-start(f32[256,2048]{1,0:T(8,128)S(1)} %bitcast_convert_fusion) | copy-start | bytes 6291460
  74.7 193.8 %all-gather.11.cloned.1.call-start = ((), (), s32[]{:S(2)}) async-start(), calls=%async_computation.14 | async-start | bytes 6488064 | tf_op jit(solution)/shard_map/all_gather | solution.py:1803
  75.7 214.8 %all-gather.9.cloned.1.call-start = ((), (), s32[]{:S(2)}) async-start(), calls=%async_computation.13 | async-start | bytes 12976128 | tf_op jit(solution)/shard_map/all_gather | solution.py:1800
  78.5 1.3 copy-start.50
  89.3 4.8 copy-start.53
  89.3 5.1 copy-start.40
  89.3 79.0 %all-to-all-start.3 = ((bf16[8,4,32,2048]{3,2,1,0:T(8,128)(2,1)}), bf16[8,4,32,2048]{3,2,1,0:T(8,128)(2,1)}, u32[]{:S(2)}, u32[]{:S(2)}) async-start(bf16[8,4,32,2048]{3,2,1,0:T(8,128)(2,1)} %bitcast.74), calls=%async_computation.3 | async-start | bytes 8388608 | tf_op jit(solution)/shard_map/all_to_all | solution.py:1768
  94.0 472.7 %reduce-scatter.6.cloned.1.call-start = ((), (), s32[]{:S(2)}) async-start(), calls=%async_computation.15 | async-start | bytes 12976128 | tf_op jit(solution)/shard_map/reduce_scatter | solution.py:702
  189.1 3.9 collective-permute-start
  191.0 2.0 copy-start.10
  225.4 1.3 copy-start.3
  226.7 17.2 %copy-start = (f32[1024,512]{1,0:T(8,128)}, f32[1024,512]{1,0:T(8,128)S(1)}, u32[]{:S(2)}) copy-start(f32[1024,512]{1,0:T(8,128)S(1)} %get-tuple-element.85.reach_ref) | copy-start | bytes 6291460
  234.1 1.0 copy-start.8
  243.9 2.3 copy-start.6
  246.2 13.4 %copy-start.12 = (f32[256,2048]{1,0:T(8,128)S(1)}, f32[256,2048]{1,0:T(8,128)}, u32[]{:S(2)}) copy-start(f32[256,2048]{1,0:T(8,128)} %copy-done.11) | copy-start | bytes 6291460
  265.8 1.5 copy-start.14
  457.7 1.6 copy-start.15
  457.7 170.3 %reduce-scatter.8.cloned.1.call-start = ((), (), s32[]{:S(2)}) async-start(), calls=%async_computation.16 | async-start | bytes 5242880 | tf_op jit(solution)/shard_map/reduce_scatter | solution.py:1850
  459.2 2.3 copy-start.18
  525.4 5.4 copy-start.26
  525.4 5.4 copy-start.33
  534.7 255.3 %reduce-scatter.12.cloned.1.call-start = ((), (), s32[]{:S(2)}) async-start(), calls=%async_computation.18 | async-start | bytes 2359296 | tf_op jit(solution)/shard_map/reduce_scatter | solution.py:702
  535.4 254.6 %reduce-scatter.10.cloned.1.call-start = ((), (), s32[]{:S(2)}) async-start(), calls=%async_computation.17 | async-start | bytes 6488064 | tf_op jit(solution)/shard_map/reduce_scatter | solution.py:702
  537.4 29.2 %copy-start.1 = (f32[1024,512]{1,0:T(8,128)S(1)}, f32[1024,512]{1,0:T(8,128)}, u32[]{:S(2)}) copy-start(f32[1024,512]{1,0:T(8,128)} %copy-done) | copy-start | bytes 6291460
  547.5 1.3 copy-start.5
  566.7 1.6 copy-start.4
  568.3 0.9 copy-start.7
  614.2 3.2 collective-permute-start.1
  625.4 6.9 copy-start.16
  634.8 19.0 %all-to-all-start.4 = ((bf16[8,32,2048]{2,1,0:T(8,128)(2,1)}), bf16[8,32,2048]{2,1,0:T(8,128)(2,1)S(1)}, u32[]{:S(2)}, u32[]{:S(2)}) async-start(bf16[8,32,2048]{2,1,0:T(8,128)(2,1)} %bitcast.75), calls=%async_computation.6 | async-start | bytes 2097152 | tf_op jit(solution)/shard_map/all_to_all | solution.py:1750
  638.4 266.3 %reduce-scatter.14.cloned.1.call-start = ((), (), s32[]{:S(2)}) async-start(), calls=%async_computation.19 | async-start | bytes 7667712 | tf_op jit(solution)/shard_map/reduce_scatter | solution.py:702
  653.9 1.0 copy-start.28
  782.3 1.6 copy-start.49
  782.3 2.4 copy-start.31
  786.4 3.7 copy-start.13
  790.0 2.9 copy-start.17
  790.0 3.7 copy-start.19
  798.0 4.7 copy-start.30
  798.0 4.7 copy-start.39
  798.0 7.6 copy-start.34
  798.0 31.3 %all-to-all-start.5 = ((bf16[8,32,2048]{2,1,0:T(8,128)(2,1)}), bf16[8,32,2048]{2,1,0:T(8,128)(2,1)}, u32[]{:S(2)}, u32[]{:S(2)}) async-start(bf16[8,32,2048]{2,1,0:T(8,128)(2,1)} %bitcast.72), calls=%async_computation.9 | async-start | bytes 2097152 | tf_op jit(solution)/shard_map/all_to_all | solution.py:1750
  802.6 3.0 copy-start.25
  802.6 3.0 copy-start.32
  802.7 7.2 copy-start.51
  805.6 4.3 copy-start.52
  815.9 85.5 %copy-start.43 = (f32[4,3,512]{2,0,1:T(4,128)S(1)}, f32[4,3,512]{2,0,1:T(4,128)}, u32[]{:S(2)}) copy-start(f32[4,3,512]{2,0,1:T(4,128)} %param.45) | copy-start | bytes 73732
  815.9 85.5 %copy-start.44 = (f32[4,3,512]{2,0,1:T(4,128)S(1)}, f32[4,3,512]{2,0,1:T(4,128)}, u32[]{:S(2)}) copy-start(f32[4,3,512]{2,0,1:T(4,128)} %param.46) | copy-start | bytes 73732
  815.9 87.5 %copy-start.45 = (f32[4224]{0:T(1024)S(1)}, f32[4224]{0:T(1024)}, u32[]{:S(2)}) copy-start(f32[4224]{0:T(1024)} %param.48) | copy-start | bytes 50692
  815.9 87.5 %copy-start.46 = (f32[4224]{0:T(1024)S(1)}, f32[4224]{0:T(1024)}, u32[]{:S(2)}) copy-start(f32[4224]{0:T(1024)} %param.49) | copy-start | bytes 50692
  904.7 1.4 copy-start.22
  906.1 1.0 copy-start.36
  907.9 6.1 copy-start.21
  919.2 3.1 copy-start.23
  925.6 8.2 copy-start.38
  925.6 8.9 copy-start.37
  (6 other events, 4.6 us)
Sparse Core Ops, SparseCore 0:
  11.2 61.1 all-gather.4
  74.8 92.3 all-gather.6
  169.6 45.7 all-gather.10
  217.7 72.7 all-gather.8
  457.8 91.1 reduce-scatter.5
  551.1 76.7 reduce-scatter.7
  631.6 41.7 reduce-scatter.11
  676.8 59.0 reduce-scatter.9
  782.5 71.0 reduce-scatter.13

commit v3 on v2

--- a/solution.py
+++ b/solution.py
@@ -46,6 +46,19 @@
 
 def mul_nt(left, right):
     return mul(left, right, ((1,), (1,)))
+
+
+def quick(left, right, dims=((1,), (0,))):
+    return lax.dot_general(
+        left.astype(jnp.bfloat16),
+        right.astype(jnp.bfloat16),
+        (dims, ((), ())),
+        preferred_element_type=jnp.float32,
+    )
+
+
+def quick_nt(left, right):
+    return quick(left, right, ((1,), (1,)))
 
 
 def grid_indices(size):
@@ -383,42 +396,42 @@
     key_scales = [unit_scale(act) for act in acts]
     keys = [act * size for act, size in zip(acts, key_scales)]
     fresh = [
-        solved[index][:, HEAD:] - mul(solved[index][:, 0:HEAD], states[index])
+        solved[index][:, HEAD:] - quick(solved[index][:, 0:HEAD], states[index])
         for index in indices
     ]
     d_fresh = [
-        mul(scores[index].T, d_out[index]) + mul(keys[index], d_states[index])
+        quick(scores[index].T, d_out[index]) + quick(keys[index], d_states[index])
         for index in indices
     ]
     d_scores = [
-        jnp.where(rows >= cols, mul_nt(d_out[index], fresh[index]), 0.0) for index in indices
+        jnp.where(rows >= cols, quick_nt(d_out[index], fresh[index]), 0.0) for index in indices
     ]
     d_solved = [
-        jnp.concatenate([-mul_nt(d_fresh[index], states[index]), d_fresh[index]], axis=1)
+        jnp.concatenate([-quick_nt(d_fresh[index], states[index]), d_fresh[index]], axis=1)
         for index in indices
     ]
     d_right = [
-        mul(square_ref[item, head, :, 0:GROUP].T, d_solved[index])
+        quick(square_ref[item, head, :, 0:GROUP].T, d_solved[index])
         for index, (item, head) in enumerate(pairs)
     ]
     d_queries = [
-        mul_nt(d_out[index], states[index]) + mul(d_scores[index], keys[index])
+        quick_nt(d_out[index], states[index]) + quick(d_scores[index], keys[index])
         for index in indices
     ]
     acts = [act_of(item, head) for item, head in pairs]
     query_scales = [unit_scale(act) for act in acts]
     queries = [act * size for act, size in zip(acts, query_scales)]
     d_keys = [
-        mul(d_scores[index].T, queries[index]) + mul_nt(fresh[index], d_states[index])
+        quick(d_scores[index].T, queries[index]) + quick_nt(fresh[index], d_states[index])
         for index in indices
     ]
     d_strict = [
-        jnp.where(rows > cols, -mul_nt(d_right[index], solved[index]), 0.0) for index in indices
+        jnp.where(rows > cols, -quick_nt(d_right[index], solved[index]), 0.0) for index in indices
     ]
     strengths = [
         sigmoid(logit_ref[spot(item), head : head + 1]) for item, head in pairs
     ]
-    overlaps = [mul_nt(key, key) for key in keys]
+    overlaps = [quick_nt(key, key) for key in keys]
     both = [
         strengths[index] * d_strict[index] + (strengths[index] * d_strict[index]).T
         for index in indices
@@ -426,7 +439,7 @@
     d_keys = [
         d_keys[index]
         + strengths[index] * d_right[index][:, 0:HEAD]
-        + mul(both[index], keys[index])
+        + quick(both[index], keys[index])
         for index in indices
     ]
     d_logits = []
@@ -1107,6 +1120,117 @@
         name="join_rows_and_sum",
     )(rows, small)
     return joined.reshape(count * size, width), summed
+
+
+def start_kernel(
+    x_ref,
+    place_ref,
+    out_ref,
+    x_got,
+    place_got,
+    out_got,
+    own_sem,
+    x_send,
+    x_recv,
+    place_send,
+    place_recv,
+    out_send,
+    out_recv,
+):
+    count, me = lax.axis_size("shard"), lax.axis_index("shard")
+    devices, here = lax.axis_size("seq"), lax.axis_index("seq")
+    barrier = pltpu.get_barrier_semaphore()
+
+    def greet(hop, carry):
+        other = lax.rem(here + hop, devices)
+        pl.semaphore_signal(barrier, inc=1, device_id={"seq": other}, device_id_type=MESH)
+        return carry
+
+    lax.fori_loop(1, devices, greet, 0)
+    for hop in range(1, count):
+        other = lax.rem(me + hop, count)
+        pl.semaphore_signal(barrier, inc=1, device_id={"shard": other}, device_id_type=MESH)
+    own_copies = [
+        pltpu.make_async_copy(x_ref.at[here], x_got.at[here], own_sem.at[0]),
+        pltpu.make_async_copy(place_ref.at[here], place_got.at[here], own_sem.at[1]),
+        pltpu.make_async_copy(out_ref, out_got.at[me], own_sem.at[2]),
+    ]
+    for copy in own_copies:
+        copy.start()
+    pl.semaphore_wait(barrier, devices + count - 2)
+
+    def seq_copies(hop):
+        other = lax.rem(here + hop, devices)
+        return [
+            pltpu.make_async_remote_copy(
+                src_ref=source.at[other],
+                dst_ref=target.at[here],
+                send_sem=send.at[hop],
+                recv_sem=recv.at[hop],
+                device_id={"seq": other},
+                device_id_type=MESH,
+            )
+            for source, target, send, recv in (
+                (x_ref, x_got, x_send, x_recv),
+                (place_ref, place_got, place_send, place_recv),
+            )
+        ]
+
+    def out_copy(hop):
+        return pltpu.make_async_remote_copy(
+            src_ref=out_ref,
+            dst_ref=out_got.at[me],
+            send_sem=out_send.at[hop],
+            recv_sem=out_recv.at[hop],
+            device_id={"shard": lax.rem(me + hop, count)},
+            device_id_type=MESH,
+        )
+
+    def start(hop, carry):
+        for copy in seq_copies(hop):
+            copy.start()
+        return carry
+
+    def finish(hop, carry):
+        for copy in seq_copies(hop):
+            copy.wait()
+        return carry
+
+    lax.fori_loop(1, devices, start, 0)
+    for hop in range(1, count):
+        out_copy(hop).start()
+    lax.fori_loop(1, devices, finish, 0)
+    for hop in range(1, count):
+        out_copy(hop).wait()
+    for copy in own_copies:
+        copy.wait()
+
+
+def start_exchange(rows, places, out_low, layers, ident):
+    devices = rows.shape[0]
+    dma = pltpu.SemaphoreType.DMA
+    return pl.pallas_call(
+        start_kernel,
+        out_shape=[
+            jax.ShapeDtypeStruct(rows.shape, rows.dtype),
+            jax.ShapeDtypeStruct(places.shape, places.dtype),
+            jax.ShapeDtypeStruct((layers,) + out_low.shape, out_low.dtype),
+        ],
+        in_specs=[pl.BlockSpec(memory_space=pl.ANY)] * 3,
+        out_specs=[pl.BlockSpec(memory_space=pl.ANY)] * 3,
+        scratch_shapes=[
+            dma((3,)),
+            dma((devices,)),
+            dma((devices,)),
+            dma((devices,)),
+            dma((devices,)),
+            dma((layers,)),
+            dma((layers,)),
+        ],
+        compiler_params=pltpu.CompilerParams(collective_id=ident, has_side_effects=True),
+        cost_estimate=busy(20),
+        name="start_exchange",
+    )(rows, places, out_low)
 
 
 def total_join_kernel(
@@ -1555,13 +1679,15 @@
     def weigh(left, right, stage, across_count):
         turned = left.reshape(rows_total, left.shape[2]).T
 
+        span = across_count * tile // 2
+
         def turn_of(turn, carry):
-            across = pl.ds(pl.multiple_of(turn * tile, tile), tile)
-            against = right[:, :, across].reshape(rows_total, tile)
+            across = pl.ds(pl.multiple_of(turn * span, HEAD), span)
+            against = right[:, :, across].reshape(rows_total, span)
             stage[:, across] = low(product(turned, against))
             return carry
 
-        lax.fori_loop(0, across_count, turn_of, 0)
+        lax.fori_loop(0, 2, turn_of, 0)
 
     open_count = width // tile
     down_count, down_rest = units // tile, units % tile
@@ -1751,22 +1877,20 @@
             rows.reshape(devices, share, width), "seq", split_axis=0, concat_axis=0, tiled=True
         ).reshape(quarter, width)
 
-    own_x = exchanged(moved_back(chosen, hidden_in)).astype(jnp.float32)
-    got_place = lax.all_to_all(
-        sent_place.reshape(devices, layers * share, 1),
-        "seq",
-        split_axis=0,
-        concat_axis=0,
-        tiled=True,
+    plane = (share, model_width) if share % 16 == 0 else (share * model_width // HEAD, HEAD)
+    chosen_x = moved_back(chosen, hidden_in).reshape((devices,) + plane)
+    sent_place = sent_place.reshape(devices, 1, layers * share)
+    sent_place = jnp.pad(sent_place, ((0, 0), (0, 0), (0, -(layers * share) % HEAD)))
+    own_x, got_place, out_rows = start_exchange(
+        chosen_x, sent_place, low(out_weight), layers, 9
     )
-    got_place = jnp.swapaxes(got_place.reshape(devices, layers, share), 0, 1).reshape(row_count)
-    to_chain = one_hot(got_place, row_count)
-
-    sorted_dy, own_x = lax.optimization_barrier(
-        (moved_back(one_hot(order, row_count), out_grad), own_x)
-    )
+    own_x = own_x.reshape(quarter, model_width).astype(jnp.float32)
+    out_rows = out_rows.reshape(layers * inner, out_weight.shape[1])
+    got_place = got_place[:, 0, : layers * share]
     all_dy = lax.all_to_all(
-        sorted_dy.reshape(devices, layers, share, model_width),
+        moved_back(one_hot(order, row_count), out_grad).reshape(
+            devices, layers, share, model_width
+        ),
         "seq",
         split_axis=0,
         concat_axis=0,
@@ -1787,15 +1911,6 @@
         axis=0,
         tiled=True,
     )
-    out_low = low(out_weight)
-    out_rows = lax.all_to_all(
-        jnp.broadcast_to(out_low[None], (layers,) + out_low.shape),
-        "shard",
-        split_axis=0,
-        concat_axis=0,
-        tiled=True,
-    ).reshape(layers * inner, out_low.shape[1])
-    out_rows, own_x = lax.optimization_barrier((out_rows, own_x))
     out_mat = lax.all_gather(out_rows, "seq", axis=1, tiled=True)
     gate_up_mat = lax.all_gather(
         low(gate_up_weight).reshape(-1, 2 * units), "seq", axis=0, tiled=True
@@ -1808,6 +1923,8 @@
 
     normed_in = join_rows(low(rms_unit(own_x) * gain_in), layers, 0)
     normed_in, all_dy = lax.optimization_barrier((normed_in, all_dy))
+    got_place = jnp.swapaxes(got_place.reshape(devices, layers, share), 0, 1).reshape(row_count)
+    to_chain = one_hot(got_place, row_count)
     all_dy = jnp.swapaxes(all_dy, 0, 1).reshape(row_count, model_width)
     own_dy = lax.dynamic_slice_in_dim(all_dy, place * quarter, quarter, 0)
     mixed_in = product(normed_in, mixer_mat)
@@ -1838,21 +1955,19 @@
     result, grad_gate_up, grad_down, d_normed_ff = feed_forward(
         low(rms_unit(residual) * gain_ff), all_dy, gate_up_mat, down_mat, layers, 2
     )
-    red_gate_up = seq_summed(grad_gate_up, 0)
+    red_down = seq_summed(grad_down, 1)
     d_residual, grad_gain_ff = rms_back(residual, gain_ff, d_normed_ff)
     d_residual = own_dy.astype(jnp.float32) + d_residual
     own_mix = low(d_residual)
     all_mix = join_rows(own_mix, layers, 4)
     out_own = lax.dynamic_slice_in_dim(out_mat, place * inner, inner, 0)
     d_normed = low(product(all_mix, out_own, ((1,), (1,))))
-    grad_out = low(product(normed, all_mix, ((0,), (0,))))
-    d_normed, grad_out, result = lax.optimization_barrier((d_normed, grad_out, result))
+    d_normed, grad_gate_up, result = lax.optimization_barrier((d_normed, grad_gate_up, result))
     result = lax.psum_scatter(result, "shard", scatter_dimension=0, tiled=True)
-    red_down = seq_summed(grad_down, 1)
-    red_out = seq_summed(grad_out, 1)
+    red_gate_up = seq_summed(grad_gate_up, 0)
     d_normed = product(to_chain, d_normed)
     d_mixed, d_first_state, grad_gain_out = rule.tail(d_normed, mixed, gain_out, step, reach)
-    d_mixed, red_gate_up = lax.optimization_barrier((d_mixed, red_gate_up))
+    d_mixed, red_down = lax.optimization_barrier((d_mixed, red_down))
     outgoing = relayed(total, d_first_state, hops, True, 8)
     d_pre, d_tail, d_edge, grad_taps = rule.back(
         outgoing, projected, edge_rows, logits, conv_mat, conv, solved, square, step, reach, state,
@@ -1860,21 +1975,31 @@
     )
     d_tail = low(d_tail + passed_along(d_edge, "seq", -1))
     d_pre = lax.dynamic_update_slice(d_pre, d_tail, (row_count - 8, 0))
+    d_pre, all_mix = lax.optimization_barrier((d_pre, all_mix))
     d_mixed_in = moved_back(to_chain, d_pre)
-    d_mixed_in, result, red_gate_up = lax.optimization_barrier((d_mixed_in, result, red_gate_up))
+    grad_out = low(product(normed, all_mix, ((0,), (0,))))
+    red_out = seq_summed(grad_out, 1)
+    d_mixed_in, result = lax.optimization_barrier((d_mixed_in, result))
     result = exchanged(low(residual + result.astype(jnp.float32)))
+    red_down = red_down.astype(jnp.float32)
+    down_new = adamw(down_weight, down_first, down_second, red_down, RATE_DOWN, SHRINK)
+    result, *down_new = lax.optimization_barrier((result, *down_new))
+    d_normed_in, result, grad_mixer = total_and_join(
+        d_mixed_in, mixer_mat, normed_in, result, layers, 5
+    )
+    d_normed_in, red_gate_up, red_out = lax.optimization_barrier(
+        (d_normed_in, red_gate_up, red_out)
+    )
+    d_input, grad_gain_in = rms_back(own_x, gain_in, d_normed_in)
+    d_input = exchanged(low(d_residual + d_input))
     red_gate_up = red_gate_up.astype(jnp.float32).reshape(gate_up_weight.shape)
     gate_up_new = adamw(
         gate_up_weight, gate_up_first, gate_up_second, red_gate_up, RATE_WIDE, SHRINK
     )
-    result, *gate_up_new = lax.optimization_barrier((result, *gate_up_new))
-    d_normed_in, result, grad_mixer = total_and_join(
-        d_mixed_in, mixer_mat, normed_in, result, layers, 5
+    d_input, grad_mixer, *gate_up_new = lax.optimization_barrier(
+        (d_input, grad_mixer, *gate_up_new)
     )
     red_mixer = seq_summed(grad_mixer, 0)
-    d_normed_in, red_down, red_out = lax.optimization_barrier((d_normed_in, red_down, red_out))
-    d_input, grad_gain_in = rms_back(own_x, gain_in, d_normed_in)
-    d_input = exchanged(low(d_residual + d_input))
     shared = -(-gains.shape[0] // (8 * HEAD)) * 8
     small = jnp.concatenate(
         [
@@ -1893,13 +2018,11 @@
     red_qkv = red_mixer[:, : 3 * inner].reshape(qkv_weight.shape)
     red_beta = red_mixer[:, 3 * inner : 3 * inner + heads]
     red_out = red_out.astype(jnp.float32)
-    red_down = red_down.astype(jnp.float32)
     red_conv = small_sum[shared:].reshape(conv_weight.shape)
     red_gains = small_sum[:shared].reshape(-1)[: gains.shape[0]]
     qkv_new = adamw(qkv_weight, qkv_first, qkv_second, red_qkv, RATE_WIDE, SHRINK)
     beta_new = adamw(beta_weight, beta_first, beta_second, red_beta, RATE_WIDE, SHRINK)
     out_new = adamw(out_weight, out_first, out_second, red_out, RATE_WIDE, SHRINK)
-    down_new = adamw(down_weight, down_first, down_second, red_down, RATE_DOWN, SHRINK)
     conv_new = adamw(conv_weight, conv_first, conv_second, red_conv, RATE_CONV, 0.0)
     gains_new = adamw(gains, gains_first, gains_second, red_gains, RATE_GAIN, 0.0)
     return (

time: 950 us -> 913 us (0.961)
  waiting for transfers between devices: 77.3 us -> 41.8 us
  Pallas kernels: 630 us -> 651 us
    pallas_call x0 -> x1, Pallas kernels: none -> 25.6 us  [start_exchange(): pl.pallas_call(start_kernel, out_shape=[jax.ShapeDtypeStruct(rows.shape,...]
    all_to_all x3 -> x2, waiting for transfers between devices: 35.7 us -> 12.7 us  [exchanged(): lax.all_to_all(rows.reshape(devices, share, width), 'seq', split_axis=0,...]
    all_to_all x2 -> x1, waiting for transfers between devices: 13.4 us -> 0.01 us  [per_device(): lax.all_to_all(moved_back(one_hot(order, row_count), out_grad).reshape(de...]
    pallas_call x1, Pallas kernels: 44.9 us -> 31.9 us  [back(): pl.pallas_call(functools.partial(back_kernel, heads, BACK_BATCH), grid=(c...]
    unnamed x126 -> x114, local copies, waits for them, and re-layouts: 34 us -> 31.4 us
  transfers between devices with their start and end apart: 16 -> 14, of which waited for: 7 -> 4; matrix products, arithmetic and copies ran while one was open for 14% -> 14% of each run, Pallas kernels for 49% -> 54%
where the time goes in v3:
time: 913 us; the launch traced here: 905 us
  Pallas kernels  651 us (71%)
  matrix products  72.6 us (8%)
  other arithmetic  57.2 us (6%)
  local copies, waits for them, and re-layouts  51.2 us (6%)
  waiting for transfers between devices  41.8 us (5%)
  starting transfers between devices  17.3 us (2%)
  between operations  14.8 us (2%)
    pallas_call x1, Pallas kernels, feed_forward(): pl.pallas_call(functools.partial(feed_kernel, count, parts), out_shape=[b...  162 us
    pallas_call x2, Pallas kernels, join_rows(): pl.pallas_call(functools.partial(join_kernel, count, parts), out_shape=ja...  136 us
    pallas_call x1, Pallas kernels, total_and_join(): pl.pallas_call(functools.partial(total_join_kernel, count, parts), out_sh...  133 us
    dot_general x12, matrix products, product(): lax.dot_general(left, right, (dims, ((), ())), preferred_element_type=jnp...  72.6 us
    pallas_call x1, Pallas kernels, join_rows_and_sum(): pl.pallas_call(functools.partial(last_join_kernel, count, parts, shared),...  72.1 us
    pallas_call x1, Pallas kernels, maps(): pl.pallas_call(functools.partial(maps_kernel, heads, MAPS_BATCH), grid=(c...  32.3 us
    pallas_call x1, Pallas kernels, back(): pl.pallas_call(functools.partial(back_kernel, heads, BACK_BATCH), grid=(c...  31.9 us
    unnamed x114, local copies, waits for them, and re-layouts  31.4 us
  transfers between devices with their start and end apart: 14, of which 4 were waited for; matrix products, arithmetic and copies ran while one was open for 14% of the time, Pallas kernels for 54%

profile of v3, /device:TPU:0, one launch (start us, length us, event | category | flops | bytes accessed | tf_op | source)
XLA Modules:
  0.0 905.4 jit_solution(7222944708050440800)
XLA Ops:
  7.2 1.9 copy.210
  11.2 4.4 sort.21
  16.6 4.5 convolution_convert_fusion.1
  21.0 25.6 %start_exchange.1 = (bf16[8,32,2048]{2,1,0:T(8,128)(2,1)}, s32[8,1,128]{2,1,0:T(1,128)}, bf16[4,512,256]{2,1,0:T(8,128)(2,1)}) custom-call(bf16[8,32,2048]{2,1,0:T(8,128)(2,1)} %bitcast.86, s32[8,1,128]{2,1,0:T(1,128)} %bitcast.92, bf16[512,256]{1,0:T(8,128)(2,1)} %convert_element_type.111.out_ref), custom_call_target="tpu_custom_call" | custom-call | flops 200000000 | tf_op jit(solution)/shard_map/start_exchange/pallas_call | solution.py:1212
  46.7 2.4 convert_element_type.129
  50.2 1.3 copy.241
  51.5 8.4 fusion.7
  59.9 4.7 all-to-all-start
  66.7 1.3 multiply_convert_fusion.1.own_ref
  68.0 76.0 %join_rows.2 = bf16[4,256,2048]{2,1,0:T(8,128)(2,1)} custom-call(bf16[256,2048]{1,0:T(8,128)(2,1)} %multiply_convert_fusion.1.own_ref), custom_call_target="tpu_custom_call" | custom-call | flops 700000000 | tf_op jit(solution)/shard_map/join_rows/pallas_call | solution.py:808
  144.0 4.8 copy.213
  148.8 11.5 %fusion.62 = f32[1024,1664]{1,0:T(8,128)S(1)} fusion(bf16[1024,2048]{1,0:T(8,128)(2,1)} %bitcast.73, bf16[2048,1664]{1,0:T(8,128)(2,1)} %all-gather.5.cloned.1.call-done.weights_ref), kind=kOutput, calls=%fused_computation.123 | convolution fusion | flops 6979321856 | bytes 17825792 | tf_op jit(solution)/shard_map/dot_general | solution.py:703
  160.8 4.1 fusion.61
  164.9 1.9 collective-permute-start
  166.9 1.9 slice.67.pre_ref
  168.9 32.3 %delta_maps.1 = (f32[1024,1536]{1,0:T(8,128)}, f32[16,4,64,256]{3,2,1,0:T(8,128)}, f32[16,4,64,128]{3,2,1,0:T(8,128)S(1)}, f32[16,4,128,128]{3,2,1,0:T(8,128)}, ...) custom-call(f32[16]{0:T(128)S(1)} %convert_element_type.112.keep_ref, ...), custom_call_target="tpu_custom_call" | custom-call | flops 350000000 | tf_op jit(solution)/shard_map/delta_maps/pallas_call | solution.py:550
  201.2 1.5 copy-done.3
  204.3 5.7 relay.1.incoming_ref
  210.9 8.9 delta_outputs.1
  219.8 2.3 fusion.30
  222.1 21.5 %swap_blocks.1 = bf16[256,2048]{1,0:T(8,128)(2,1)} custom-call(bf16[4,256,512]{2,1,0:T(8,128)(2,1)} %bitcast.88), custom_call_target="tpu_custom_call" | custom-call | flops 230000000 | tf_op jit(solution)/shard_map/swap_blocks/pallas_call | solution.py:873
  243.6 6.9 multiply_reduce_fusion.4
  250.5 1.3 copy-done.11
  253.0 25.4 %all-gather.9.cloned.1.call-done.gate_up_ref = bf16[2048,2816]{1,0:T(8,128)(2,1)} async-done(((bf16[256,2816]{1,0:T(8,128)(2,1)}), bf16[2048,2816]{1,0:T(8,128)(2,1)}) %all-gather.9.cloned.1.call-update) | async-done | bytes 11534352 | tf_op jit(solution)/shard_map/all_gather | solution.py:1915
  278.4 162.5 %feed_forward.1 = (bf16[4,256,2048]{2,1,0:T(8,128)(2,1)}, bf16[2048,2816]{1,0:T(8,128)(2,1)}, bf16[1408,2048]{1,0:T(8,128)(2,1)}, f32[256,2048]{1,0:T(8,128)}) custom-call(bf16[256,2048]{1,0:T(8,128)(2,1)} %multiply_convert_fusion.own_ref, bf16[4,256,2048]{2,1,0:T(8,128)(2,1)} %bitcast.69, bf16[2048,2816]{1,0:T(8,128)(2,1)} %all-gather.9.cloned.1.call-done.gate_up_ref, ...), custom_call_target="tpu_custom_call" | custom-call | flops 1200000000 | tf_op jit(solution)/shard_map/feed_forward/pallas_call | solution.py:1787
  441.0 1.5 copy-done.12
  442.5 2.7 multiply_reduce_fusion
  445.2 3.0 fusion.48.own_ref
  448.3 59.7 %join_rows.3 = bf16[4,256,2048]{2,1,0:T(8,128)(2,1)} custom-call(bf16[256,2048]{1,0:T(8,128)(2,1)} %fusion.48.own_ref), custom_call_target="tpu_custom_call" | custom-call | flops 700000000 | tf_op jit(solution)/shard_map/join_rows/pallas_call | solution.py:808
  507.9 5.2 fusion.27
  513.3 1.3 fusion.1.d_normed_ref
  514.5 10.1 %delta_tail.1 = (f32[1024,512]{1,0:T(8,128)S(1)}, f32[4,128,128]{2,1,0:T(8,128)S(1)}, f32[1,128]{1,0:T(1,128)S(1)}) custom-call(f32[16]{0:T(128)S(1)} %convert_element_type.112.keep_ref, f32[1024,512]{1,0:T(8,128)S(1)} %fusion.1.d_normed_ref, f32[1024,512]{1,0:T(8,128)} %copy-done.6, f32[1,128]{1,0:T(1,128)S(1)} %slice_bitcast_fusion.gain_ref, ...), custom_call_target="tpu_custom_call" | custom-call | flops 110000000 | tf_op jit(solution)/shard_map/delta_tail/pallas_call | solution.py:617
  524.6 1.3 copy-done.5
  526.7 11.6 %relay_back.1.outgoing_ref = f32[4,128,128]{2,1,0:T(8,128)} custom-call(f32[4,128,256]{2,1,0:T(8,128)} %copy-done.2, f32[4,128,128]{2,1,0:T(8,128)} %copy-done.9), custom_call_target="tpu_custom_call" | custom-call | flops 150000000 | tf_op jit(solution)/shard_map/relay_back/pallas_call | solution.py:962
  538.3 1.6 copy-done.4
  540.8 31.9 %delta_back.1 = (bf16[1024,1664]{1,0:T(8,128)(2,1)}, f32[8,1536]{1,0:T(8,128)S(1)}, f32[8,1536]{1,0:T(8,128)S(1)}, f32[4,1536]{1,0:T(4,128)S(1)}) custom-call(f32[16]{0:T(128)S(1)} %convert_element_type.112.keep_ref, f32[4,128,128]{2,1,0:T(8,128)S(1)} %copy-done.7, bf16[1024,1536]{1,0:T(8,128)(2,1)} %slice.67.pre_ref, ...), custom_call_target="tpu_custom_call" | custom-call | flops 450000000 | tf_op jit(solution)/shard_map/delta_back/pallas_call | solution.py:642
  572.7 1.5 collective-permute-start.1
  574.2 2.8 collective-permute-done.1
  577.6 3.7 convolution_convert_fusion
  582.1 7.6 fusion.10
  589.7 2.5 add_convert_fusion.1
  592.2 5.0 all-to-all-start.1
  597.2 5.1 multiply_subtract_fusion.2
  602.3 10.4 %all-to-all-done.1 = bf16[8,32,2048]{2,1,0:T(8,128)(2,1)} async-done(((bf16[8,32,2048]{2,1,0:T(8,128)(2,1)}), bf16[8,32,2048]{2,1,0:T(8,128)(2,1)}, u32[]{:S(2)}, u32[]{:S(2)}) %all-to-all-start.1) | async-done | bytes 1048608 | tf_op jit(solution)/shard_map/all_to_all | solution.py:1876
  612.7 132.8 %total_and_join.1 = (f32[256,2048]{1,0:T(8,128)}, bf16[4,256,2048]{2,1,0:T(8,128)(2,1)}, bf16[2048,1664]{1,0:T(8,128)(2,1)}) custom-call(bf16[4,256,1664]{2,1,0:T(8,128)(2,1)} %bitcast.84, bf16[2048,1664]{1,0:T(8,128)(2,1)} %all-gather.5.cloned.1.call-done.weights_ref, bf16[1024,2048]{1,0:T(8,128)(2,1)} %bitcast.74, bf16[256,2048]{1,0:T(8,128)(2,1)} %bitcast.21.own_ref), custom_call_target="tpu_custom_call" | custom-call | flops 950000000 | tf_op jit(solution)/shard_map/total_and_join/pallas_call | solution.py:1453
  745.6 2.5 multiply_reduce_fusion.1
  748.1 4.3 reshape.244
  752.5 5.0 add_convert_fusion
  757.5 3.6 all-to-all-start.2
  761.3 12.8 %multiply_subtract_fusion = (f32[256,2,1408]{2,1,0:T(2,128)}, f32[256,2,1408]{2,1,0:T(2,128)}, f32[256,2,1408]{2,1,0:T(2,128)}) fusion(f32[256,2,1408]{2,1,0:T(2,128)} %param.38, f32[256,2,1408]{2,1,0:T(2,128)} %reshape.244, f32[256,2,1408]{2,1,0:T(2,128)} %param.39, f32[256,2,1408]{2,1,0:T(2,128)} %param.40), kind=kLoop, calls=%fused_computation.23 | loop fusion | flops 10813440 | bytes 20185088 | tf_op jit(solution)/shard_map/sub | solution.py:511
  774.1 2.2 all-to-all-done.2
  778.8 1.6 copy.215
  780.4 3.2 copy.217
  783.8 9.0 fusion.8
  792.9 1.4 multiply_subtract_fusion.3
  794.3 72.1 %join_rows_and_sum.1 = (bf16[4,256,2048]{2,1,0:T(8,128)(2,1)}, f32[88,128]{1,0:T(8,128)}) custom-call(bf16[256,2048]{1,0:T(8,128)(2,1)} %bitcast.89, f32[88,128]{1,0:T(8,128)} %bitcast.93), custom_call_target="tpu_custom_call" | custom-call | flops 700000000 | tf_op jit(solution)/shard_map/join_rows_and_sum/pallas_call | solution.py:1102
  869.2 1.4 multiply_subtract_fusion.4
  870.5 1.3 convert_element_type.141
  875.9 1.6 copy.216
  877.5 5.2 multiply_subtract_fusion.1
  882.7 3.1 copy.232
  885.9 1.6 copy.233
  887.5 1.6 copy.234
  889.1 8.2 fusion.9
  (188 shorter events, 24.5 us)
Async XLA Ops:
  7.2 141.6 %all-gather.5.cloned.1.call-start = ((), (), s32[]{:S(2)}) async-start(), calls=%async_computation.8 | async-start | bytes 7667712 | tf_op jit(solution)/shard_map/all_gather | solution.py:1906
  9.1 2.0 copy-start.17
  9.1 0.7 copy-start.36
  9.2 1.9 copy-start.42
  9.8 6.0 copy-start.23
  11.1 232.5 %all-gather.7.cloned.1.call-start = ((), (), s32[]{:S(2)}) async-start(), calls=%async_computation.9 | async-start | bytes 9437184 | tf_op jit(solution)/shard_map/all_gather | solution.py:1914
  46.6 2.6 copy-start.19
  46.7 206.4 %all-gather.11.cloned.1.call-start = ((), (), s32[]{:S(2)}) async-start(), calls=%async_computation.11 | async-start | bytes 6488064 | tf_op jit(solution)/shard_map/all_gather | solution.py:1918
  49.2 229.2 %all-gather.9.cloned.1.call-start = ((), (), s32[]{:S(2)}) async-start(), calls=%async_computation.10 | async-start | bytes 12976128 | tf_op jit(solution)/shard_map/all_gather | solution.py:1915
  59.9 4.8 copy-start.15
  59.9 5.7 copy-start.45
  59.9 6.5 copy-start.47
  59.9 6.8 copy-start.34
  59.9 84.1 %all-to-all-start = ((bf16[8,4,32,2048]{3,2,1,0:T(8,128)(2,1)}), bf16[8,4,32,2048]{3,2,1,0:T(8,128)(2,1)}, u32[]{:S(2)}, u32[]{:S(2)}) async-start(bf16[8,4,32,2048]{3,2,1,0:T(8,128)(2,1)} %bitcast.82), calls=%async_computation | async-start | bytes 8388608 | tf_op jit(solution)/shard_map/all_to_all | solution.py:1890
  64.6 473.6 %reduce-scatter.6.cloned.1.call-start = ((), (), s32[]{:S(2)}) async-start(), calls=%async_computation.12 | async-start | bytes 6488064 | tf_op jit(solution)/shard_map/reduce_scatter | solution.py:715
  164.9 3.9 collective-permute-start
  166.9 2.0 copy-start.10
  201.2 1.5 copy-start.3
  202.7 0.8 copy-start.2
  202.7 17.1 %copy-start = (f32[1024,512]{1,0:T(8,128)}, f32[1024,512]{1,0:T(8,128)S(1)}, u32[]{:S(2)}) copy-start(f32[1024,512]{1,0:T(8,128)S(1)} %get-tuple-element.89.reach_ref) | copy-start | bytes 6291460
  209.9 1.0 copy-start.8
  219.8 2.3 copy-start.6
  222.1 21.5 %copy-start.16 = (bf16[8,32,2048]{2,1,0:T(8,128)(2,1)S(1)}, bf16[8,32,2048]{2,1,0:T(8,128)(2,1)}, u32[]{:S(2)}) copy-start(bf16[8,32,2048]{2,1,0:T(8,128)(2,1)} %get-tuple-element.83) | copy-start | bytes 3145732
  250.5 1.3 copy-start.11
  440.9 1.6 copy-start.12
  440.9 148.8 %reduce-scatter.8.cloned.1.call-start = ((), (), s32[]{:S(2)}) async-start(), calls=%async_computation.13 | async-start | bytes 5242880 | tf_op jit(solution)/shard_map/reduce_scatter | solution.py:1966
  442.5 2.8 copy-start.14
  513.2 232.4 %reduce-scatter.12.cloned.1.call-start = ((), (), s32[]{:S(2)}) async-start(), calls=%async_computation.15 | async-start | bytes 2359296 | tf_op jit(solution)/shard_map/reduce_scatter | solution.py:715
  514.5 23.8 %copy-start.1 = (f32[1024,512]{1,0:T(8,128)S(1)}, f32[1024,512]{1,0:T(8,128)}, u32[]{:S(2)}) copy-start(f32[1024,512]{1,0:T(8,128)} %copy-done) | copy-start | bytes 6291460
  524.6 1.3 copy-start.5
  525.9 0.7 copy-start.9
  538.3 1.6 copy-start.4
  539.9 0.9 copy-start.7
  540.8 36.8 %copy-start.22 = (bf16[4,256,2048]{2,1,0:T(8,128)(2,1)S(1)}, bf16[4,256,2048]{2,1,0:T(8,128)(2,1)}, u32[]{:S(2)}) copy-start(bf16[4,256,2048]{2,1,0:T(8,128)(2,1)} %join_rows.3) | copy-start | bytes 12582916
  540.8 36.8 %copy-start.26 = (bf16[1024,512]{1,0:T(8,128)(2,1)S(1)}, bf16[1024,512]{1,0:T(8,128)(2,1)}, u32[]{:S(2)}) copy-start(bf16[1024,512]{1,0:T(8,128)(2,1)} %fusion.30) | copy-start | bytes 3145732
  572.7 4.3 collective-permute-start.1
  581.3 164.3 %reduce-scatter.10.cloned.1.call-start = ((), (), s32[]{:S(2)}) async-start(), calls=%async_computation.14 | async-start | bytes 12976128 | tf_op jit(solution)/shard_map/reduce_scatter | solution.py:715
  582.1 7.6 copy-start.13
  592.2 5.0 copy-start.28
  592.2 20.5 %all-to-all-start.1 = ((bf16[8,32,2048]{2,1,0:T(8,128)(2,1)}), bf16[8,32,2048]{2,1,0:T(8,128)(2,1)}, u32[]{:S(2)}, u32[]{:S(2)}) async-start(bf16[8,32,2048]{2,1,0:T(8,128)(2,1)} %bitcast.83), calls=%async_computation.3 | async-start | bytes 2097152 | tf_op jit(solution)/shard_map/all_to_all | solution.py:1876
  757.5 18.9 %all-to-all-start.2 = ((bf16[8,32,2048]{2,1,0:T(8,128)(2,1)}), bf16[8,32,2048]{2,1,0:T(8,128)(2,1)S(1)}, u32[]{:S(2)}, u32[]{:S(2)}) async-start(bf16[8,32,2048]{2,1,0:T(8,128)(2,1)} %bitcast.80), calls=%async_computation.6 | async-start | bytes 2097152 | tf_op jit(solution)/shard_map/all_to_all | solution.py:1876
  761.0 109.5 %reduce-scatter.14.cloned.1.call-start = ((), (), s32[]{:S(2)}) async-start(), calls=%async_computation.16 | async-start | bytes 7667712 | tf_op jit(solution)/shard_map/reduce_scatter | solution.py:715
  776.4 1.0 copy-start.27
  777.3 0.7 copy-start.43
  777.3 0.8 copy-start.44
  777.3 1.4 copy-start.25
  783.7 9.1 %copy-start.24 = (f32[512,256]{1,0:T(8,128)S(1)}, f32[512,256]{1,0:T(8,128)}, u32[]{:S(2)}) copy-start(f32[512,256]{1,0:T(8,128)} %param.35) | copy-start | bytes 1572868
  783.7 9.1 %copy-start.31 = (f32[512,256]{1,0:T(8,128)S(1)}, f32[512,256]{1,0:T(8,128)}, u32[]{:S(2)}) copy-start(f32[512,256]{1,0:T(8,128)} %param.36) | copy-start | bytes 1572868
  783.7 9.1 %copy-start.32 = (f32[512,256]{1,0:T(8,128)S(1)}, f32[512,256]{1,0:T(8,128)}, u32[]{:S(2)}) copy-start(f32[512,256]{1,0:T(8,128)} %param.37) | copy-start | bytes 1572868
  783.7 9.1 %copy-start.33 = (bf16[512,256]{1,0:T(8,128)(2,1)S(1)}, bf16[512,256]{1,0:T(8,128)(2,1)}, u32[]{:S(2)}) copy-start(bf16[512,256]{1,0:T(8,128)(2,1)} %reduce-scatter.12.cloned.1.call-done) | copy-start | bytes 786436
  792.9 1.4 copy-start.46
  794.3 72.9 %copy-start.38 = (f32[4,3,512]{2,0,1:T(4,128)S(1)}, f32[4,3,512]{2,0,1:T(4,128)}, u32[]{:S(2)}) copy-start(f32[4,3,512]{2,0,1:T(4,128)} %param.45) | copy-start | bytes 73732
  794.3 72.9 %copy-start.39 = (f32[4,3,512]{2,0,1:T(4,128)S(1)}, f32[4,3,512]{2,0,1:T(4,128)}, u32[]{:S(2)}) copy-start(f32[4,3,512]{2,0,1:T(4,128)} %param.46) | copy-start | bytes 73732
  794.3 74.9 %copy-start.35 = (f32[4224]{0:T(1024)S(1)}, f32[4224]{0:T(1024)}, u32[]{:S(2)}) copy-start(f32[4224]{0:T(1024)} %param.47) | copy-start | bytes 50692
  794.3 74.9 %copy-start.40 = (f32[4224]{0:T(1024)S(1)}, f32[4224]{0:T(1024)}, u32[]{:S(2)}) copy-start(f32[4224]{0:T(1024)} %param.48) | copy-start | bytes 50692
  794.3 74.9 %copy-start.41 = (f32[4224]{0:T(1024)S(1)}, f32[4224]{0:T(1024)}, u32[]{:S(2)}) copy-start(f32[4224]{0:T(1024)} %param.49) | copy-start | bytes 50692
  870.5 1.4 copy-start.20
  872.0 3.1 copy-start.37
  873.0 4.6 copy-start.18
  882.7 3.1 copy-start.21
  889.1 8.2 copy-start.30
  889.1 8.9 copy-start.29
Sparse Core Ops, SparseCore 0:
  11.2 65.1 all-gather.4
  78.3 82.8 all-gather.6
  163.7 44.3 all-gather.10
  210.4 67.9 all-gather.8
  441.0 56.3 reduce-scatter.5
  513.3 74.3 reduce-scatter.7
  591.6 41.7 reduce-scatter.11
  637.3 86.8 reduce-scatter.9
  777.5 60.9 reduce-scatter.13

commit v4 on v3

--- a/solution.py
+++ b/solution.py
@@ -1905,7 +1905,7 @@
     beta_pad = jnp.zeros((beta_weight.shape[0], HEAD - heads), jnp.bfloat16)
     mixer_mat = lax.all_gather(
         jnp.concatenate(
-            [low(qkv_weight).reshape(-1, 3 * inner), low(beta_weight), beta_pad], axis=1
+            [low(qkv_weight[:, item]) for item in range(3)] + [low(beta_weight), beta_pad], axis=1
         ),
         "seq",
         axis=0,
@@ -2015,7 +2015,9 @@
 
 
     red_mixer = red_mixer.astype(jnp.float32)
-    red_qkv = red_mixer[:, : 3 * inner].reshape(qkv_weight.shape)
+    red_qkv = jnp.stack(
+        [red_mixer[:, item * inner : (item + 1) * inner] for item in range(3)], axis=1
+    )
     red_beta = red_mixer[:, 3 * inner : 3 * inner + heads]
     red_out = red_out.astype(jnp.float32)
     red_conv = small_sum[shared:].reshape(conv_weight.shape)

time: 913 us -> 894 us (0.979)
  local copies, waits for them, and re-layouts: 51.2 us -> 33 us
    unnamed x114 -> x92, local copies, waits for them, and re-layouts: 31.4 us -> 16.9 us
  transfers between devices with their start and end apart: 14 -> 14, of which waited for: 4 -> 4; matrix products, arithmetic and copies ran while one was open for 14% -> 13% of each run, Pallas kernels for 54% -> 55%
where the time goes in v4:
time: 894 us; the launch traced here: 887 us
  Pallas kernels  650 us (73%)
  matrix products  72.1 us (8%)
  other arithmetic  57.6 us (6%)
  waiting for transfers between devices  41.7 us (5%)
  local copies, waits for them, and re-layouts  33 us (4%)
  starting transfers between devices  17.6 us (2%)
  between operations  14.8 us (2%)
    pallas_call x1, Pallas kernels, feed_forward(): pl.pallas_call(functools.partial(feed_kernel, count, parts), out_shape=[b...  162 us
    pallas_call x2, Pallas kernels, join_rows(): pl.pallas_call(functools.partial(join_kernel, count, parts), out_shape=ja...  135 us
    pallas_call x1, Pallas kernels, total_and_join(): pl.pallas_call(functools.partial(total_join_kernel, count, parts), out_sh...  133 us
    dot_general x12, matrix products, product(): lax.dot_general(left, right, (dims, ((), ())), preferred_element_type=jnp...  72.1 us
    pallas_call x1, Pallas kernels, join_rows_and_sum(): pl.pallas_call(functools.partial(last_join_kernel, count, parts, shared),...  71.9 us
    pallas_call x1, Pallas kernels, maps(): pl.pallas_call(functools.partial(maps_kernel, heads, MAPS_BATCH), grid=(c...  32.3 us
    pallas_call x1, Pallas kernels, back(): pl.pallas_call(functools.partial(back_kernel, heads, BACK_BATCH), grid=(c...  31.8 us
    sub x7, other arithmetic, adamw(): return (weight - rate * (stepped + decay * weight), first, second)  25.8 us
  transfers between devices with their start and end apart: 14, of which 4 were waited for; matrix products, arithmetic and copies ran while one was open for 13% of the time, Pallas kernels for 55%

profile of v4, /device:TPU:0, one launch (start us, length us, event | category | flops | bytes accessed | tf_op | source)
XLA Modules:
  0.0 886.8 jit_solution(11011221315762381027)
XLA Ops:
  7.2 1.5 convert.13
  9.0 1.1 concatenate.9
  10.2 4.4 sort.21
  15.6 4.5 convolution_convert_fusion.1
  20.0 25.6 %start_exchange.1 = (bf16[8,32,2048]{2,1,0:T(8,128)(2,1)}, s32[8,1,128]{2,1,0:T(1,128)}, bf16[4,512,256]{2,1,0:T(8,128)(2,1)}) custom-call(bf16[8,32,2048]{2,1,0:T(8,128)(2,1)} %bitcast.94, s32[8,1,128]{2,1,0:T(1,128)} %bitcast.100, bf16[512,256]{1,0:T(8,128)(2,1)} %convert_element_type.120.out_ref), custom_call_target="tpu_custom_call" | custom-call | flops 200000000 | tf_op jit(solution)/shard_map/start_exchange/pallas_call | solution.py:1212
  45.7 2.4 convert_element_type.140
  48.2 1.0 convert_element_type.139
  49.2 1.3 copy.187
  50.5 8.6 fusion.7
  59.2 4.7 all-to-all-start
  66.0 1.3 multiply_convert_fusion.1.own_ref
  67.2 75.6 %join_rows.2 = bf16[4,256,2048]{2,1,0:T(8,128)(2,1)} custom-call(bf16[256,2048]{1,0:T(8,128)(2,1)} %multiply_convert_fusion.1.own_ref), custom_call_target="tpu_custom_call" | custom-call | flops 700000000 | tf_op jit(solution)/shard_map/join_rows/pallas_call | solution.py:808
  142.9 4.8 copy.167
  147.7 11.5 %fusion.62 = f32[1024,1664]{1,0:T(8,128)S(1)} fusion(bf16[1024,2048]{1,0:T(8,128)(2,1)} %bitcast.83, bf16[2048,1664]{1,0:T(8,128)(2,1)} %all-gather.5.cloned.1.call-done.weights_ref), kind=kOutput, calls=%fused_computation.130 | convolution fusion | flops 6979321856 | bytes 17825792 | tf_op jit(solution)/shard_map/dot_general | solution.py:703
  159.6 4.1 fusion.61
  163.7 2.1 collective-permute-start
  166.0 2.0 slice.93.pre_ref
  168.0 32.3 %delta_maps.1 = (f32[1024,1536]{1,0:T(8,128)}, f32[16,4,64,256]{3,2,1,0:T(8,128)}, f32[16,4,64,128]{3,2,1,0:T(8,128)S(1)}, f32[16,4,128,128]{3,2,1,0:T(8,128)}, ...) custom-call(f32[16]{0:T(128)S(1)} %convert_element_type.121.keep_ref, ...), custom_call_target="tpu_custom_call" | custom-call | flops 350000000 | tf_op jit(solution)/shard_map/delta_maps/pallas_call | solution.py:550
  200.3 1.5 copy-done.3
  203.4 5.6 relay.1.incoming_ref
  209.0 0.9 copy-done.8
  209.9 9.0 %delta_outputs.1 = (f32[16,4,128,128]{3,2,1,0:T(8,128)}, f32[1024,512]{1,0:T(8,128)S(1)}, bf16[1024,512]{1,0:T(8,128)(2,1)S(1)}) custom-call(f32[16]{0:T(128)S(1)} %convert_element_type.121.keep_ref, f32[4,128,128]{2,1,0:T(8,128)S(1)} %copy-done.8, f32[16,4,128,128]{3,2,1,0:T(8,128)} %get-tuple-element.87.step_ref, ...), custom_call_target="tpu_custom_call" | custom-call | flops 90000000 | tf_op jit(solution)/shard_map/delta_outputs/pallas_call | solution.py:591
  218.9 2.3 fusion.30
  221.2 21.5 %swap_blocks.1 = bf16[256,2048]{1,0:T(8,128)(2,1)} custom-call(bf16[4,256,512]{2,1,0:T(8,128)(2,1)} %bitcast.96), custom_call_target="tpu_custom_call" | custom-call | flops 230000000 | tf_op jit(solution)/shard_map/swap_blocks/pallas_call | solution.py:873
  242.8 6.7 multiply_reduce_fusion.4
  249.5 1.3 copy-done.11
  250.8 1.2 multiply_convert_fusion.own_ref
  252.0 25.4 %all-gather.9.cloned.1.call-done.gate_up_ref = bf16[2048,2816]{1,0:T(8,128)(2,1)} async-done(((bf16[256,2816]{1,0:T(8,128)(2,1)}), bf16[2048,2816]{1,0:T(8,128)(2,1)}) %all-gather.9.cloned.1.call-update) | async-done | bytes 11534352 | tf_op jit(solution)/shard_map/all_gather | solution.py:1915
  277.4 162.5 %feed_forward.1 = (bf16[4,256,2048]{2,1,0:T(8,128)(2,1)}, bf16[2048,2816]{1,0:T(8,128)(2,1)}, bf16[1408,2048]{1,0:T(8,128)(2,1)}, f32[256,2048]{1,0:T(8,128)}) custom-call(bf16[256,2048]{1,0:T(8,128)(2,1)} %multiply_convert_fusion.own_ref, bf16[4,256,2048]{2,1,0:T(8,128)(2,1)} %bitcast.79, bf16[2048,2816]{1,0:T(8,128)(2,1)} %all-gather.9.cloned.1.call-done.gate_up_ref, ...), custom_call_target="tpu_custom_call" | custom-call | flops 1200000000 | tf_op jit(solution)/shard_map/feed_forward/pallas_call | solution.py:1787
  440.0 1.5 copy-done.12
  441.5 2.8 multiply_reduce_fusion
  444.2 3.0 fusion.48.own_ref
  447.2 59.7 %join_rows.3 = bf16[4,256,2048]{2,1,0:T(8,128)(2,1)} custom-call(bf16[256,2048]{1,0:T(8,128)(2,1)} %fusion.48.own_ref), custom_call_target="tpu_custom_call" | custom-call | flops 700000000 | tf_op jit(solution)/shard_map/join_rows/pallas_call | solution.py:808
  506.9 5.2 fusion.27
  512.2 1.3 fusion.1.d_normed_ref
  513.5 10.1 %delta_tail.1 = (f32[1024,512]{1,0:T(8,128)S(1)}, f32[4,128,128]{2,1,0:T(8,128)S(1)}, f32[1,128]{1,0:T(1,128)S(1)}) custom-call(f32[16]{0:T(128)S(1)} %convert_element_type.121.keep_ref, f32[1024,512]{1,0:T(8,128)S(1)} %fusion.1.d_normed_ref, f32[1024,512]{1,0:T(8,128)} %copy-done.6, f32[1,128]{1,0:T(1,128)S(1)} %slice_bitcast_fusion.6.gain_ref, ...), custom_call_target="tpu_custom_call" | custom-call | flops 110000000 | tf_op jit(solution)/shard_map/delta_tail/pallas_call | solution.py:617
  523.6 1.3 copy-done.5
  525.6 11.6 %relay_back.1.outgoing_ref = f32[4,128,128]{2,1,0:T(8,128)} custom-call(f32[4,128,256]{2,1,0:T(8,128)} %copy-done.2, f32[4,128,128]{2,1,0:T(8,128)} %copy-done.9), custom_call_target="tpu_custom_call" | custom-call | flops 150000000 | tf_op jit(solution)/shard_map/relay_back/pallas_call | solution.py:962
  537.3 1.6 copy-done.4
  538.9 0.9 copy-done.7
  539.8 31.8 %delta_back.1 = (bf16[1024,1664]{1,0:T(8,128)(2,1)}, f32[8,1536]{1,0:T(8,128)S(1)}, f32[8,1536]{1,0:T(8,128)S(1)}, f32[4,1536]{1,0:T(4,128)S(1)}) custom-call(f32[16]{0:T(128)S(1)} %convert_element_type.121.keep_ref, f32[4,128,128]{2,1,0:T(8,128)S(1)} %copy-done.7, bf16[1024,1536]{1,0:T(8,128)(2,1)} %slice.93.pre_ref, ...), custom_call_target="tpu_custom_call" | custom-call | flops 450000000 | tf_op jit(solution)/shard_map/delta_back/pallas_call | solution.py:642
  571.7 1.5 collective-permute-start.1
  573.1 2.7 collective-permute-done.1
  576.4 3.7 convolution_convert_fusion
  580.9 7.6 fusion.10
  588.5 2.5 add_convert_fusion.1
  591.0 5.1 all-to-all-start.1
  596.2 5.1 multiply_subtract_fusion.2
  601.2 10.4 %all-to-all-done.1 = bf16[8,32,2048]{2,1,0:T(8,128)(2,1)} async-done(((bf16[8,32,2048]{2,1,0:T(8,128)(2,1)}), bf16[8,32,2048]{2,1,0:T(8,128)(2,1)}, u32[]{:S(2)}, u32[]{:S(2)}) %all-to-all-start.1) | async-done | bytes 1048608 | tf_op jit(solution)/shard_map/all_to_all | solution.py:1876
  611.7 132.8 %total_and_join.1 = (f32[256,2048]{1,0:T(8,128)}, bf16[4,256,2048]{2,1,0:T(8,128)(2,1)}, bf16[2048,1664]{1,0:T(8,128)(2,1)}) custom-call(bf16[4,256,1664]{2,1,0:T(8,128)(2,1)} %bitcast.93, bf16[2048,1664]{1,0:T(8,128)(2,1)} %all-gather.5.cloned.1.call-done.weights_ref, bf16[1024,2048]{1,0:T(8,128)(2,1)} %bitcast.84, bf16[256,2048]{1,0:T(8,128)(2,1)} %bitcast.23.own_ref), custom_call_target="tpu_custom_call" | custom-call | flops 950000000 | tf_op jit(solution)/shard_map/total_and_join/pallas_call | solution.py:1453
  744.5 2.5 multiply_reduce_fusion.1
  747.0 4.3 reshape.239
  751.4 5.0 add_convert_fusion
  756.4 3.6 all-to-all-start.2
  760.2 12.8 %multiply_subtract_fusion = (f32[256,2,1408]{2,1,0:T(2,128)}, f32[256,2,1408]{2,1,0:T(2,128)}, f32[256,2,1408]{2,1,0:T(2,128)}) fusion(f32[256,2,1408]{2,1,0:T(2,128)} %param.38, f32[256,2,1408]{2,1,0:T(2,128)} %reshape.239, f32[256,2,1408]{2,1,0:T(2,128)} %param.39, f32[256,2,1408]{2,1,0:T(2,128)} %param.40), kind=kLoop, calls=%fused_computation.23 | loop fusion | flops 10813440 | bytes 20185088 | tf_op jit(solution)/shard_map/sub | solution.py:511
  773.0 2.2 all-to-all-done.2
  775.3 0.9 copy-done.23
  776.8 8.4 fusion.8
  785.3 1.4 multiply_subtract_fusion.3
  786.8 71.9 %join_rows_and_sum.1 = (bf16[4,256,2048]{2,1,0:T(8,128)(2,1)}, f32[88,128]{1,0:T(8,128)}) custom-call(bf16[256,2048]{1,0:T(8,128)(2,1)} %bitcast.97, f32[88,128]{1,0:T(8,128)} %bitcast.101), custom_call_target="tpu_custom_call" | custom-call | flops 700000000 | tf_op jit(solution)/shard_map/join_rows_and_sum/pallas_call | solution.py:1102
  861.4 1.4 multiply_subtract_fusion.4
  862.8 1.3 convert_element_type.152
  865.4 8.3 fusion.9
  875.1 5.0 multiply_subtract_fusion.1
  (165 shorter events, 14.1 us)
Async XLA Ops:
  7.2 1.7 copy-start.29
  7.2 140.5 %all-gather.5.cloned.1.call-start = ((), (), s32[]{:S(2)}) async-start(), calls=%async_computation.8 | async-start | bytes 7667712 | tf_op jit(solution)/shard_map/all_gather | solution.py:1906
  8.8 1.4 copy-start.34
  8.8 6.1 copy-start.20
  10.1 232.6 %all-gather.7.cloned.1.call-start = ((), (), s32[]{:S(2)}) async-start(), calls=%async_computation.9 | async-start | bytes 9437184 | tf_op jit(solution)/shard_map/all_gather | solution.py:1914
  45.6 2.6 copy-start.17
  45.7 206.3 %all-gather.11.cloned.1.call-start = ((), (), s32[]{:S(2)}) async-start(), calls=%async_computation.11 | async-start | bytes 6488064 | tf_op jit(solution)/shard_map/all_gather | solution.py:1918
  48.2 229.2 %all-gather.9.cloned.1.call-start = ((), (), s32[]{:S(2)}) async-start(), calls=%async_computation.10 | async-start | bytes 12976128 | tf_op jit(solution)/shard_map/all_gather | solution.py:1915
  59.1 4.8 copy-start.15
  59.1 5.7 copy-start.37
  59.1 6.5 copy-start.39
  59.2 6.8 copy-start.28
  59.2 83.7 %all-to-all-start = ((bf16[8,4,32,2048]{3,2,1,0:T(8,128)(2,1)}), bf16[8,4,32,2048]{3,2,1,0:T(8,128)(2,1)}, u32[]{:S(2)}, u32[]{:S(2)}) async-start(bf16[8,4,32,2048]{3,2,1,0:T(8,128)(2,1)} %bitcast.91), calls=%async_computation | async-start | bytes 8388608 | tf_op jit(solution)/shard_map/all_to_all | solution.py:1890
  63.9 473.4 %reduce-scatter.6.cloned.1.call-start = ((), (), s32[]{:S(2)}) async-start(), calls=%async_computation.12 | async-start | bytes 6488064 | tf_op jit(solution)/shard_map/reduce_scatter | solution.py:715
  163.7 4.2 collective-permute-start
  165.9 2.1 copy-start.10
  200.3 1.5 copy-start.3
  201.8 0.8 copy-start.2
  201.8 17.1 %copy-start = (f32[1024,512]{1,0:T(8,128)}, f32[1024,512]{1,0:T(8,128)S(1)}, u32[]{:S(2)}) copy-start(f32[1024,512]{1,0:T(8,128)S(1)} %get-tuple-element.89.reach_ref) | copy-start | bytes 6291460
  209.0 1.0 copy-start.8
  218.9 2.3 copy-start.6
  221.2 21.5 %copy-start.16 = (bf16[8,32,2048]{2,1,0:T(8,128)(2,1)S(1)}, bf16[8,32,2048]{2,1,0:T(8,128)(2,1)}, u32[]{:S(2)}) copy-start(bf16[8,32,2048]{2,1,0:T(8,128)(2,1)} %get-tuple-element.83) | copy-start | bytes 3145732
  249.4 1.3 copy-start.11
  439.9 1.6 copy-start.12
  439.9 148.6 %reduce-scatter.8.cloned.1.call-start = ((), (), s32[]{:S(2)}) async-start(), calls=%async_computation.13 | async-start | bytes 5242880 | tf_op jit(solution)/shard_map/reduce_scatter | solution.py:1966
  441.5 2.8 copy-start.14
  512.2 232.3 %reduce-scatter.12.cloned.1.call-start = ((), (), s32[]{:S(2)}) async-start(), calls=%async_computation.15 | async-start | bytes 2359296 | tf_op jit(solution)/shard_map/reduce_scatter | solution.py:715
  513.5 23.8 %copy-start.1 = (f32[1024,512]{1,0:T(8,128)S(1)}, f32[1024,512]{1,0:T(8,128)}, u32[]{:S(2)}) copy-start(f32[1024,512]{1,0:T(8,128)} %copy-done) | copy-start | bytes 6291460
  523.6 1.3 copy-start.5
  524.9 0.7 copy-start.9
  537.3 1.6 copy-start.4
  538.9 0.9 copy-start.7
  539.8 36.6 %copy-start.19 = (bf16[4,256,2048]{2,1,0:T(8,128)(2,1)S(1)}, bf16[4,256,2048]{2,1,0:T(8,128)(2,1)}, u32[]{:S(2)}) copy-start(bf16[4,256,2048]{2,1,0:T(8,128)(2,1)} %join_rows.3) | copy-start | bytes 12582916
  539.8 36.6 %copy-start.22 = (bf16[1024,512]{1,0:T(8,128)(2,1)S(1)}, bf16[1024,512]{1,0:T(8,128)(2,1)}, u32[]{:S(2)}) copy-start(bf16[1024,512]{1,0:T(8,128)(2,1)} %fusion.30) | copy-start | bytes 3145732
  571.7 4.1 collective-permute-start.1
  580.1 164.4 %reduce-scatter.10.cloned.1.call-start = ((), (), s32[]{:S(2)}) async-start(), calls=%async_computation.14 | async-start | bytes 12976128 | tf_op jit(solution)/shard_map/reduce_scatter | solution.py:715
  580.9 7.6 copy-start.13
  591.0 5.1 copy-start.24
  591.0 20.7 %all-to-all-start.1 = ((bf16[8,32,2048]{2,1,0:T(8,128)(2,1)}), bf16[8,32,2048]{2,1,0:T(8,128)(2,1)}, u32[]{:S(2)}, u32[]{:S(2)}) async-start(bf16[8,32,2048]{2,1,0:T(8,128)(2,1)} %bitcast.92), calls=%async_computation.3 | async-start | bytes 2097152 | tf_op jit(solution)/shard_map/all_to_all | solution.py:1876
  756.4 18.9 %all-to-all-start.2 = ((bf16[8,32,2048]{2,1,0:T(8,128)(2,1)}), bf16[8,32,2048]{2,1,0:T(8,128)(2,1)S(1)}, u32[]{:S(2)}, u32[]{:S(2)}) async-start(bf16[8,32,2048]{2,1,0:T(8,128)(2,1)} %bitcast.89), calls=%async_computation.6 | async-start | bytes 2097152 | tf_op jit(solution)/shard_map/all_to_all | solution.py:1876
  759.9 102.9 %reduce-scatter.14.cloned.1.call-start = ((), (), s32[]{:S(2)}) async-start(), calls=%async_computation.16 | async-start | bytes 7667712 | tf_op jit(solution)/shard_map/reduce_scatter | solution.py:715
  775.3 1.0 copy-start.23
  775.3 1.1 copy-start.35
  775.3 1.3 copy-start.36
  776.8 8.5 copy-start.21
  776.8 8.5 copy-start.25
  776.8 8.5 copy-start.26
  776.8 8.5 copy-start.27
  785.3 1.4 copy-start.38
  786.8 72.7 %copy-start.30 = (f32[4,3,512]{2,0,1:T(4,128)S(1)}, f32[4,3,512]{2,0,1:T(4,128)}, u32[]{:S(2)}) copy-start(f32[4,3,512]{2,0,1:T(4,128)} %param.45) | copy-start | bytes 73732
  786.8 72.7 %copy-start.31 = (f32[4,3,512]{2,0,1:T(4,128)S(1)}, f32[4,3,512]{2,0,1:T(4,128)}, u32[]{:S(2)}) copy-start(f32[4,3,512]{2,0,1:T(4,128)} %param.46) | copy-start | bytes 73732
  786.8 74.7 %copy-start.32 = (f32[4224]{0:T(1024)S(1)}, f32[4224]{0:T(1024)}, u32[]{:S(2)}) copy-start(f32[4224]{0:T(1024)} %param.48) | copy-start | bytes 50692
  786.8 74.7 %copy-start.33 = (f32[4224]{0:T(1024)S(1)}, f32[4224]{0:T(1024)}, u32[]{:S(2)}) copy-start(f32[4224]{0:T(1024)} %param.49) | copy-start | bytes 50692
  865.4 9.7 %copy-start.18 = (f32[256,3,512]{2,0,1:T(8,128)S(1)}, f32[256,3,512]{2,0,1:T(8,128)}, u32[]{:S(2)}) copy-start(f32[256,3,512]{2,0,1:T(8,128)} %param.29) | copy-start | bytes 4718596
Sparse Core Ops, SparseCore 0:
  10.5 65.1 all-gather.4
  77.5 82.6 all-gather.6
  162.7 44.3 all-gather.10
  209.4 67.9 all-gather.8
  440.0 56.3 reduce-scatter.5
  512.3 74.3 reduce-scatter.7
  590.6 41.7 reduce-scatter.11
  636.2 86.7 reduce-scatter.9
  775.4 60.5 reduce-scatter.13

commit v5 on v4

--- a/solution.py
+++ b/solution.py
@@ -1960,9 +1960,9 @@
     d_residual = own_dy.astype(jnp.float32) + d_residual
     own_mix = low(d_residual)
     all_mix = join_rows(own_mix, layers, 4)
+    all_mix, grad_gate_up, result = lax.optimization_barrier((all_mix, grad_gate_up, result))
     out_own = lax.dynamic_slice_in_dim(out_mat, place * inner, inner, 0)
     d_normed = low(product(all_mix, out_own, ((1,), (1,))))
-    d_normed, grad_gate_up, result = lax.optimization_barrier((d_normed, grad_gate_up, result))
     result = lax.psum_scatter(result, "shard", scatter_dimension=0, tiled=True)
     red_gate_up = seq_summed(grad_gate_up, 0)
     d_normed = product(to_chain, d_normed)
@@ -1976,10 +1976,10 @@
     d_tail = low(d_tail + passed_along(d_edge, "seq", -1))
     d_pre = lax.dynamic_update_slice(d_pre, d_tail, (row_count - 8, 0))
     d_pre, all_mix = lax.optimization_barrier((d_pre, all_mix))
-    d_mixed_in = moved_back(to_chain, d_pre)
     grad_out = low(product(normed, all_mix, ((0,), (0,))))
     red_out = seq_summed(grad_out, 1)
-    d_mixed_in, result = lax.optimization_barrier((d_mixed_in, result))
+    d_pre, result = lax.optimization_barrier((d_pre, result))
+    d_mixed_in = moved_back(to_chain, d_pre)
     result = exchanged(low(residual + result.astype(jnp.float32)))
     red_down = red_down.astype(jnp.float32)
     down_new = adamw(down_weight, down_first, down_second, red_down, RATE_DOWN, SHRINK)
@@ -1991,7 +1991,8 @@
         (d_normed_in, red_gate_up, red_out)
     )
     d_input, grad_gain_in = rms_back(own_x, gain_in, d_normed_in)
-    d_input = exchanged(low(d_residual + d_input))
+    d_input, red_gate_up = lax.optimization_barrier((low(d_residual + d_input), red_gate_up))
+    d_input = exchanged(d_input)
     red_gate_up = red_gate_up.astype(jnp.float32).reshape(gate_up_weight.shape)
     gate_up_new = adamw(
         gate_up_weight, gate_up_first, gate_up_second, red_gate_up, RATE_WIDE, SHRINK

time: 894 us -> 889 us (level)
    unnamed x92 -> x98, local copies, waits for them, and re-layouts: 16.9 us -> 19.3 us
    dot_general x12 -> x11, matrix products: 72.1 us -> 71.2 us  [product(): lax.dot_general(left, right, (dims, ((), ())), preferred_element_type=jnp...]
where the time goes in v5:
time: 889 us; the launch traced here: 882 us
  Pallas kernels  650 us (73%)
  matrix products  71.2 us (8%)
  other arithmetic  57.5 us (6%)
  waiting for transfers between devices  35.6 us (4%)
  local copies, waits for them, and re-layouts  35.4 us (4%)
  starting transfers between devices  17.7 us (2%)
  between operations  14.9 us (2%)
    pallas_call x1, Pallas kernels, feed_forward(): pl.pallas_call(functools.partial(feed_kernel, count, parts), out_shape=[b...  163 us
    pallas_call x2, Pallas kernels, join_rows(): pl.pallas_call(functools.partial(join_kernel, count, parts), out_shape=ja...  135 us
    pallas_call x1, Pallas kernels, total_and_join(): pl.pallas_call(functools.partial(total_join_kernel, count, parts), out_sh...  132 us
    pallas_call x1, Pallas kernels, join_rows_and_sum(): pl.pallas_call(functools.partial(last_join_kernel, count, parts, shared),...  72 us
    dot_general x11, matrix products, product(): lax.dot_general(left, right, (dims, ((), ())), preferred_element_type=jnp...  71.2 us
    pallas_call x1, Pallas kernels, maps(): pl.pallas_call(functools.partial(maps_kernel, heads, MAPS_BATCH), grid=(c...  32.3 us
    pallas_call x1, Pallas kernels, back(): pl.pallas_call(functools.partial(back_kernel, heads, BACK_BATCH), grid=(c...  31.8 us
    sub x7, other arithmetic, adamw(): return (weight - rate * (stepped + decay * weight), first, second)  26.1 us
  transfers between devices with their start and end apart: 14, of which 4 were waited for; matrix products, arithmetic and copies ran while one was open for 13% of the time, Pallas kernels for 55%

profile of v5, /device:TPU:0, one launch (start us, length us, event | category | flops | bytes accessed | tf_op | source)
XLA Modules:
  0.0 881.9 jit_solution(15952148069556971024)
XLA Ops:
  7.2 1.5 convert.13
  9.0 1.1 concatenate.9
  10.2 4.4 sort.21
  15.6 4.5 convolution_convert_fusion.1
  20.0 25.6 %start_exchange.1 = (bf16[8,32,2048]{2,1,0:T(8,128)(2,1)}, s32[8,1,128]{2,1,0:T(1,128)}, bf16[4,512,256]{2,1,0:T(8,128)(2,1)}) custom-call(bf16[8,32,2048]{2,1,0:T(8,128)(2,1)} %bitcast.92, s32[8,1,128]{2,1,0:T(1,128)} %bitcast.98, bf16[512,256]{1,0:T(8,128)(2,1)} %convert_element_type.120.out_ref), custom_call_target="tpu_custom_call" | custom-call | flops 200000000 | tf_op jit(solution)/shard_map/start_exchange/pallas_call | solution.py:1212
  45.7 2.4 convert_element_type.140
  48.2 1.0 convert_element_type.139
  49.2 1.3 copy.187
  50.5 8.6 fusion.7
  59.2 4.7 all-to-all-start
  66.0 1.3 multiply_convert_fusion.1.own_ref
  67.2 75.6 %join_rows.2 = bf16[4,256,2048]{2,1,0:T(8,128)(2,1)} custom-call(bf16[256,2048]{1,0:T(8,128)(2,1)} %multiply_convert_fusion.1.own_ref), custom_call_target="tpu_custom_call" | custom-call | flops 700000000 | tf_op jit(solution)/shard_map/join_rows/pallas_call | solution.py:808
  142.9 4.8 copy.167
  147.7 11.5 %fusion.65 = f32[1024,1664]{1,0:T(8,128)S(1)} fusion(bf16[1024,2048]{1,0:T(8,128)(2,1)} %bitcast.82, bf16[2048,1664]{1,0:T(8,128)(2,1)} %all-gather.5.cloned.1.call-done.weights_ref), kind=kOutput, calls=%fused_computation.130 | convolution fusion | flops 6979321856 | bytes 17825792 | tf_op jit(solution)/shard_map/dot_general | solution.py:703
  159.6 4.1 fusion.64
  163.8 2.2 collective-permute-start
  166.1 1.9 slice.93.pre_ref
  168.1 32.3 %delta_maps.1 = (f32[1024,1536]{1,0:T(8,128)}, f32[16,4,64,256]{3,2,1,0:T(8,128)}, f32[16,4,64,128]{3,2,1,0:T(8,128)S(1)}, f32[16,4,128,128]{3,2,1,0:T(8,128)}, ...) custom-call(f32[16]{0:T(128)S(1)} %convert_element_type.121.keep_ref, ...), custom_call_target="tpu_custom_call" | custom-call | flops 350000000 | tf_op jit(solution)/shard_map/delta_maps/pallas_call | solution.py:550
  200.4 1.5 copy-done.3
  203.5 5.6 relay.1.incoming_ref
  209.1 0.9 copy-done.9
  210.0 9.1 %delta_outputs.1 = (f32[16,4,128,128]{3,2,1,0:T(8,128)}, f32[1024,512]{1,0:T(8,128)S(1)}, bf16[1024,512]{1,0:T(8,128)(2,1)S(1)}) custom-call(f32[16]{0:T(128)S(1)} %convert_element_type.121.keep_ref, f32[4,128,128]{2,1,0:T(8,128)S(1)} %copy-done.9, f32[16,4,128,128]{3,2,1,0:T(8,128)} %get-tuple-element.89.step_ref, ...), custom_call_target="tpu_custom_call" | custom-call | flops 90000000 | tf_op jit(solution)/shard_map/delta_outputs/pallas_call | solution.py:591
  219.1 2.3 fusion.30
  221.4 21.1 %swap_blocks.1 = bf16[256,2048]{1,0:T(8,128)(2,1)} custom-call(bf16[4,256,512]{2,1,0:T(8,128)(2,1)} %bitcast.94), custom_call_target="tpu_custom_call" | custom-call | flops 230000000 | tf_op jit(solution)/shard_map/swap_blocks/pallas_call | solution.py:873
  242.6 6.7 multiply_reduce_fusion.4
  249.3 1.3 copy-done.12
  250.6 1.2 multiply_convert_fusion.own_ref
  251.8 25.4 %all-gather.9.cloned.1.call-done.gate_up_ref = bf16[2048,2816]{1,0:T(8,128)(2,1)} async-done(((bf16[256,2816]{1,0:T(8,128)(2,1)}), bf16[2048,2816]{1,0:T(8,128)(2,1)}) %all-gather.9.cloned.1.call-update) | async-done | bytes 11534352 | tf_op jit(solution)/shard_map/all_gather | solution.py:1915
  277.2 162.5 %feed_forward.1 = (bf16[4,256,2048]{2,1,0:T(8,128)(2,1)}, bf16[2048,2816]{1,0:T(8,128)(2,1)}, bf16[1408,2048]{1,0:T(8,128)(2,1)}, f32[256,2048]{1,0:T(8,128)}) custom-call(bf16[256,2048]{1,0:T(8,128)(2,1)} %multiply_convert_fusion.own_ref, bf16[4,256,2048]{2,1,0:T(8,128)(2,1)} %bitcast.78, bf16[2048,2816]{1,0:T(8,128)(2,1)} %all-gather.9.cloned.1.call-done.gate_up_ref, ...), custom_call_target="tpu_custom_call" | custom-call | flops 1200000000 | tf_op jit(solution)/shard_map/feed_forward/pallas_call | solution.py:1787
  439.8 1.5 copy-done.13
  441.3 2.8 multiply_reduce_fusion
  444.1 3.0 fusion.51.own_ref
  447.1 59.7 %join_rows.3 = bf16[4,256,2048]{2,1,0:T(8,128)(2,1)} custom-call(bf16[256,2048]{1,0:T(8,128)(2,1)} %fusion.51.own_ref), custom_call_target="tpu_custom_call" | custom-call | flops 700000000 | tf_op jit(solution)/shard_map/join_rows/pallas_call | solution.py:808
  506.9 7.6 fusion.1.d_normed_ref
  514.5 1.6 copy-done.7
  516.1 10.1 %delta_tail.1 = (f32[1024,512]{1,0:T(8,128)S(1)}, f32[4,128,128]{2,1,0:T(8,128)S(1)}, f32[1,128]{1,0:T(1,128)S(1)}) custom-call(f32[16]{0:T(128)S(1)} %convert_element_type.121.keep_ref, f32[1024,512]{1,0:T(8,128)S(1)} %copy-done.7, f32[1024,512]{1,0:T(8,128)} %copy-done.6, f32[1,128]{1,0:T(1,128)S(1)} %slice_bitcast_fusion.6.gain_ref, ...), custom_call_target="tpu_custom_call" | custom-call | flops 110000000 | tf_op jit(solution)/shard_map/delta_tail/pallas_call | solution.py:617
  526.2 1.3 copy-done.5
  528.2 11.9 %relay_back.1.outgoing_ref = f32[4,128,128]{2,1,0:T(8,128)} custom-call(f32[4,128,256]{2,1,0:T(8,128)} %copy-done.2, f32[4,128,128]{2,1,0:T(8,128)} %copy-done.10), custom_call_target="tpu_custom_call" | custom-call | flops 150000000 | tf_op jit(solution)/shard_map/relay_back/pallas_call | solution.py:962
  540.2 1.6 copy-done.4
  541.8 0.9 copy-done.8
  542.7 31.8 %delta_back.1 = (bf16[1024,1664]{1,0:T(8,128)(2,1)}, f32[8,1536]{1,0:T(8,128)S(1)}, f32[8,1536]{1,0:T(8,128)S(1)}, f32[4,1536]{1,0:T(4,128)S(1)}) custom-call(f32[16]{0:T(128)S(1)} %convert_element_type.121.keep_ref, f32[4,128,128]{2,1,0:T(8,128)S(1)} %copy-done.8, bf16[1024,1536]{1,0:T(8,128)(2,1)} %slice.93.pre_ref, ...), custom_call_target="tpu_custom_call" | custom-call | flops 450000000 | tf_op jit(solution)/shard_map/delta_back/pallas_call | solution.py:642
  574.6 1.5 collective-permute-start.1
  576.0 2.4 collective-permute-done.1
  579.0 3.7 convolution_convert_fusion
  584.3 2.5 add_convert_fusion.1
  586.9 5.2 all-to-all-start.1
  592.0 5.4 multiply_subtract_fusion.2
  597.4 5.4 fusion.10
  602.9 4.7 all-to-all-done.1
  607.5 132.4 %total_and_join.1 = (f32[256,2048]{1,0:T(8,128)}, bf16[4,256,2048]{2,1,0:T(8,128)(2,1)}, bf16[2048,1664]{1,0:T(8,128)(2,1)}) custom-call(bf16[4,256,1664]{2,1,0:T(8,128)(2,1)} %bitcast.91, bf16[2048,1664]{1,0:T(8,128)(2,1)} %all-gather.5.cloned.1.call-done.weights_ref, bf16[1024,2048]{1,0:T(8,128)(2,1)} %bitcast.83, bf16[256,2048]{1,0:T(8,128)(2,1)} %bitcast.23.own_ref), custom_call_target="tpu_custom_call" | custom-call | flops 950000000 | tf_op jit(solution)/shard_map/total_and_join/pallas_call | solution.py:1453
  740.0 2.7 multiply_reduce_fusion.1
  742.7 4.4 add_convert_fusion
  747.1 4.3 reshape.239
  751.4 3.6 all-to-all-start.2
  755.2 12.8 %multiply_subtract_fusion = (f32[256,2,1408]{2,1,0:T(2,128)}, f32[256,2,1408]{2,1,0:T(2,128)}, f32[256,2,1408]{2,1,0:T(2,128)}) fusion(f32[256,2,1408]{2,1,0:T(2,128)} %param.38, f32[256,2,1408]{2,1,0:T(2,128)} %reshape.239, f32[256,2,1408]{2,1,0:T(2,128)} %param.39, f32[256,2,1408]{2,1,0:T(2,128)} %param.40), kind=kLoop, calls=%fused_computation.23 | loop fusion | flops 10813440 | bytes 20185088 | tf_op jit(solution)/shard_map/sub | solution.py:511
  768.1 2.2 all-to-all-done.2
  770.3 0.9 copy-done.25
  771.9 8.4 fusion.8
  780.4 1.5 multiply_subtract_fusion.3
  781.9 72.0 %join_rows_and_sum.1 = (bf16[4,256,2048]{2,1,0:T(8,128)(2,1)}, f32[88,128]{1,0:T(8,128)}) custom-call(bf16[256,2048]{1,0:T(8,128)(2,1)} %bitcast.95, f32[88,128]{1,0:T(8,128)} %bitcast.99), custom_call_target="tpu_custom_call" | custom-call | flops 700000000 | tf_op jit(solution)/shard_map/join_rows_and_sum/pallas_call | solution.py:1102
  856.6 1.4 multiply_subtract_fusion.4
  857.9 1.3 convert_element_type.152
  860.5 8.3 fusion.9
  870.2 5.0 multiply_subtract_fusion.1
  (170 shorter events, 14.9 us)
Async XLA Ops:
  7.2 1.7 copy-start.31
  7.2 140.5 %all-gather.5.cloned.1.call-start = ((), (), s32[]{:S(2)}) async-start(), calls=%async_computation.8 | async-start | bytes 7667712 | tf_op jit(solution)/shard_map/all_gather | solution.py:1906
  8.8 1.4 copy-start.36
  8.8 6.1 copy-start.22
  10.1 232.4 %all-gather.7.cloned.1.call-start = ((), (), s32[]{:S(2)}) async-start(), calls=%async_computation.9 | async-start | bytes 9437184 | tf_op jit(solution)/shard_map/all_gather | solution.py:1914
  45.6 2.6 copy-start.19
  45.7 206.2 %all-gather.11.cloned.1.call-start = ((), (), s32[]{:S(2)}) async-start(), calls=%async_computation.11 | async-start | bytes 6488064 | tf_op jit(solution)/shard_map/all_gather | solution.py:1918
  48.2 229.0 %all-gather.9.cloned.1.call-start = ((), (), s32[]{:S(2)}) async-start(), calls=%async_computation.10 | async-start | bytes 12976128 | tf_op jit(solution)/shard_map/all_gather | solution.py:1915
  59.1 4.8 copy-start.17
  59.1 5.7 copy-start.39
  59.2 6.5 copy-start.42
  59.2 6.8 copy-start.30
  59.2 83.8 %all-to-all-start = ((bf16[8,4,32,2048]{3,2,1,0:T(8,128)(2,1)}), bf16[8,4,32,2048]{3,2,1,0:T(8,128)(2,1)}, u32[]{:S(2)}, u32[]{:S(2)}) async-start(bf16[8,4,32,2048]{3,2,1,0:T(8,128)(2,1)} %bitcast.89), calls=%async_computation | async-start | bytes 8388608 | tf_op jit(solution)/shard_map/all_to_all | solution.py:1890
  63.9 476.3 %reduce-scatter.6.cloned.1.call-start = ((), (), s32[]{:S(2)}) async-start(), calls=%async_computation.12 | async-start | bytes 6488064 | tf_op jit(solution)/shard_map/reduce_scatter | solution.py:715
  163.8 4.3 collective-permute-start
  166.1 2.0 copy-start.11
  200.4 1.5 copy-start.3
  201.9 0.8 copy-start.2
  201.9 17.2 %copy-start = (f32[1024,512]{1,0:T(8,128)}, f32[1024,512]{1,0:T(8,128)S(1)}, u32[]{:S(2)}) copy-start(f32[1024,512]{1,0:T(8,128)S(1)} %get-tuple-element.91.reach_ref) | copy-start | bytes 6291460
  209.1 1.0 copy-start.9
  219.1 2.3 copy-start.6
  221.4 21.2 %copy-start.18 = (bf16[8,32,2048]{2,1,0:T(8,128)(2,1)S(1)}, bf16[8,32,2048]{2,1,0:T(8,128)(2,1)}, u32[]{:S(2)}) copy-start(bf16[8,32,2048]{2,1,0:T(8,128)(2,1)} %get-tuple-element.85) | copy-start | bytes 3145732
  249.3 1.3 copy-start.12
  439.7 1.6 copy-start.13
  439.8 143.8 %reduce-scatter.8.cloned.1.call-start = ((), (), s32[]{:S(2)}) async-start(), calls=%async_computation.13 | async-start | bytes 5242880 | tf_op jit(solution)/shard_map/reduce_scatter | solution.py:1966
  441.3 2.8 copy-start.15
  506.8 233.1 %reduce-scatter.12.cloned.1.call-start = ((), (), s32[]{:S(2)}) async-start(), calls=%async_computation.15 | async-start | bytes 2359296 | tf_op jit(solution)/shard_map/reduce_scatter | solution.py:715
  514.5 1.6 copy-start.7
  516.1 24.1 %copy-start.1 = (f32[1024,512]{1,0:T(8,128)S(1)}, f32[1024,512]{1,0:T(8,128)}, u32[]{:S(2)}) copy-start(f32[1024,512]{1,0:T(8,128)} %copy-done) | copy-start | bytes 6291460
  526.2 1.3 copy-start.5
  527.5 0.7 copy-start.10
  540.2 1.6 copy-start.4
  541.8 0.9 copy-start.8
  542.7 36.3 %copy-start.21 = (bf16[4,256,2048]{2,1,0:T(8,128)(2,1)S(1)}, bf16[4,256,2048]{2,1,0:T(8,128)(2,1)}, u32[]{:S(2)}) copy-start(bf16[4,256,2048]{2,1,0:T(8,128)(2,1)} %join_rows.3) | copy-start | bytes 12582916
  542.7 36.3 %copy-start.24 = (bf16[1024,512]{1,0:T(8,128)(2,1)S(1)}, bf16[1024,512]{1,0:T(8,128)(2,1)}, u32[]{:S(2)}) copy-start(bf16[1024,512]{1,0:T(8,128)(2,1)} %fusion.30) | copy-start | bytes 3145732
  574.6 3.8 collective-permute-start.1
  582.7 1.6 copy-start.14
  582.8 157.2 %reduce-scatter.10.cloned.1.call-start = ((), (), s32[]{:S(2)}) async-start(), calls=%async_computation.14 | async-start | bytes 12976128 | tf_op jit(solution)/shard_map/reduce_scatter | solution.py:715
  586.9 5.2 copy-start.26
  586.9 20.7 %all-to-all-start.1 = ((bf16[8,32,2048]{2,1,0:T(8,128)(2,1)}), bf16[8,32,2048]{2,1,0:T(8,128)(2,1)}, u32[]{:S(2)}, u32[]{:S(2)}) async-start(bf16[8,32,2048]{2,1,0:T(8,128)(2,1)} %bitcast.90), calls=%async_computation.3 | async-start | bytes 2097152 | tf_op jit(solution)/shard_map/all_to_all | solution.py:1876
  592.0 5.4 copy-start.41
  740.0 2.7 copy-start.16
  751.4 18.9 %all-to-all-start.2 = ((bf16[8,32,2048]{2,1,0:T(8,128)(2,1)}), bf16[8,32,2048]{2,1,0:T(8,128)(2,1)S(1)}, u32[]{:S(2)}, u32[]{:S(2)}) async-start(bf16[8,32,2048]{2,1,0:T(8,128)(2,1)} %bitcast.25), calls=%async_computation.6 | async-start | bytes 2097152 | tf_op jit(solution)/shard_map/all_to_all | solution.py:1876
  755.0 103.0 %reduce-scatter.14.cloned.1.call-start = ((), (), s32[]{:S(2)}) async-start(), calls=%async_computation.16 | async-start | bytes 7667712 | tf_op jit(solution)/shard_map/reduce_scatter | solution.py:715
  770.3 1.0 copy-start.25
  770.3 1.1 copy-start.37
  770.3 1.3 copy-start.38
  771.8 8.5 copy-start.23
  771.8 8.5 copy-start.27
  771.9 8.5 copy-start.28
  771.9 8.5 copy-start.29
  780.4 1.5 copy-start.40
  781.8 72.7 %copy-start.32 = (f32[4,3,512]{2,0,1:T(4,128)S(1)}, f32[4,3,512]{2,0,1:T(4,128)}, u32[]{:S(2)}) copy-start(f32[4,3,512]{2,0,1:T(4,128)} %param.45) | copy-start | bytes 73732
  781.8 72.8 %copy-start.33 = (f32[4,3,512]{2,0,1:T(4,128)S(1)}, f32[4,3,512]{2,0,1:T(4,128)}, u32[]{:S(2)}) copy-start(f32[4,3,512]{2,0,1:T(4,128)} %param.46) | copy-start | bytes 73732
  781.9 74.7 %copy-start.34 = (f32[4224]{0:T(1024)S(1)}, f32[4224]{0:T(1024)}, u32[]{:S(2)}) copy-start(f32[4224]{0:T(1024)} %param.48) | copy-start | bytes 50692
  781.9 74.7 %copy-start.35 = (f32[4224]{0:T(1024)S(1)}, f32[4224]{0:T(1024)}, u32[]{:S(2)}) copy-start(f32[4224]{0:T(1024)} %param.49) | copy-start | bytes 50692
  860.5 9.7 %copy-start.20 = (f32[256,3,512]{2,0,1:T(8,128)S(1)}, f32[256,3,512]{2,0,1:T(8,128)}, u32[]{:S(2)}) copy-start(f32[256,3,512]{2,0,1:T(8,128)} %param.29) | copy-start | bytes 4718596
Sparse Core Ops, SparseCore 0:
  10.5 65.1 all-gather.4
  77.6 82.6 all-gather.6
  162.7 44.3 all-gather.10
  209.4 67.7 all-gather.8
  439.9 56.3 reduce-scatter.5
  506.9 74.3 reduce-scatter.7
  585.1 41.7 reduce-scatter.11
  630.8 86.8 reduce-scatter.9
  770.5 60.5 reduce-scatter.13
